TPU v7x, 32 devices: a whole 2x2x4 slice. The times are simulated.
32 devices in a mesh: grp: 1, row: 32 (over z, y, x, core), ka: 1.
Axes of the slice: x: 2, y: 2, z: 4, core: 2. Of those that a mesh axis runs over, the one named last changes fastest.
Arguments:
- pair_rep: bfloat16 [128, 128, 128], P(('grp', 'row'), 'ka'), may hold values from -6 to 6
- pair_mask: int32 [128, 128], P(('grp', 'row'), 'ka'), may hold values from 0 to 1, as said below
- proj_weight: bfloat16 [2, 128, 512], replicated, may hold values from -0.5 to 0.5
- proj_bias: float32 [2, 512], replicated, may hold values from -4 to 4
- gate_weight: bfloat16 [2, 128, 128], replicated, may hold values from -0.5 to 0.5
- gate_bias: float32 [2, 128], replicated, may hold values from -4 to 4
- out_weight: bfloat16 [2, 128, 128], replicated, may hold values from -0.5 to 0.5
- out_bias: float32 [2, 128], replicated, may hold values from -3 to 3
- norm_scale: float32 [2, 2, 128], replicated, may hold values from 0.1 to 1.9
- norm_offset: float32 [2, 2, 128], replicated, may hold values from -3 to 3
Outputs:
- pair_out: bfloat16 [128, 128, 128], P(('grp', 'row'), 'ka')
Inputs may be any that keep to these rules, and one draw needn't show every extreme that they name: pair_mask[a, b] is 1 wherever the circular residue distance min(|a - b|, 128 - |a - b|) is under 2 * 4; elsewhere it is 0 or 1.
All inputs are finite; a program needn't handle non-finite values.
Results may differ from a plain program's by a relative error of at most 0.014.
Values may be sent and summed in bfloat16 or wider, within the bound.
No kernel may reach another device: no remote copies, remote signals or barrier semaphores. Data moves between devices by JAX's collectives and lax.ppermute only.
A program may use at most 128 MiB of HBM per device.

v0:
```python
import functools

import jax
import jax.numpy as jnp
from jax import lax
from jax.experimental import pallas as pl
from jax.experimental.pallas import tpu as pltpu
from jax.sharding import PartitionSpec as P

PEERS = ("row", "ka")
OWN = 4
ORDERS = (
    ((0, 1, 2, 3, 4, 6, 8, 5, 12, 7, 9, 10, 13, 14, 11, 15), (0, 1, 2, 3, 4, 6, 8, 5, 12, 7, 9, 10, 13, 14, 11, 15)),
    ((0, 15, 11, 14, 13, 10, 9, 7, 12, 5, 8, 6, 4, 3, 2, 1), (0, 15, 11, 14, 13, 10, 9, 7, 12, 5, 8, 6, 4, 3, 2, 1)),
)
EACH = 16
BF16, F32 = jnp.bfloat16, jnp.float32


def over_rows(a, b):
    return lax.dot_general(a, b, (((0,), (0,)), ((), ())), preferred_element_type=F32)


def over_columns(a, b):
    return lax.dot_general(a, b, (((1,), (1,)), ((), ())), preferred_element_type=F32)


def layer_norm(values, norm_gain, norm_bias):
    average = jnp.mean(values, 0, keepdims=True)
    centred = values - average
    variance = jnp.mean(centred * centred, 0, keepdims=True)
    return centred * lax.rsqrt(variance + 1e-05) * norm_gain + norm_bias


def pack(blocks):
    channels, width = blocks[0].shape
    tiles = [b.reshape(channels // 8, 8, width) for b in blocks]
    turned = [pltpu.roll(b, 4, axis=0).reshape(channels // 8, 8, width) for b in blocks]
    low = lax.broadcasted_iota(jnp.int32, tiles[0].shape, 1) < 4
    back = [pltpu.roll(b, channels - 4, axis=0).reshape(channels // 8, 8, width) for b in blocks]
    even = [jnp.where(low, tiles[n], turned[n + 1]) for n in (0, 2)]
    odd = [jnp.where(low, back[n], tiles[n + 1]) for n in (0, 2)]
    return jnp.stack([jnp.stack(even, 1), jnp.stack(odd, 1)], 1).reshape(channels // 4, 16, width)


def unpack(packed):
    count, _, width = packed.shape
    tiles = packed.reshape(count // 2, 2, 2, 8, width)
    low = lax.broadcasted_iota(jnp.int32, (count // 2, 8, width), 1) < 4
    blocks = []
    for n in range(2):
        even, odd = tiles[:, 0, n], tiles[:, 1, n]
        down = pltpu.roll(odd.reshape(count * 4, width), 4, axis=0).reshape(even.shape)
        up = pltpu.roll(even.reshape(count * 4, width), count * 4 - 4, axis=0).reshape(even.shape)
        blocks.append(jnp.where(low, even, down).reshape(count * 4, width))
        blocks.append(jnp.where(low, up, odd).reshape(count * 4, width))
    return blocks


def sigmoid(x):
    return 0.5 * jnp.tanh(0.5 * x) + 0.5


def broadcast_columns(columns, first, many, width):
    held = columns[...]
    return [jnp.broadcast_to(held[:, n : n + 1], (held.shape[0], width)) for n in range(first, first + many)]


def project(u, z, mask, proj_weight, gate_weight, columns, send, gate, mixed):
    width = z[0].shape[1]
    h = proj_weight.shape[1] // 4
    rows = mixed.shape[1]
    gain, offset, *biases = broadcast_columns(columns, u * EACH, 7, width)
    turned = [proj_weight[:, n * h : (n + 1) * h].T for n in range(4)] + [gate_weight.T]
    for pair in range(0, OWN, 2):
        normed = [layer_norm(z[i], gain, offset).astype(BF16) for i in (pair, pair + 1)]
        normed = jnp.concatenate(normed, 1)
        both = [jnp.dot(w, normed, preferred_element_type=F32) for w in turned]
        for n in range(2):
            i = pair + n
            parts = [v[:, n * width : (n + 1) * width] + b for v, b in zip(both, biases)]
            keep = mask[i : i + 1, :]
            mixed[0, pl.ds(i, h, stride=OWN), :] = keep * sigmoid(parts[1]) * parts[0]
            mixed[1, pl.ds(i, h, stride=OWN), :] = keep * sigmoid(parts[3]) * parts[2]
            gate[:, i * width : (i + 1) * width] = sigmoid(parts[4])
    send[:, 0:16, :] = mixed[0].reshape(rows // 16, 16, width).astype(BF16)
    send[:, 16:32, :] = mixed[1].reshape(rows // 16, 16, width).astype(BF16)


def finish(u, z, summed, gate, out_weight, columns, mixed):
    width = z[0].shape[1]
    gain, offset, bias = broadcast_columns(columns, u * EACH + 7, 3, width)
    turned = out_weight.T
    mixed[...] = summed[...].astype(F32).reshape(mixed.shape)
    results = []
    for pair in range(0, OWN, 2):
        blocks = [mixed[pl.ds(i, mixed.shape[0] // OWN, stride=OWN), :] for i in (pair, pair + 1)]
        blocks = [reorder(v, ORDERS[u][1], ORDERS[u][0]) for v in blocks]
        hidden = jnp.concatenate([layer_norm(v, gain, offset).astype(BF16) for v in blocks], 1)
        both = jnp.dot(turned, hidden, preferred_element_type=F32)
        for n in range(2):
            change = both[:, n * width : (n + 1) * width] + bias
            at = slice((pair + n) * width, (pair + n + 1) * width)
            results.append((z[pair + n].astype(F32) + gate[:, at] * change).astype(BF16))
    return results


def first_kernel(
    pair, mask, pw, gw, pb, gb, ob, ns, no, send, gate, turned, columns, keep, pair_in, mask_in, pw_in, gw_in, pb_in, gb_in, ob_in, ns_in, no_in, rows, arrived, mixed
):
    moves = [(pair, pair_in), (pb, pb_in), (gb, gb_in), (ob, ob_in), (ns, ns_in), (no, no_in)]
    moves += [(pw.at[0], pw_in), (gw.at[0], gw_in), (mask, mask_in)]
    moves = [pltpu.make_async_copy(a, b, arrived.at[n]) for n, (a, b) in enumerate(moves)]
    for move in moves:
        move.start()
    moves[0].wait()
    width = pair.shape[1]
    z = [pair_in[i].T for i in range(OWN)]
    for i in range(OWN):
        turned[:, i * width : (i + 1) * width] = z[i]
    for move in moves[1:6]:
        move.wait()
    h = pw.shape[2] // 4
    for u in range(2):
        found = [ns_in[u, 0:1, :], no_in[u, 0:1, :]] + [pb_in[u : u + 1, n * h : (n + 1) * h] for n in range(4)]
        found += [gb_in[u : u + 1, :], ns_in[u, 1:2, :], no_in[u, 1:2, :], ob_in[u : u + 1, :]]
        for n, row in enumerate(found):
            rows[u * EACH + n : u * EACH + n + 1, :] = row
    columns[...] = rows[...].T
    for move in moves[6:]:
        move.wait()
    keep[0:OWN, :] = mask_in[...].astype(F32)
    project(0, [v.astype(F32) for v in z], keep, pw_in[...], gw_in[...], columns, send, gate, mixed)


def middle_kernel(summed, old, old_gate, columns, keep, pw, gw, ow, send, gate, turned, mixed, mixed_back):
    width = keep.shape[1]
    z = finish(0, [old[:, i * width : (i + 1) * width] for i in range(OWN)], summed, old_gate, ow[0], columns, mixed_back)
    for i in range(OWN):
        turned[:, i * width : (i + 1) * width] = z[i]
    project(1, [v.astype(F32) for v in z], keep, pw[1], gw[1], columns, send, gate, mixed)


def last_kernel(summed, old, old_gate, columns, ow, out, mixed_back):
    width = out.shape[1]
    z = finish(1, [old[:, i * width : (i + 1) * width] for i in range(OWN)], summed, old_gate, ow[1], columns, mixed_back)
    for i in range(OWN):
        out[i] = z[i].T


def reorder(values, have, want):
    tiles = values.reshape(len(have), 2 * OWN, values.shape[1])
    places = [have.index(chip) for chip in want]
    return jnp.concatenate([tiles[n : n + 1] for n in places]).reshape(values.shape)


def triangle_kernel(incoming, sides, out):
    come, go = ORDERS[1 if incoming else 0]
    in_mesh = tuple(range(len(come)))
    left, right = [unpack(sides[:, n : n + 16, :].astype(F32)) for n in (0, 16)]
    if incoming:
        summed = [over_rows(a.astype(BF16), b.astype(BF16)) for a, b in zip(left, right)]
        summed = [reorder(v, in_mesh, go) for v in summed]
    else:
        left = [reorder(v, come, go) for v in left]
        right = [reorder(v, come, in_mesh) for v in right]
        summed = [over_columns(a.astype(BF16), b.astype(BF16)) for a, b in zip(left, right)]
    out[...] = pack(summed).astype(BF16)


def call(kernel, outs, scratch, *args, place=pltpu.VMEM):
    in_vmem = pl.BlockSpec(memory_space=pltpu.VMEM)
    return pl.pallas_call(
        kernel,
        out_shape=[jax.ShapeDtypeStruct(*o) for o in outs],
        in_specs=[pl.BlockSpec(memory_space=place)] * len(args),
        out_specs=[in_vmem] * len(outs),
        scratch_shapes=scratch,
        compiler_params=pltpu.CompilerParams(vmem_limit_bytes=24 * 2**20),
    )(*args)


def exchange(blocks):
    return lax.all_to_all(blocks, PEERS, split_axis=0, concat_axis=0, tiled=True)


def exchange_in_order(blocks, chips):
    listed = [[2 * chip + core for chip in chips for core in range(2)]]
    return lax.all_to_all(blocks, "row", split_axis=0, concat_axis=0, axis_index_groups=listed, tiled=True)


def packed_updates(count, pair_rep, pair_mask, pw, pb, gw, gb, ow, ob, ns, no):
    rows_of, width, channels = pair_rep.shape
    flat = (channels, rows_of * width)
    projected = [((count, 32, width), BF16), (flat, F32), (flat, BF16)]
    summed = [((count, 16, width), BF16)]
    params = [pair_rep, pair_mask, pw, gw, pb, gb, ob, ns, no]
    params = [pltpu.with_memory_space_constraint(v, pltpu.HBM) for v in params]
    held = [pltpu.VMEM(v.shape[1:] if n in (2, 3) else v.shape, v.dtype) for n, v in enumerate(params)]
    held += [pltpu.VMEM((2 * EACH, channels), F32), pltpu.SemaphoreType.DMA((len(params),))]
    back = pltpu.VMEM((OWN * channels, width), F32)
    mixed = pltpu.VMEM((2, OWN * channels, width), F32)
    kept = [((channels, 2 * EACH), F32), ((2 * OWN, width), F32)]
    send, gate, turned, columns, keep = call(first_kernel, projected + kept, held + [mixed], *params, place=pltpu.HBM)
    (send,) = call(functools.partial(triangle_kernel, False), summed, [], exchange_in_order(send, ORDERS[0][0]))
    send, gate, turned = call(middle_kernel, projected, [mixed, back], exchange_in_order(send, ORDERS[0][1]), turned, gate, columns, keep, pw, gw, ow)
    (send,) = call(functools.partial(triangle_kernel, True), summed, [], exchange_in_order(send, ORDERS[1][0]))
    (out,) = call(last_kernel, [(pair_rep.shape, BF16)], [back], exchange_in_order(send, ORDERS[1][1]), turned, gate, columns, ow)
    return out


def update(pair_t, pair_mask, u, incoming, peers, rows_of, pw, pb, gw, gb, ow, ob, ns, no):
    channels, positions = pair_t.shape
    width = positions // rows_of
    h = pw.shape[2] // 4
    count = peers[0] * peers[1]
    own = h // count
    normed = layer_norm(pair_t, ns[u, 0][:, None], no[u, 0][:, None]).astype(BF16)
    projected = over_rows(jnp.concatenate([pw[u], gw[u]], 1), normed) + jnp.concatenate([pb[u], gb[u]], 0)[:, None]
    parts = [projected[n * h : (n + 1) * h] for n in range(4)]
    gating = jax.nn.sigmoid(projected[4 * h :])
    mask = pair_mask.astype(F32).reshape(1, positions)
    left = (mask * jax.nn.sigmoid(parts[1]) * parts[0]).astype(BF16)
    right = (mask * jax.nn.sigmoid(parts[3]) * parts[2]).astype(BF16)
    sides = exchange(jnp.stack([v.reshape(count, own, rows_of, width) for v in (left, right)], 1))
    sides = sides.reshape(peers[0], peers[1], 2, own, rows_of, width)
    sides = sides.transpose(2, 3, 0, 4, 1, 5).reshape(2, own, peers[0] * rows_of, peers[1] * width)
    form = "cki,ckj->cij" if incoming else "cik,cjk->cij"
    summed = jnp.einsum(form, sides[0], sides[1], preferred_element_type=F32).astype(BF16)
    summed = summed.reshape(own, peers[0], rows_of, peers[1], width).transpose(1, 3, 0, 2, 4)
    summed = exchange(summed.reshape(count, own, rows_of, width)).reshape(h, positions).astype(F32)
    hidden = layer_norm(summed, ns[u, 1][:, None], no[u, 1][:, None]).astype(BF16)
    change = over_rows(ow[u], hidden) + ob[u][:, None]
    return (pair_t + gating * change).astype(BF16)


def plain_updates(peers, pair_rep, pair_mask, *params):
    rows_of, width, channels = pair_rep.shape
    pair_t = pair_rep.reshape(rows_of * width, channels).T
    for u in range(2):
        pair_t = update(pair_t.astype(F32), pair_mask, u, u == 1, peers, rows_of, *params)
    return pair_t.T.reshape(rows_of, width, channels)


def solution(mesh):
    peers = (mesh.shape["row"], mesh.shape["ka"])
    count = peers[0] * peers[1]

    def on_device(pair_rep, pair_mask, *params):
        rows_of, width, channels = pair_rep.shape
        hidden = params[0].shape[2] // 4
        fits = peers[1] == 1 and rows_of == OWN and hidden == OWN * count and count == 2 * len(ORDERS[0][0])
        if fits and channels == hidden == 128 and width % 128 == 0:
            return packed_updates(count, pair_rep, pair_mask, *params)
        return plain_updates(peers, pair_rep, pair_mask, *params)

    split = P(("grp", "row"), "ka", None)
    in_specs = (split, P(("grp", "row"), "ka")) + (P(),) * 8
    return jax.shard_map(on_device, mesh=mesh, in_specs=in_specs, out_specs=split, check_vma=False)
```

profile of v0, /device:TPU:0, one launch (start us, length us, event | category | flops | bytes accessed | tf_op | source)
XLA Modules:
  0.0 54.6 jit_solution(14515903640297873477)
XLA Ops:
  0.0 1.7 %shard_map.100 = (bf16[32,32,128]{2,1,0:T(8,128)(2,1)S(1)}, f32[128,512]{1,0:T(8,128)S(1)}, bf16[128,512]{1,0:T(8,128)(2,1)S(1)}, f32[128,32]{1,0:T(8,128)S(1)}, f32[8,128]{1,0:T(8,128)S(1)}) custom-call(bf16[4,128,128]{2,1,0:T(8,128)(2,1)} %pair.1, s32[4,128]{1,0:T(4,128)} %mask.1, bf16[2,128,512]{2,1,0:T(8,128)(2,1)} %pw.3, bf16[2,128,128]{2,1,0:T(8,128)(2,1)} %gw.3, ...), custom_call_target="tpu_custom_call" | custom-call | tf_op jit(solution)/shard_map/pallas_call | solution.py:173
  1.7 17.4 %all_to_all.20.sides = bf16[32,32,128]{2,1,0:T(8,128)(2,1)S(1)} all-to-all(bf16[32,32,128]{2,1,0:T(8,128)(2,1)S(1)} %get-tuple-element.13), channel_id=1, replica_groups={{0,1,2,3,4,5,6,7,8,9,12,13,16,17,10,11,24,25,14,15,18,19,20,21,26,27,28..., dimensions={0} | all-to-all | bytes 524288 | tf_op jit(solution)/shard_map/all_to_all | solution.py:189
  19.1 0.0 copy-start
  19.1 0.2 shard_map.101
  19.3 0.0 copy-start.1
  19.3 0.0 copy-start.2
  19.3 10.8 %all_to_all.21.summed = bf16[32,16,128]{2,1,0:T(8,128)(2,1)S(1)} all-to-all(bf16[32,16,128]{2,1,0:T(8,128)(2,1)S(1)} %shard_map.101), channel_id=1, replica_groups={{0,1,2,3,4,5,6,7,8,9,12,13,16,17,10,11,24,25,14,15,18,19,20,21,26,27,28..., dimensions={0} | all-to-all | bytes 262144 | tf_op jit(solution)/shard_map/all_to_all | solution.py:189
  30.1 0.0 copy-done
  30.1 0.0 copy-done.1
  30.1 0.0 copy-done.2
  30.1 0.8 %shard_map.102 = (bf16[32,32,128]{2,1,0:T(8,128)(2,1)S(1)}, f32[128,512]{1,0:T(8,128)S(1)}, bf16[128,512]{1,0:T(8,128)(2,1)S(1)}) custom-call(bf16[32,16,128]{2,1,0:T(8,128)(2,1)S(1)} %all_to_all.21.summed, bf16[128,512]{1,0:T(8,128)(2,1)S(1)} %get-tuple-element.14.old, f32[128,512]{1,0:T(8,128)S(1)} %get-tuple-element.15.old_gate, ...), custom_call_target="tpu_custom_call" | custom-call | tf_op jit(solution)/shard_map/pallas_call | solution.py:173
  30.9 12.5 %all_to_all.22.sides = bf16[32,32,128]{2,1,0:T(8,128)(2,1)S(1)} all-to-all(bf16[32,32,128]{2,1,0:T(8,128)(2,1)S(1)} %get-tuple-element.18), channel_id=1, replica_groups={{0,1,30,31,22,23,28,29,26,27,20,21,18,19,14,15,24,25,10,11,16,17,12,13,..., dimensions={0} | all-to-all | bytes 524288 | tf_op jit(solution)/shard_map/all_to_all | solution.py:189
  43.4 0.2 shard_map.103
  43.6 9.9 %all_to_all.23.summed = bf16[32,16,128]{2,1,0:T(8,128)(2,1)S(1)} all-to-all(bf16[32,16,128]{2,1,0:T(8,128)(2,1)S(1)} %shard_map.103), channel_id=1, replica_groups={{0,1,30,31,22,23,28,29,26,27,20,21,18,19,14,15,24,25,10,11,16,17,12,13,..., dimensions={0} | all-to-all | bytes 262144 | tf_op jit(solution)/shard_map/all_to_all | solution.py:189
  53.6 1.0 %shard_map.104 = bf16[4,128,128]{2,1,0:T(8,128)(2,1)} custom-call(bf16[32,16,128]{2,1,0:T(8,128)(2,1)S(1)} %all_to_all.23.summed, bf16[128,512]{1,0:T(8,128)(2,1)S(1)} %get-tuple-element.19.old, f32[128,512]{1,0:T(8,128)S(1)} %get-tuple-element.20.old_gate, f32[128,32]{1,0:T(8,128)S(1)} %get-tuple-element.16.columns, bf16[2,128,128]{2,1,0:T(8,128)(2,1)S(1)} %copy-done.2), custom_call_target="tpu_custom_call" | custom-call | tf_op jit(solution)/shard_map/pallas_call | solution.py:173
Async XLA Ops:
  19.1 11.0 %copy-start = (bf16[2,128,512]{2,1,0:T(8,128)(2,1)S(1)}, bf16[2,128,512]{2,1,0:T(8,128)(2,1)}, u32[]{:S(2)}) copy-start(bf16[2,128,512]{2,1,0:T(8,128)(2,1)} %pw.3) | copy-start | bytes 786436
  19.3 10.8 %copy-start.1 = (bf16[2,128,128]{2,1,0:T(8,128)(2,1)S(1)}, bf16[2,128,128]{2,1,0:T(8,128)(2,1)}, u32[]{:S(2)}) copy-start(bf16[2,128,128]{2,1,0:T(8,128)(2,1)} %gw.3) | copy-start | bytes 196612
  19.3 10.8 %copy-start.2 = (bf16[2,128,128]{2,1,0:T(8,128)(2,1)S(1)}, bf16[2,128,128]{2,1,0:T(8,128)(2,1)}, u32[]{:S(2)}) copy-start(bf16[2,128,128]{2,1,0:T(8,128)(2,1)} %ow.3) | copy-start | bytes 196612
where the time goes:
time: 54.8 us; the launch traced here: 54.6 us
  blocking collectives  50.5 us (92%)
  Pallas kernels  3.96 us (7%)
    all_to_all x4, blocking collectives, exchange_in_order(): lax.all_to_all(blocks, 'row', split_axis=0, concat_axis=0, axis_index_gro...  50.5 us
    pallas_call x5, Pallas kernels, call(): pl.pallas_call(kernel, out_shape=[jax.ShapeDtypeStruct(*o) for o in outs]...  3.96 us

commit v1 on v0

--- a/solution.py
+++ b/solution.py
@@ -10,7 +10,7 @@
 PEERS = ("row", "ka")
 OWN = 4
 ORDERS = (
-    ((0, 1, 2, 3, 4, 6, 8, 5, 12, 7, 9, 10, 13, 14, 11, 15), (0, 1, 2, 3, 4, 6, 8, 5, 12, 7, 9, 10, 13, 14, 11, 15)),
+    ((0, 15, 11, 14, 13, 10, 9, 7, 12, 5, 8, 6, 4, 3, 2, 1), (0, 15, 11, 14, 13, 10, 9, 7, 12, 5, 8, 6, 4, 3, 2, 1)),
     ((0, 15, 11, 14, 13, 10, 9, 7, 12, 5, 8, 6, 4, 3, 2, 1), (0, 15, 11, 14, 13, 10, 9, 7, 12, 5, 8, 6, 4, 3, 2, 1)),
 )
 EACH = 16

time: 54.8 us -> 54.8 us (level)
  no operation moved by 1% of the time
where the time goes in v1:
time: 54.8 us; the launch traced here: 54.6 us
  blocking collectives  50.5 us (92%)
  Pallas kernels  3.95 us (7%)
    all_to_all x4, blocking collectives, exchange_in_order(): lax.all_to_all(blocks, 'row', split_axis=0, concat_axis=0, axis_index_gro...  50.5 us
    pallas_call x5, Pallas kernels, call(): pl.pallas_call(kernel, out_shape=[jax.ShapeDtypeStruct(*o) for o in outs]...  3.95 us

profile of v1, /device:TPU:0, one launch (start us, length us, event | category | flops | bytes accessed | tf_op | source)
XLA Modules:
  0.0 54.6 jit_solution(7011346754757926544)
XLA Ops:
  0.0 1.7 %shard_map.100 = (bf16[32,32,128]{2,1,0:T(8,128)(2,1)S(1)}, f32[128,512]{1,0:T(8,128)S(1)}, bf16[128,512]{1,0:T(8,128)(2,1)S(1)}, f32[128,32]{1,0:T(8,128)S(1)}, f32[8,128]{1,0:T(8,128)S(1)}) custom-call(bf16[4,128,128]{2,1,0:T(8,128)(2,1)} %pair.1, s32[4,128]{1,0:T(4,128)} %mask.1, bf16[2,128,512]{2,1,0:T(8,128)(2,1)} %pw.3, bf16[2,128,128]{2,1,0:T(8,128)(2,1)} %gw.3, ...), custom_call_target="tpu_custom_call" | custom-call | tf_op jit(solution)/shard_map/pallas_call | solution.py:173
  1.7 17.8 %all_to_all.20.sides = bf16[32,32,128]{2,1,0:T(8,128)(2,1)S(1)} all-to-all(bf16[32,32,128]{2,1,0:T(8,128)(2,1)S(1)} %get-tuple-element.13), channel_id=1, replica_groups={{0,1,30,31,22,23,28,29,26,27,20,21,18,19,14,15,24,25,10,11,16,17,12,13,..., dimensions={0} | all-to-all | bytes 524288 | tf_op jit(solution)/shard_map/all_to_all | solution.py:189
  19.5 0.0 copy-start
  19.5 0.2 shard_map.101
  19.7 0.0 copy-start.1
  19.7 0.0 copy-start.2
  19.7 9.9 %all_to_all.21.summed = bf16[32,16,128]{2,1,0:T(8,128)(2,1)S(1)} all-to-all(bf16[32,16,128]{2,1,0:T(8,128)(2,1)S(1)} %shard_map.101), channel_id=1, replica_groups={{0,1,30,31,22,23,28,29,26,27,20,21,18,19,14,15,24,25,10,11,16,17,12,13,..., dimensions={0} | all-to-all | bytes 262144 | tf_op jit(solution)/shard_map/all_to_all | solution.py:189
  29.7 0.0 copy-done
  29.7 0.0 copy-done.1
  29.7 0.0 copy-done.2
  29.7 0.8 %shard_map.102 = (bf16[32,32,128]{2,1,0:T(8,128)(2,1)S(1)}, f32[128,512]{1,0:T(8,128)S(1)}, bf16[128,512]{1,0:T(8,128)(2,1)S(1)}) custom-call(bf16[32,16,128]{2,1,0:T(8,128)(2,1)S(1)} %all_to_all.21.summed, bf16[128,512]{1,0:T(8,128)(2,1)S(1)} %get-tuple-element.14.old, f32[128,512]{1,0:T(8,128)S(1)} %get-tuple-element.15.old_gate, ...), custom_call_target="tpu_custom_call" | custom-call | tf_op jit(solution)/shard_map/pallas_call | solution.py:173
  30.5 12.9 %all_to_all.22.sides = bf16[32,32,128]{2,1,0:T(8,128)(2,1)S(1)} all-to-all(bf16[32,32,128]{2,1,0:T(8,128)(2,1)S(1)} %get-tuple-element.18), channel_id=1, replica_groups={{0,1,30,31,22,23,28,29,26,27,20,21,18,19,14,15,24,25,10,11,16,17,12,13,..., dimensions={0} | all-to-all | bytes 524288 | tf_op jit(solution)/shard_map/all_to_all | solution.py:189
  43.4 0.2 shard_map.103
  43.6 9.9 %all_to_all.23.summed = bf16[32,16,128]{2,1,0:T(8,128)(2,1)S(1)} all-to-all(bf16[32,16,128]{2,1,0:T(8,128)(2,1)S(1)} %shard_map.103), channel_id=1, replica_groups={{0,1,30,31,22,23,28,29,26,27,20,21,18,19,14,15,24,25,10,11,16,17,12,13,..., dimensions={0} | all-to-all | bytes 262144 | tf_op jit(solution)/shard_map/all_to_all | solution.py:189
  53.6 1.0 %shard_map.104 = bf16[4,128,128]{2,1,0:T(8,128)(2,1)} custom-call(bf16[32,16,128]{2,1,0:T(8,128)(2,1)S(1)} %all_to_all.23.summed, bf16[128,512]{1,0:T(8,128)(2,1)S(1)} %get-tuple-element.19.old, f32[128,512]{1,0:T(8,128)S(1)} %get-tuple-element.20.old_gate, f32[128,32]{1,0:T(8,128)S(1)} %get-tuple-element.16.columns, bf16[2,128,128]{2,1,0:T(8,128)(2,1)S(1)} %copy-done.2), custom_call_target="tpu_custom_call" | custom-call | tf_op jit(solution)/shard_map/pallas_call | solution.py:173
Async XLA Ops:
  19.5 10.2 %copy-start = (bf16[2,128,512]{2,1,0:T(8,128)(2,1)S(1)}, bf16[2,128,512]{2,1,0:T(8,128)(2,1)}, u32[]{:S(2)}) copy-start(bf16[2,128,512]{2,1,0:T(8,128)(2,1)} %pw.3) | copy-start | bytes 786436
  19.7 10.0 %copy-start.1 = (bf16[2,128,128]{2,1,0:T(8,128)(2,1)S(1)}, bf16[2,128,128]{2,1,0:T(8,128)(2,1)}, u32[]{:S(2)}) copy-start(bf16[2,128,128]{2,1,0:T(8,128)(2,1)} %gw.3) | copy-start | bytes 196612
  19.7 10.0 %copy-start.2 = (bf16[2,128,128]{2,1,0:T(8,128)(2,1)S(1)}, bf16[2,128,128]{2,1,0:T(8,128)(2,1)}, u32[]{:S(2)}) copy-start(bf16[2,128,128]{2,1,0:T(8,128)(2,1)} %ow.3) | copy-start | bytes 196612

commit v2 on v1

--- a/solution.py
+++ b/solution.py
@@ -10,8 +10,8 @@
 PEERS = ("row", "ka")
 OWN = 4
 ORDERS = (
-    ((0, 15, 11, 14, 13, 10, 9, 7, 12, 5, 8, 6, 4, 3, 2, 1), (0, 15, 11, 14, 13, 10, 9, 7, 12, 5, 8, 6, 4, 3, 2, 1)),
-    ((0, 15, 11, 14, 13, 10, 9, 7, 12, 5, 8, 6, 4, 3, 2, 1), (0, 15, 11, 14, 13, 10, 9, 7, 12, 5, 8, 6, 4, 3, 2, 1)),
+    ((0, 1, 2, 3, 4, 5, 6, 7, 8, 9, 10, 11, 12, 13, 14, 15), (0, 15, 11, 14, 13, 10, 9, 7, 12, 5, 8, 6, 4, 3, 2, 1)),
+    ((0, 1, 2, 3, 4, 5, 6, 7, 8, 9, 10, 11, 12, 13, 14, 15), (0, 15, 11, 14, 13, 10, 9, 7, 12, 5, 8, 6, 4, 3, 2, 1)),
 )
 EACH = 16
 BF16, F32 = jnp.bfloat16, jnp.float32

time: 54.8 us -> 54.8 us (level)
  no operation moved by 1% of the time
where the time goes in v2:
time: 54.8 us; the launch traced here: 54.6 us
  blocking collectives  50.6 us (92%)
  Pallas kernels  3.97 us (7%)
    all_to_all x4, blocking collectives, exchange_in_order(): lax.all_to_all(blocks, 'row', split_axis=0, concat_axis=0, axis_index_gro...  50.6 us
    pallas_call x5, Pallas kernels, call(): pl.pallas_call(kernel, out_shape=[jax.ShapeDtypeStruct(*o) for o in outs]...  3.97 us

profile of v2, /device:TPU:0, one launch (start us, length us, event | category | flops | bytes accessed | tf_op | source)
XLA Modules:
  0.0 54.6 jit_solution(1172649053254684643)
XLA Ops:
  0.0 1.7 %shard_map.100 = (bf16[32,32,128]{2,1,0:T(8,128)(2,1)S(1)}, f32[128,512]{1,0:T(8,128)S(1)}, bf16[128,512]{1,0:T(8,128)(2,1)S(1)}, f32[128,32]{1,0:T(8,128)S(1)}, f32[8,128]{1,0:T(8,128)S(1)}) custom-call(bf16[4,128,128]{2,1,0:T(8,128)(2,1)} %pair.1, s32[4,128]{1,0:T(4,128)} %mask.1, bf16[2,128,512]{2,1,0:T(8,128)(2,1)} %pw.3, bf16[2,128,128]{2,1,0:T(8,128)(2,1)} %gw.3, ...), custom_call_target="tpu_custom_call" | custom-call | tf_op jit(solution)/shard_map/pallas_call | solution.py:173
  1.7 17.7 %all_to_all.20.sides = bf16[32,32,128]{2,1,0:T(8,128)(2,1)S(1)} all-to-all(bf16[32,32,128]{2,1,0:T(8,128)(2,1)S(1)} %get-tuple-element.13), channel_id=1, replica_groups={{0,1,2,3,4,5,6,7,8,9,10,11,12,13,14,15,16,17,18,19,20,21,22,23,24,25,26..., dimensions={0} | all-to-all | bytes 524288 | tf_op jit(solution)/shard_map/all_to_all | solution.py:189
  19.4 0.0 copy-start
  19.4 0.2 shard_map.101
  19.6 0.0 copy-start.1
  19.6 0.0 copy-start.2
  19.7 10.0 %all_to_all.21.summed = bf16[32,16,128]{2,1,0:T(8,128)(2,1)S(1)} all-to-all(bf16[32,16,128]{2,1,0:T(8,128)(2,1)S(1)} %shard_map.101), channel_id=1, replica_groups={{0,1,30,31,22,23,28,29,26,27,20,21,18,19,14,15,24,25,10,11,16,17,12,13,..., dimensions={0} | all-to-all | bytes 262144 | tf_op jit(solution)/shard_map/all_to_all | solution.py:189
  29.7 0.0 copy-done
  29.7 0.0 copy-done.1
  29.7 0.0 copy-done.2
  29.7 0.8 %shard_map.102 = (bf16[32,32,128]{2,1,0:T(8,128)(2,1)S(1)}, f32[128,512]{1,0:T(8,128)S(1)}, bf16[128,512]{1,0:T(8,128)(2,1)S(1)}) custom-call(bf16[32,16,128]{2,1,0:T(8,128)(2,1)S(1)} %all_to_all.21.summed, bf16[128,512]{1,0:T(8,128)(2,1)S(1)} %get-tuple-element.14.old, f32[128,512]{1,0:T(8,128)S(1)} %get-tuple-element.15.old_gate, ...), custom_call_target="tpu_custom_call" | custom-call | tf_op jit(solution)/shard_map/pallas_call | solution.py:173
  30.5 12.8 %all_to_all.22.sides = bf16[32,32,128]{2,1,0:T(8,128)(2,1)S(1)} all-to-all(bf16[32,32,128]{2,1,0:T(8,128)(2,1)S(1)} %get-tuple-element.18), channel_id=1, replica_groups={{0,1,2,3,4,5,6,7,8,9,10,11,12,13,14,15,16,17,18,19,20,21,22,23,24,25,26..., dimensions={0} | all-to-all | bytes 524288 | tf_op jit(solution)/shard_map/all_to_all | solution.py:189
  43.3 0.2 shard_map.103
  43.5 10.0 %all_to_all.23.summed = bf16[32,16,128]{2,1,0:T(8,128)(2,1)S(1)} all-to-all(bf16[32,16,128]{2,1,0:T(8,128)(2,1)S(1)} %shard_map.103), channel_id=1, replica_groups={{0,1,30,31,22,23,28,29,26,27,20,21,18,19,14,15,24,25,10,11,16,17,12,13,..., dimensions={0} | all-to-all | bytes 262144 | tf_op jit(solution)/shard_map/all_to_all | solution.py:189
  53.6 1.0 %shard_map.104 = bf16[4,128,128]{2,1,0:T(8,128)(2,1)} custom-call(bf16[32,16,128]{2,1,0:T(8,128)(2,1)S(1)} %all_to_all.23.summed, bf16[128,512]{1,0:T(8,128)(2,1)S(1)} %get-tuple-element.19.old, f32[128,512]{1,0:T(8,128)S(1)} %get-tuple-element.20.old_gate, f32[128,32]{1,0:T(8,128)S(1)} %get-tuple-element.16.columns, bf16[2,128,128]{2,1,0:T(8,128)(2,1)S(1)} %copy-done.2), custom_call_target="tpu_custom_call" | custom-call | tf_op jit(solution)/shard_map/pallas_call | solution.py:173
Async XLA Ops:
  19.4 10.3 %copy-start = (bf16[2,128,512]{2,1,0:T(8,128)(2,1)S(1)}, bf16[2,128,512]{2,1,0:T(8,128)(2,1)}, u32[]{:S(2)}) copy-start(bf16[2,128,512]{2,1,0:T(8,128)(2,1)} %pw.3) | copy-start | bytes 786436
  19.6 10.1 %copy-start.1 = (bf16[2,128,128]{2,1,0:T(8,128)(2,1)S(1)}, bf16[2,128,128]{2,1,0:T(8,128)(2,1)}, u32[]{:S(2)}) copy-start(bf16[2,128,128]{2,1,0:T(8,128)(2,1)} %gw.3) | copy-start | bytes 196612
  19.6 10.1 %copy-start.2 = (bf16[2,128,128]{2,1,0:T(8,128)(2,1)S(1)}, bf16[2,128,128]{2,1,0:T(8,128)(2,1)}, u32[]{:S(2)}) copy-start(bf16[2,128,128]{2,1,0:T(8,128)(2,1)} %ow.3) | copy-start | bytes 196612

commit v3 on v1

--- a/solution.py
+++ b/solution.py
@@ -108,18 +108,20 @@
 def first_kernel(
     pair, mask, pw, gw, pb, gb, ob, ns, no, send, gate, turned, columns, keep, pair_in, mask_in, pw_in, gw_in, pb_in, gb_in, ob_in, ns_in, no_in, rows, arrived, mixed
 ):
-    moves = [(pair, pair_in), (pb, pb_in), (gb, gb_in), (ob, ob_in), (ns, ns_in), (no, no_in)]
-    moves += [(pw.at[0], pw_in), (gw.at[0], gw_in), (mask, mask_in)]
+    halves = [pl.ds(0, OWN // 2), pl.ds(OWN // 2, OWN // 2)]
+    depth = pw.shape[1] // 2
+    moves = [(pair.at[n], pair_in.at[n]) for n in halves]
+    moves += [(pw.at[0, pl.ds(n * depth, depth)], pw_in.at[pl.ds(n * depth, depth)]) for n in range(2)]
+    moves += [(pb, pb_in), (gb, gb_in), (ob, ob_in), (ns, ns_in), (no, no_in), (mask, mask_in), (gw.at[0], gw_in)]
     moves = [pltpu.make_async_copy(a, b, arrived.at[n]) for n, (a, b) in enumerate(moves)]
     for move in moves:
         move.start()
-    moves[0].wait()
+    for move in moves:
+        move.wait()
     width = pair.shape[1]
     z = [pair_in[i].T for i in range(OWN)]
     for i in range(OWN):
         turned[:, i * width : (i + 1) * width] = z[i]
-    for move in moves[1:6]:
-        move.wait()
     h = pw.shape[2] // 4
     for u in range(2):
         found = [ns_in[u, 0:1, :], no_in[u, 0:1, :]] + [pb_in[u : u + 1, n * h : (n + 1) * h] for n in range(4)]
@@ -127,8 +129,6 @@
         for n, row in enumerate(found):
             rows[u * EACH + n : u * EACH + n + 1, :] = row
     columns[...] = rows[...].T
-    for move in moves[6:]:
-        move.wait()
     keep[0:OWN, :] = mask_in[...].astype(F32)
     project(0, [v.astype(F32) for v in z], keep, pw_in[...], gw_in[...], columns, send, gate, mixed)
 
@@ -141,11 +141,16 @@
     project(1, [v.astype(F32) for v in z], keep, pw[1], gw[1], columns, send, gate, mixed)
 
 
-def last_kernel(summed, old, old_gate, columns, ow, out, mixed_back):
+def last_kernel(summed, old, old_gate, columns, ow, out, ready, left, mixed_back):
     width = out.shape[1]
-    z = finish(1, [old[:, i * width : (i + 1) * width] for i in range(OWN)], summed, old_gate, ow[1], columns, mixed_back)
+    z = [old[:, i * width : (i + 1) * width] for i in range(OWN)]
+    z = finish(1, z, summed, old_gate, ow[1], columns, mixed_back)
+    moves = [pltpu.make_async_copy(ready.at[i], out.at[i], left.at[i]) for i in range(OWN)]
     for i in range(OWN):
-        out[i] = z[i].T
+        ready[i] = z[i].T
+        moves[i].start()
+    for move in moves:
+        move.wait()
 
 
 def reorder(values, have, want):
@@ -168,13 +173,12 @@
     out[...] = pack(summed).astype(BF16)
 
 
-def call(kernel, outs, scratch, *args, place=pltpu.VMEM):
-    in_vmem = pl.BlockSpec(memory_space=pltpu.VMEM)
+def call(kernel, outs, scratch, *args, place=pltpu.VMEM, result=pltpu.VMEM):
     return pl.pallas_call(
         kernel,
         out_shape=[jax.ShapeDtypeStruct(*o) for o in outs],
         in_specs=[pl.BlockSpec(memory_space=place)] * len(args),
-        out_specs=[in_vmem] * len(outs),
+        out_specs=[pl.BlockSpec(memory_space=result)] * len(outs),
         scratch_shapes=scratch,
         compiler_params=pltpu.CompilerParams(vmem_limit_bytes=24 * 2**20),
     )(*args)
@@ -197,7 +201,7 @@
     params = [pair_rep, pair_mask, pw, gw, pb, gb, ob, ns, no]
     params = [pltpu.with_memory_space_constraint(v, pltpu.HBM) for v in params]
     held = [pltpu.VMEM(v.shape[1:] if n in (2, 3) else v.shape, v.dtype) for n, v in enumerate(params)]
-    held += [pltpu.VMEM((2 * EACH, channels), F32), pltpu.SemaphoreType.DMA((len(params),))]
+    held += [pltpu.VMEM((2 * EACH, channels), F32), pltpu.SemaphoreType.DMA((len(params) + 2,))]
     back = pltpu.VMEM((OWN * channels, width), F32)
     mixed = pltpu.VMEM((2, OWN * channels, width), F32)
     kept = [((channels, 2 * EACH), F32), ((2 * OWN, width), F32)]
@@ -205,7 +209,9 @@
     (send,) = call(functools.partial(triangle_kernel, False), summed, [], exchange_in_order(send, ORDERS[0][0]))
     send, gate, turned = call(middle_kernel, projected, [mixed, back], exchange_in_order(send, ORDERS[0][1]), turned, gate, columns, keep, pw, gw, ow)
     (send,) = call(functools.partial(triangle_kernel, True), summed, [], exchange_in_order(send, ORDERS[1][0]))
-    (out,) = call(last_kernel, [(pair_rep.shape, BF16)], [back], exchange_in_order(send, ORDERS[1][1]), turned, gate, columns, ow)
+    held = [pltpu.VMEM(pair_rep.shape, BF16), pltpu.SemaphoreType.DMA((rows_of,)), back]
+    send = exchange_in_order(send, ORDERS[1][1])
+    (out,) = call(last_kernel, [(pair_rep.shape, BF16)], held, send, turned, gate, columns, ow, result=pltpu.HBM)
     return out
 
 

time: 54.8 us -> 54.8 us (level)
  no operation moved by 1% of the time
where the time goes in v3:
time: 54.8 us; the launch traced here: 54.6 us
  blocking collectives  50.5 us (92%)
  Pallas kernels  3.96 us (7%)
    all_to_all x4, blocking collectives, exchange_in_order(): lax.all_to_all(blocks, 'row', split_axis=0, concat_axis=0, axis_index_gro...  50.5 us
    pallas_call x5, Pallas kernels, call(): pl.pallas_call(kernel, out_shape=[jax.ShapeDtypeStruct(*o) for o in outs]...  3.96 us

profile of v3, /device:TPU:0, one launch (start us, length us, event | category | flops | bytes accessed | tf_op | source)
XLA Modules:
  0.0 54.6 jit_solution(2268967412282446442)
XLA Ops:
  0.0 1.7 %shard_map.100 = (bf16[32,32,128]{2,1,0:T(8,128)(2,1)S(1)}, f32[128,512]{1,0:T(8,128)S(1)}, bf16[128,512]{1,0:T(8,128)(2,1)S(1)}, f32[128,32]{1,0:T(8,128)S(1)}, f32[8,128]{1,0:T(8,128)S(1)}) custom-call(bf16[4,128,128]{2,1,0:T(8,128)(2,1)} %pair.1, s32[4,128]{1,0:T(4,128)} %mask.1, bf16[2,128,512]{2,1,0:T(8,128)(2,1)} %pw.3, bf16[2,128,128]{2,1,0:T(8,128)(2,1)} %gw.3, ...), custom_call_target="tpu_custom_call" | custom-call | tf_op jit(solution)/shard_map/pallas_call | solution.py:177
  1.7 17.8 %all_to_all.20.sides = bf16[32,32,128]{2,1,0:T(8,128)(2,1)S(1)} all-to-all(bf16[32,32,128]{2,1,0:T(8,128)(2,1)S(1)} %get-tuple-element.13), channel_id=1, replica_groups={{0,1,30,31,22,23,28,29,26,27,20,21,18,19,14,15,24,25,10,11,16,17,12,13,..., dimensions={0} | all-to-all | bytes 524288 | tf_op jit(solution)/shard_map/all_to_all | solution.py:193
  19.5 0.0 copy-start
  19.5 0.2 shard_map.101
  19.7 0.0 copy-start.1
  19.7 0.0 copy-start.2
  19.7 9.9 %all_to_all.21.summed = bf16[32,16,128]{2,1,0:T(8,128)(2,1)S(1)} all-to-all(bf16[32,16,128]{2,1,0:T(8,128)(2,1)S(1)} %shard_map.101), channel_id=1, replica_groups={{0,1,30,31,22,23,28,29,26,27,20,21,18,19,14,15,24,25,10,11,16,17,12,13,..., dimensions={0} | all-to-all | bytes 262144 | tf_op jit(solution)/shard_map/all_to_all | solution.py:193
  29.7 0.0 copy-done
  29.7 0.0 copy-done.1
  29.7 0.0 copy-done.2
  29.7 0.8 %shard_map.102 = (bf16[32,32,128]{2,1,0:T(8,128)(2,1)S(1)}, f32[128,512]{1,0:T(8,128)S(1)}, bf16[128,512]{1,0:T(8,128)(2,1)S(1)}) custom-call(bf16[32,16,128]{2,1,0:T(8,128)(2,1)S(1)} %all_to_all.21.summed, bf16[128,512]{1,0:T(8,128)(2,1)S(1)} %get-tuple-element.14.old, f32[128,512]{1,0:T(8,128)S(1)} %get-tuple-element.15.old_gate, ...), custom_call_target="tpu_custom_call" | custom-call | tf_op jit(solution)/shard_map/pallas_call | solution.py:177
  30.5 12.9 %all_to_all.22.sides = bf16[32,32,128]{2,1,0:T(8,128)(2,1)S(1)} all-to-all(bf16[32,32,128]{2,1,0:T(8,128)(2,1)S(1)} %get-tuple-element.18), channel_id=1, replica_groups={{0,1,30,31,22,23,28,29,26,27,20,21,18,19,14,15,24,25,10,11,16,17,12,13,..., dimensions={0} | all-to-all | bytes 524288 | tf_op jit(solution)/shard_map/all_to_all | solution.py:193
  43.4 0.2 shard_map.103
  43.6 9.9 %all_to_all.23.summed = bf16[32,16,128]{2,1,0:T(8,128)(2,1)S(1)} all-to-all(bf16[32,16,128]{2,1,0:T(8,128)(2,1)S(1)} %shard_map.103), channel_id=1, replica_groups={{0,1,30,31,22,23,28,29,26,27,20,21,18,19,14,15,24,25,10,11,16,17,12,13,..., dimensions={0} | all-to-all | bytes 262144 | tf_op jit(solution)/shard_map/all_to_all | solution.py:193
  53.6 1.0 %shard_map.104 = bf16[4,128,128]{2,1,0:T(8,128)(2,1)} custom-call(bf16[32,16,128]{2,1,0:T(8,128)(2,1)S(1)} %all_to_all.23.summed, bf16[128,512]{1,0:T(8,128)(2,1)S(1)} %get-tuple-element.19.old, f32[128,512]{1,0:T(8,128)S(1)} %get-tuple-element.20.old_gate, f32[128,32]{1,0:T(8,128)S(1)} %get-tuple-element.16.columns, bf16[2,128,128]{2,1,0:T(8,128)(2,1)S(1)} %copy-done.2), custom_call_target="tpu_custom_call" | custom-call | tf_op jit(solution)/shard_map/pallas_call | solution.py:177
Async XLA Ops:
  19.5 10.2 %copy-start = (bf16[2,128,512]{2,1,0:T(8,128)(2,1)S(1)}, bf16[2,128,512]{2,1,0:T(8,128)(2,1)}, u32[]{:S(2)}) copy-start(bf16[2,128,512]{2,1,0:T(8,128)(2,1)} %pw.3) | copy-start | bytes 786436
  19.7 10.0 %copy-start.1 = (bf16[2,128,128]{2,1,0:T(8,128)(2,1)S(1)}, bf16[2,128,128]{2,1,0:T(8,128)(2,1)}, u32[]{:S(2)}) copy-start(bf16[2,128,128]{2,1,0:T(8,128)(2,1)} %gw.3) | copy-start | bytes 196612
  19.7 10.0 %copy-start.2 = (bf16[2,128,128]{2,1,0:T(8,128)(2,1)S(1)}, bf16[2,128,128]{2,1,0:T(8,128)(2,1)}, u32[]{:S(2)}) copy-start(bf16[2,128,128]{2,1,0:T(8,128)(2,1)} %ow.3) | copy-start | bytes 196612

commit v4 on v1

--- a/solution.py
+++ b/solution.py
@@ -1,5 +1,3 @@
-import functools
-
 import jax
 import jax.numpy as jnp
 from jax import lax
@@ -10,7 +8,7 @@
 PEERS = ("row", "ka")
 OWN = 4
 ORDERS = (
-    ((0, 15, 11, 14, 13, 10, 9, 7, 12, 5, 8, 6, 4, 3, 2, 1), (0, 15, 11, 14, 13, 10, 9, 7, 12, 5, 8, 6, 4, 3, 2, 1)),
+    ((15, 14, 13, 12, 11, 10, 9, 8, 7, 6, 5, 4, 3, 2, 1, 0), (0, 15, 11, 14, 13, 10, 9, 7, 12, 5, 8, 6, 4, 3, 2, 1)),
     ((0, 15, 11, 14, 13, 10, 9, 7, 12, 5, 8, 6, 4, 3, 2, 1), (0, 15, 11, 14, 13, 10, 9, 7, 12, 5, 8, 6, 4, 3, 2, 1)),
 )
 EACH = 16
@@ -154,7 +152,7 @@
     return jnp.concatenate([tiles[n : n + 1] for n in places]).reshape(values.shape)
 
 
-def triangle_kernel(incoming, sides, out):
+def triangle(incoming, sides, out):
     come, go = ORDERS[1 if incoming else 0]
     in_mesh = tuple(range(len(come)))
     left, right = [unpack(sides[:, n : n + 16, :].astype(F32)) for n in (0, 16)]
@@ -168,6 +166,21 @@
     out[...] = pack(summed).astype(BF16)
 
 
+def theirs_kernel(sides, theirs):
+    theirs[...] = sides[:, 1 - (lax.axis_index("row") & 1)]
+
+
+def outgoing_kernel(sides, others, out, both):
+    core = lax.axis_index("row") & 1
+    both[:, core] = sides[:, core]
+    both[:, 1 - core] = others[...]
+    triangle(False, both[...].reshape(2 * both.shape[0], *both.shape[2:]), out)
+
+
+def incoming_kernel(sides, out):
+    triangle(True, sides, out)
+
+
 def call(kernel, outs, scratch, *args, place=pltpu.VMEM):
     in_vmem = pl.BlockSpec(memory_space=pltpu.VMEM)
     return pl.pallas_call(
@@ -187,6 +200,15 @@
 def exchange_in_order(blocks, chips):
     listed = [[2 * chip + core for chip in chips for core in range(2)]]
     return lax.all_to_all(blocks, "row", split_axis=0, concat_axis=0, axis_index_groups=listed, tiled=True)
+
+
+def first_exchange(blocks, chips):
+    groups = [[2 * chip + core for chip in chips] for core in range(2)]
+    joined = blocks.reshape(len(chips), -1, blocks.shape[2])
+    joined = lax.all_to_all(joined, "row", split_axis=0, concat_axis=0, axis_index_groups=groups, tiled=True)
+    sides = joined.reshape(len(chips), 2, *blocks.shape[1:])
+    (theirs,) = call(theirs_kernel, [((len(chips), *blocks.shape[1:]), BF16)], [], sides)
+    return sides, lax.ppermute(theirs, "row", [(n, n ^ 1) for n in range(2 * len(chips))])
 
 
 def packed_updates(count, pair_rep, pair_mask, pw, pb, gw, gb, ow, ob, ns, no):
@@ -202,9 +224,10 @@
     mixed = pltpu.VMEM((2, OWN * channels, width), F32)
     kept = [((channels, 2 * EACH), F32), ((2 * OWN, width), F32)]
     send, gate, turned, columns, keep = call(first_kernel, projected + kept, held + [mixed], *params, place=pltpu.HBM)
-    (send,) = call(functools.partial(triangle_kernel, False), summed, [], exchange_in_order(send, ORDERS[0][0]))
+    both = pltpu.VMEM((count // 2, 2, 32, width), BF16)
+    (send,) = call(outgoing_kernel, summed, [both], *first_exchange(send, ORDERS[0][0]))
     send, gate, turned = call(middle_kernel, projected, [mixed, back], exchange_in_order(send, ORDERS[0][1]), turned, gate, columns, keep, pw, gw, ow)
-    (send,) = call(functools.partial(triangle_kernel, True), summed, [], exchange_in_order(send, ORDERS[1][0]))
+    (send,) = call(incoming_kernel, summed, [], exchange_in_order(send, ORDERS[1][0]))
     (out,) = call(last_kernel, [(pair_rep.shape, BF16)], [back], exchange_in_order(send, ORDERS[1][1]), turned, gate, columns, ow)
     return out
 

time: 54.8 us -> 56.2 us (1.026)
  waiting for transfers between devices: 0 us -> 1.33 us
    all_to_all x4 -> x3, blocking collectives: 50.5 us -> 34.3 us  [exchange_in_order(): lax.all_to_all(blocks, 'row', split_axis=0, concat_axis=0, axis_index_gro...]
    all_to_all x0 -> x1, blocking collectives: none -> 16.2 us  [first_exchange(): lax.all_to_all(joined, 'row', split_axis=0, concat_axis=0, axis_index_gro...]
    ppermute x0 -> x1, waiting for transfers between devices: none -> 1.33 us  [first_exchange(): lax.ppermute(theirs, 'row', [(n, n ^ 1) for n in range(2 * len(chips))])]
    pallas_call x5 -> x6, Pallas kernels: 3.95 us -> 4.01 us  [call(): pl.pallas_call(kernel, out_shape=[jax.ShapeDtypeStruct(*o) for o in outs]...]
  transfers between devices with their start and end apart: 0 -> 1, of which waited for: 0 -> 1; matrix products, arithmetic and copies ran while one was open for 0% -> 0% of each run, Pallas kernels for 0% -> 0%
where the time goes in v4:
time: 56.2 us; the launch traced here: 55.9 us
  blocking collectives  50.5 us (90%)
  Pallas kernels  4.01 us (7%)
  waiting for transfers between devices  1.33 us (2%)
    all_to_all x3, blocking collectives, exchange_in_order(): lax.all_to_all(blocks, 'row', split_axis=0, concat_axis=0, axis_index_gro...  34.3 us
    all_to_all x1, blocking collectives, first_exchange(): lax.all_to_all(joined, 'row', split_axis=0, concat_axis=0, axis_index_gro...  16.2 us
    pallas_call x6, Pallas kernels, call(): pl.pallas_call(kernel, out_shape=[jax.ShapeDtypeStruct(*o) for o in outs]...  4.01 us
    ppermute x1, waiting for transfers between devices, first_exchange(): lax.ppermute(theirs, 'row', [(n, n ^ 1) for n in range(2 * len(chips))])  1.33 us
  transfers between devices with their start and end apart: 1, of which 1 were waited for; matrix products, arithmetic and copies ran while one was open for 0% of the time, Pallas kernels for 0%

profile of v4, /device:TPU:0, one launch (start us, length us, event | category | flops | bytes accessed | tf_op | source)
XLA Modules:
  0.0 55.9 jit_solution(7786696246691073230)
XLA Ops:
  0.0 1.7 %shard_map.100 = (bf16[32,32,128]{2,1,0:T(8,128)(2,1)S(1)}, f32[128,512]{1,0:T(8,128)S(1)}, bf16[128,512]{1,0:T(8,128)(2,1)S(1)}, f32[128,32]{1,0:T(8,128)S(1)}, f32[8,128]{1,0:T(8,128)S(1)}) custom-call(bf16[4,128,128]{2,1,0:T(8,128)(2,1)} %pair.1, s32[4,128]{1,0:T(4,128)} %mask.1, bf16[2,128,512]{2,1,0:T(8,128)(2,1)} %pw.3, bf16[2,128,128]{2,1,0:T(8,128)(2,1)} %gw.3, ...), custom_call_target="tpu_custom_call" | custom-call | tf_op jit(solution)/shard_map/pallas_call | solution.py:186
  1.7 16.2 %all_to_all.20 = bf16[16,64,128]{2,1,0:T(8,128)(2,1)S(1)} all-to-all(bf16[16,64,128]{2,1,0:T(8,128)(2,1)S(1)} %bitcast.4), channel_id=1, replica_groups={{30,28,26,24,22,20,18,16,14,12,10,8,6,4,2,0},{31,29,27,25,23,21,19,17,1..., dimensions={0} | all-to-all | bytes 524288 | tf_op jit(solution)/shard_map/all_to_all | solution.py:208
  17.9 0.1 collective-permute-start
  18.0 1.3 %collective-permute-done.others = bf16[16,32,128]{2,1,0:T(8,128)(2,1)S(1)} collective-permute-done((bf16[16,32,128]{2,1,0:T(8,128)(2,1)S(1)}, bf16[16,32,128]{2,1,0:T(8,128)(2,1)S(1)}, u32[]{:S(2)}, u32[]{:S(2)}) %collective-permute-start) | collective-permute-done | bytes 131104 | tf_op jit(solution)/shard_map/ppermute | solution.py:211
  19.3 0.0 copy-start.1
  19.3 0.0 copy-start.2
  19.3 0.3 shard_map.102
  19.6 0.0 copy-start
  19.6 11.5 %all_to_all.21.summed = bf16[32,16,128]{2,1,0:T(8,128)(2,1)S(1)} all-to-all(bf16[32,16,128]{2,1,0:T(8,128)(2,1)S(1)} %shard_map.102), channel_id=1, replica_groups={{0,1,30,31,22,23,28,29,26,27,20,21,18,19,14,15,24,25,10,11,16,17,12,13,..., dimensions={0} | all-to-all | bytes 262144 | tf_op jit(solution)/shard_map/all_to_all | solution.py:202
  31.1 0.0 copy-done.1
  31.1 0.0 copy-done.2
  31.1 0.0 copy-done
  31.1 0.8 %shard_map.103 = (bf16[32,32,128]{2,1,0:T(8,128)(2,1)S(1)}, f32[128,512]{1,0:T(8,128)S(1)}, bf16[128,512]{1,0:T(8,128)(2,1)S(1)}) custom-call(bf16[32,16,128]{2,1,0:T(8,128)(2,1)S(1)} %all_to_all.21.summed, bf16[128,512]{1,0:T(8,128)(2,1)S(1)} %get-tuple-element.14.old, f32[128,512]{1,0:T(8,128)S(1)} %get-tuple-element.15.old_gate, ...), custom_call_target="tpu_custom_call" | custom-call | tf_op jit(solution)/shard_map/pallas_call | solution.py:186
  31.9 12.9 %all_to_all.22.sides = bf16[32,32,128]{2,1,0:T(8,128)(2,1)S(1)} all-to-all(bf16[32,32,128]{2,1,0:T(8,128)(2,1)S(1)} %get-tuple-element.18), channel_id=1, replica_groups={{0,1,30,31,22,23,28,29,26,27,20,21,18,19,14,15,24,25,10,11,16,17,12,13,..., dimensions={0} | all-to-all | bytes 524288 | tf_op jit(solution)/shard_map/all_to_all | solution.py:202
  44.8 0.2 shard_map.104
  45.0 9.9 %all_to_all.23.summed = bf16[32,16,128]{2,1,0:T(8,128)(2,1)S(1)} all-to-all(bf16[32,16,128]{2,1,0:T(8,128)(2,1)S(1)} %shard_map.104), channel_id=1, replica_groups={{0,1,30,31,22,23,28,29,26,27,20,21,18,19,14,15,24,25,10,11,16,17,12,13,..., dimensions={0} | all-to-all | bytes 262144 | tf_op jit(solution)/shard_map/all_to_all | solution.py:202
  54.9 1.0 %shard_map.105 = bf16[4,128,128]{2,1,0:T(8,128)(2,1)} custom-call(bf16[32,16,128]{2,1,0:T(8,128)(2,1)S(1)} %all_to_all.23.summed, bf16[128,512]{1,0:T(8,128)(2,1)S(1)} %get-tuple-element.19.old, f32[128,512]{1,0:T(8,128)S(1)} %get-tuple-element.20.old_gate, f32[128,32]{1,0:T(8,128)S(1)} %get-tuple-element.16.columns, bf16[2,128,128]{2,1,0:T(8,128)(2,1)S(1)} %copy-done.2), custom_call_target="tpu_custom_call" | custom-call | tf_op jit(solution)/shard_map/pallas_call | solution.py:186
  (1 shorter events, 0.0 us)
Async XLA Ops:
  17.9 1.4 %collective-permute-start = (bf16[16,32,128]{2,1,0:T(8,128)(2,1)S(1)}, bf16[16,32,128]{2,1,0:T(8,128)(2,1)S(1)}, u32[]{:S(2)}, u32[]{:S(2)}) collective-permute-start(bf16[16,32,128]{2,1,0:T(8,128)(2,1)S(1)} %shard_map.101), channel_id=1, source_target_pairs={{0,1},{1,0},{2,3},{3,2},{4,5},{5,4},{6,7},{7,6},{8,9},{9,8},{10,11... | collective-permute-start | bytes 393224 | tf_op jit(solution)/shard_map/ppermute | solution.py:211
  19.3 11.8 %copy-start.1 = (bf16[2,128,128]{2,1,0:T(8,128)(2,1)S(1)}, bf16[2,128,128]{2,1,0:T(8,128)(2,1)}, u32[]{:S(2)}) copy-start(bf16[2,128,128]{2,1,0:T(8,128)(2,1)} %gw.3) | copy-start | bytes 196612
  19.3 11.8 %copy-start.2 = (bf16[2,128,128]{2,1,0:T(8,128)(2,1)S(1)}, bf16[2,128,128]{2,1,0:T(8,128)(2,1)}, u32[]{:S(2)}) copy-start(bf16[2,128,128]{2,1,0:T(8,128)(2,1)} %ow.3) | copy-start | bytes 196612
  19.6 11.5 %copy-start = (bf16[2,128,512]{2,1,0:T(8,128)(2,1)S(1)}, bf16[2,128,512]{2,1,0:T(8,128)(2,1)}, u32[]{:S(2)}) copy-start(bf16[2,128,512]{2,1,0:T(8,128)(2,1)} %pw.3) | copy-start | bytes 786436

commit v5 on v1

--- a/solution.py
+++ b/solution.py
@@ -33,27 +33,27 @@
 
 
 def pack(blocks):
-    channels, width = blocks[0].shape
-    tiles = [b.reshape(channels // 8, 8, width) for b in blocks]
-    turned = [pltpu.roll(b, 4, axis=0).reshape(channels // 8, 8, width) for b in blocks]
+    rows, width = blocks[0].shape
+    tiles = [b.reshape(rows // 8, 8, width) for b in blocks]
+    turned = [pltpu.roll(b, 4, axis=0).reshape(rows // 8, 8, width) for b in blocks]
     low = lax.broadcasted_iota(jnp.int32, tiles[0].shape, 1) < 4
-    back = [pltpu.roll(b, channels - 4, axis=0).reshape(channels // 8, 8, width) for b in blocks]
-    even = [jnp.where(low, tiles[n], turned[n + 1]) for n in (0, 2)]
-    odd = [jnp.where(low, back[n], tiles[n + 1]) for n in (0, 2)]
-    return jnp.stack([jnp.stack(even, 1), jnp.stack(odd, 1)], 1).reshape(channels // 4, 16, width)
+    back = [pltpu.roll(b, rows - 4, axis=0).reshape(rows // 8, 8, width) for b in blocks]
+    first = [jnp.where(low, tiles[n], turned[n + 1]) for n in (0, 2)]
+    second = [jnp.where(low, back[n], tiles[n + 1]) for n in (0, 2)]
+    return jnp.stack([jnp.stack(first, 1), jnp.stack(second, 1)]).reshape(rows // 4, 16, width)
 
 
 def unpack(packed):
     count, _, width = packed.shape
-    tiles = packed.reshape(count // 2, 2, 2, 8, width)
+    tiles = packed.reshape(2, count // 2, 2, 8, width)
     low = lax.broadcasted_iota(jnp.int32, (count // 2, 8, width), 1) < 4
     blocks = []
     for n in range(2):
-        even, odd = tiles[:, 0, n], tiles[:, 1, n]
-        down = pltpu.roll(odd.reshape(count * 4, width), 4, axis=0).reshape(even.shape)
-        up = pltpu.roll(even.reshape(count * 4, width), count * 4 - 4, axis=0).reshape(even.shape)
-        blocks.append(jnp.where(low, even, down).reshape(count * 4, width))
-        blocks.append(jnp.where(low, up, odd).reshape(count * 4, width))
+        first, second = tiles[0, :, n], tiles[1, :, n]
+        down = pltpu.roll(second.reshape(count * 4, width), 4, axis=0).reshape(first.shape)
+        up = pltpu.roll(first.reshape(count * 4, width), count * 4 - 4, axis=0).reshape(first.shape)
+        blocks.append(jnp.where(low, first, down).reshape(count * 4, width))
+        blocks.append(jnp.where(low, up, second).reshape(count * 4, width))
     return blocks
 
 
@@ -185,7 +185,7 @@
 
 
 def exchange_in_order(blocks, chips):
-    listed = [[2 * chip + core for chip in chips for core in range(2)]]
+    listed = [[2 * chip + core for core in range(2) for chip in chips]]
     return lax.all_to_all(blocks, "row", split_axis=0, concat_axis=0, axis_index_groups=listed, tiled=True)
 
 

time: 54.8 us -> 55.4 us (1.011)
  blocking collectives: 50.5 us -> 51.2 us
    all_to_all x4, blocking collectives: 50.5 us -> 51.2 us  [exchange_in_order(): lax.all_to_all(blocks, 'row', split_axis=0, concat_axis=0, axis_index_gro...]
where the time goes in v5:
time: 55.4 us; the launch traced here: 55.2 us
  blocking collectives  51.2 us (92%)
  Pallas kernels  3.96 us (7%)
    all_to_all x4, blocking collectives, exchange_in_order(): lax.all_to_all(blocks, 'row', split_axis=0, concat_axis=0, axis_index_gro...  51.2 us
    pallas_call x5, Pallas kernels, call(): pl.pallas_call(kernel, out_shape=[jax.ShapeDtypeStruct(*o) for o in outs]...  3.96 us

profile of v5, /device:TPU:0, one launch (start us, length us, event | category | flops | bytes accessed | tf_op | source)
XLA Modules:
  0.0 55.2 jit_solution(1431680664969986771)
XLA Ops:
  0.0 1.7 %shard_map.100 = (bf16[32,32,128]{2,1,0:T(8,128)(2,1)S(1)}, f32[128,512]{1,0:T(8,128)S(1)}, bf16[128,512]{1,0:T(8,128)(2,1)S(1)}, f32[128,32]{1,0:T(8,128)S(1)}, f32[8,128]{1,0:T(8,128)S(1)}) custom-call(bf16[4,128,128]{2,1,0:T(8,128)(2,1)} %pair.1, s32[4,128]{1,0:T(4,128)} %mask.1, bf16[2,128,512]{2,1,0:T(8,128)(2,1)} %pw.3, bf16[2,128,128]{2,1,0:T(8,128)(2,1)} %gw.3, ...), custom_call_target="tpu_custom_call" | custom-call | tf_op jit(solution)/shard_map/pallas_call | solution.py:173
  1.7 17.5 %all_to_all.20.sides = bf16[32,32,128]{2,1,0:T(8,128)(2,1)S(1)} all-to-all(bf16[32,32,128]{2,1,0:T(8,128)(2,1)S(1)} %get-tuple-element.13), channel_id=1, replica_groups={{0,30,22,28,26,20,18,14,24,10,16,12,8,6,4,2,1,31,23,29,27,21,19,15,25,1..., dimensions={0} | all-to-all | bytes 524288 | tf_op jit(solution)/shard_map/all_to_all | solution.py:189
  19.2 0.0 copy-start
  19.2 0.2 shard_map.101
  19.5 0.0 copy-start.1
  19.5 0.0 copy-start.2
  19.5 10.8 %all_to_all.21.summed = bf16[32,16,128]{2,1,0:T(8,128)(2,1)S(1)} all-to-all(bf16[32,16,128]{2,1,0:T(8,128)(2,1)S(1)} %shard_map.101), channel_id=1, replica_groups={{0,30,22,28,26,20,18,14,24,10,16,12,8,6,4,2,1,31,23,29,27,21,19,15,25,1..., dimensions={0} | all-to-all | bytes 262144 | tf_op jit(solution)/shard_map/all_to_all | solution.py:189
  30.3 0.0 copy-done
  30.3 0.0 copy-done.1
  30.3 0.0 copy-done.2
  30.3 0.8 %shard_map.102 = (bf16[32,32,128]{2,1,0:T(8,128)(2,1)S(1)}, f32[128,512]{1,0:T(8,128)S(1)}, bf16[128,512]{1,0:T(8,128)(2,1)S(1)}) custom-call(bf16[32,16,128]{2,1,0:T(8,128)(2,1)S(1)} %all_to_all.21.summed, bf16[128,512]{1,0:T(8,128)(2,1)S(1)} %get-tuple-element.14.old, f32[128,512]{1,0:T(8,128)S(1)} %get-tuple-element.15.old_gate, ...), custom_call_target="tpu_custom_call" | custom-call | tf_op jit(solution)/shard_map/pallas_call | solution.py:173
  31.1 12.1 %all_to_all.22.sides = bf16[32,32,128]{2,1,0:T(8,128)(2,1)S(1)} all-to-all(bf16[32,32,128]{2,1,0:T(8,128)(2,1)S(1)} %get-tuple-element.18), channel_id=1, replica_groups={{0,30,22,28,26,20,18,14,24,10,16,12,8,6,4,2,1,31,23,29,27,21,19,15,25,1..., dimensions={0} | all-to-all | bytes 524288 | tf_op jit(solution)/shard_map/all_to_all | solution.py:189
  43.2 0.2 shard_map.103
  43.5 10.7 %all_to_all.23.summed = bf16[32,16,128]{2,1,0:T(8,128)(2,1)S(1)} all-to-all(bf16[32,16,128]{2,1,0:T(8,128)(2,1)S(1)} %shard_map.103), channel_id=1, replica_groups={{0,30,22,28,26,20,18,14,24,10,16,12,8,6,4,2,1,31,23,29,27,21,19,15,25,1..., dimensions={0} | all-to-all | bytes 262144 | tf_op jit(solution)/shard_map/all_to_all | solution.py:189
  54.2 1.0 %shard_map.104 = bf16[4,128,128]{2,1,0:T(8,128)(2,1)} custom-call(bf16[32,16,128]{2,1,0:T(8,128)(2,1)S(1)} %all_to_all.23.summed, bf16[128,512]{1,0:T(8,128)(2,1)S(1)} %get-tuple-element.19.old, f32[128,512]{1,0:T(8,128)S(1)} %get-tuple-element.20.old_gate, f32[128,32]{1,0:T(8,128)S(1)} %get-tuple-element.16.columns, bf16[2,128,128]{2,1,0:T(8,128)(2,1)S(1)} %copy-done.2), custom_call_target="tpu_custom_call" | custom-call | tf_op jit(solution)/shard_map/pallas_call | solution.py:173
Async XLA Ops:
  19.2 11.0 %copy-start = (bf16[2,128,512]{2,1,0:T(8,128)(2,1)S(1)}, bf16[2,128,512]{2,1,0:T(8,128)(2,1)}, u32[]{:S(2)}) copy-start(bf16[2,128,512]{2,1,0:T(8,128)(2,1)} %pw.3) | copy-start | bytes 786436
  19.5 10.8 %copy-start.1 = (bf16[2,128,128]{2,1,0:T(8,128)(2,1)S(1)}, bf16[2,128,128]{2,1,0:T(8,128)(2,1)}, u32[]{:S(2)}) copy-start(bf16[2,128,128]{2,1,0:T(8,128)(2,1)} %gw.3) | copy-start | bytes 196612
  19.5 10.8 %copy-start.2 = (bf16[2,128,128]{2,1,0:T(8,128)(2,1)S(1)}, bf16[2,128,128]{2,1,0:T(8,128)(2,1)}, u32[]{:S(2)}) copy-start(bf16[2,128,128]{2,1,0:T(8,128)(2,1)} %ow.3) | copy-start | bytes 196612

commit v6 on v1

--- a/solution.py
+++ b/solution.py
@@ -57,10 +57,6 @@
     return blocks
 
 
-def sigmoid(x):
-    return 0.5 * jnp.tanh(0.5 * x) + 0.5
-
-
 def broadcast_columns(columns, first, many, width):
     held = columns[...]
     return [jnp.broadcast_to(held[:, n : n + 1], (held.shape[0], width)) for n in range(first, first + many)]
@@ -71,20 +67,29 @@
     h = proj_weight.shape[1] // 4
     rows = mixed.shape[1]
     gain, offset, *biases = broadcast_columns(columns, u * EACH, 7, width)
-    turned = [proj_weight[:, n * h : (n + 1) * h].T for n in range(4)] + [gate_weight.T]
+    scales = (1.0, 0.5, 1.0, 0.5, 0.5)
+    biases = [b * k for b, k in zip(biases, scales)]
+    turned = [proj_weight[:, n * h : (n + 1) * h] for n in range(4)] + [gate_weight]
+    turned = [(w * jnp.asarray(k, BF16)).T if k != 1.0 else w.T for w, k in zip(turned, scales)]
+    pairs = []
     for pair in range(0, OWN, 2):
         normed = [layer_norm(z[i], gain, offset).astype(BF16) for i in (pair, pair + 1)]
-        normed = jnp.concatenate(normed, 1)
-        both = [jnp.dot(w, normed, preferred_element_type=F32) for w in turned]
+        pairs.append(jnp.concatenate(normed, 1))
+    for side in range(2):
+        for pair, normed in enumerate(pairs):
+            value, gating = [jnp.dot(turned[2 * side + n], normed, preferred_element_type=F32) for n in range(2)]
+            for n in range(2):
+                i, at = 2 * pair + n, slice(n * width, (n + 1) * width)
+                half = mask[i : i + 1, :] * 0.5
+                weight = jnp.tanh(gating[:, at] + biases[2 * side + 1]) * half + half
+                mixed[side, pl.ds(i, h, stride=OWN), :] = weight * (value[:, at] + biases[2 * side])
+    for side in range(2):
+        send[:, side * 16 : (side + 1) * 16, :] = mixed[side].reshape(rows // 16, 16, width).astype(BF16)
+    for pair, normed in enumerate(pairs):
+        gating = jnp.dot(turned[4], normed, preferred_element_type=F32)
         for n in range(2):
-            i = pair + n
-            parts = [v[:, n * width : (n + 1) * width] + b for v, b in zip(both, biases)]
-            keep = mask[i : i + 1, :]
-            mixed[0, pl.ds(i, h, stride=OWN), :] = keep * sigmoid(parts[1]) * parts[0]
-            mixed[1, pl.ds(i, h, stride=OWN), :] = keep * sigmoid(parts[3]) * parts[2]
-            gate[:, i * width : (i + 1) * width] = sigmoid(parts[4])
-    send[:, 0:16, :] = mixed[0].reshape(rows // 16, 16, width).astype(BF16)
-    send[:, 16:32, :] = mixed[1].reshape(rows // 16, 16, width).astype(BF16)
+            i = 2 * pair + n
+            gate[:, i * width : (i + 1) * width] = 0.5 * jnp.tanh(gating[:, n * width : (n + 1) * width] + biases[4]) + 0.5
 
 
 def finish(u, z, summed, gate, out_weight, columns, mixed):
@@ -113,13 +118,12 @@
     moves = [pltpu.make_async_copy(a, b, arrived.at[n]) for n, (a, b) in enumerate(moves)]
     for move in moves:
         move.start()
-    moves[0].wait()
+    for move in moves:
+        move.wait()
     width = pair.shape[1]
     z = [pair_in[i].T for i in range(OWN)]
     for i in range(OWN):
         turned[:, i * width : (i + 1) * width] = z[i]
-    for move in moves[1:6]:
-        move.wait()
     h = pw.shape[2] // 4
     for u in range(2):
         found = [ns_in[u, 0:1, :], no_in[u, 0:1, :]] + [pb_in[u : u + 1, n * h : (n + 1) * h] for n in range(4)]
@@ -127,8 +131,6 @@
         for n, row in enumerate(found):
             rows[u * EACH + n : u * EACH + n + 1, :] = row
     columns[...] = rows[...].T
-    for move in moves[6:]:
-        move.wait()
     keep[0:OWN, :] = mask_in[...].astype(F32)
     project(0, [v.astype(F32) for v in z], keep, pw_in[...], gw_in[...], columns, send, gate, mixed)
 

time: 54.8 us -> 54.8 us (level)
  no operation moved by 1% of the time
where the time goes in v6:
time: 54.8 us; the launch traced here: 54.6 us
  blocking collectives  50.5 us (92%)
  Pallas kernels  3.94 us (7%)
    all_to_all x4, blocking collectives, exchange_in_order(): lax.all_to_all(blocks, 'row', split_axis=0, concat_axis=0, axis_index_gro...  50.5 us
    pallas_call x5, Pallas kernels, call(): pl.pallas_call(kernel, out_shape=[jax.ShapeDtypeStruct(*o) for o in outs]...  3.94 us

profile of v6, /device:TPU:0, one launch (start us, length us, event | category | flops | bytes accessed | tf_op | source)
XLA Modules:
  0.0 54.6 jit_solution(8818587974111591623)
XLA Ops:
  0.0 1.7 %shard_map.100 = (bf16[32,32,128]{2,1,0:T(8,128)(2,1)S(1)}, f32[128,512]{1,0:T(8,128)S(1)}, bf16[128,512]{1,0:T(8,128)(2,1)S(1)}, f32[128,32]{1,0:T(8,128)S(1)}, f32[8,128]{1,0:T(8,128)S(1)}) custom-call(bf16[4,128,128]{2,1,0:T(8,128)(2,1)} %pair.1, s32[4,128]{1,0:T(4,128)} %mask.1, bf16[2,128,512]{2,1,0:T(8,128)(2,1)} %pw.3, bf16[2,128,128]{2,1,0:T(8,128)(2,1)} %gw.3, ...), custom_call_target="tpu_custom_call" | custom-call | tf_op jit(solution)/shard_map/pallas_call | solution.py:175
  1.7 17.8 %all_to_all.20.sides = bf16[32,32,128]{2,1,0:T(8,128)(2,1)S(1)} all-to-all(bf16[32,32,128]{2,1,0:T(8,128)(2,1)S(1)} %get-tuple-element.13), channel_id=1, replica_groups={{0,1,30,31,22,23,28,29,26,27,20,21,18,19,14,15,24,25,10,11,16,17,12,13,..., dimensions={0} | all-to-all | bytes 524288 | tf_op jit(solution)/shard_map/all_to_all | solution.py:191
  19.5 0.0 copy-start
  19.5 0.2 shard_map.101
  19.7 0.0 copy-start.1
  19.8 0.0 copy-start.2
  19.8 9.9 %all_to_all.21.summed = bf16[32,16,128]{2,1,0:T(8,128)(2,1)S(1)} all-to-all(bf16[32,16,128]{2,1,0:T(8,128)(2,1)S(1)} %shard_map.101), channel_id=1, replica_groups={{0,1,30,31,22,23,28,29,26,27,20,21,18,19,14,15,24,25,10,11,16,17,12,13,..., dimensions={0} | all-to-all | bytes 262144 | tf_op jit(solution)/shard_map/all_to_all | solution.py:191
  29.7 0.0 copy-done
  29.7 0.0 copy-done.1
  29.7 0.0 copy-done.2
  29.7 0.8 %shard_map.102 = (bf16[32,32,128]{2,1,0:T(8,128)(2,1)S(1)}, f32[128,512]{1,0:T(8,128)S(1)}, bf16[128,512]{1,0:T(8,128)(2,1)S(1)}) custom-call(bf16[32,16,128]{2,1,0:T(8,128)(2,1)S(1)} %all_to_all.21.summed, bf16[128,512]{1,0:T(8,128)(2,1)S(1)} %get-tuple-element.14.old, f32[128,512]{1,0:T(8,128)S(1)} %get-tuple-element.15.old_gate, ...), custom_call_target="tpu_custom_call" | custom-call | tf_op jit(solution)/shard_map/pallas_call | solution.py:175
  30.5 12.9 %all_to_all.22.sides = bf16[32,32,128]{2,1,0:T(8,128)(2,1)S(1)} all-to-all(bf16[32,32,128]{2,1,0:T(8,128)(2,1)S(1)} %get-tuple-element.18), channel_id=1, replica_groups={{0,1,30,31,22,23,28,29,26,27,20,21,18,19,14,15,24,25,10,11,16,17,12,13,..., dimensions={0} | all-to-all | bytes 524288 | tf_op jit(solution)/shard_map/all_to_all | solution.py:191
  43.4 0.2 shard_map.103
  43.6 9.9 %all_to_all.23.summed = bf16[32,16,128]{2,1,0:T(8,128)(2,1)S(1)} all-to-all(bf16[32,16,128]{2,1,0:T(8,128)(2,1)S(1)} %shard_map.103), channel_id=1, replica_groups={{0,1,30,31,22,23,28,29,26,27,20,21,18,19,14,15,24,25,10,11,16,17,12,13,..., dimensions={0} | all-to-all | bytes 262144 | tf_op jit(solution)/shard_map/all_to_all | solution.py:191
  53.5 1.0 %shard_map.104 = bf16[4,128,128]{2,1,0:T(8,128)(2,1)} custom-call(bf16[32,16,128]{2,1,0:T(8,128)(2,1)S(1)} %all_to_all.23.summed, bf16[128,512]{1,0:T(8,128)(2,1)S(1)} %get-tuple-element.19.old, f32[128,512]{1,0:T(8,128)S(1)} %get-tuple-element.20.old_gate, f32[128,32]{1,0:T(8,128)S(1)} %get-tuple-element.16.columns, bf16[2,128,128]{2,1,0:T(8,128)(2,1)S(1)} %copy-done.2), custom_call_target="tpu_custom_call" | custom-call | tf_op jit(solution)/shard_map/pallas_call | solution.py:175
Async XLA Ops:
  19.5 10.2 %copy-start = (bf16[2,128,512]{2,1,0:T(8,128)(2,1)S(1)}, bf16[2,128,512]{2,1,0:T(8,128)(2,1)}, u32[]{:S(2)}) copy-start(bf16[2,128,512]{2,1,0:T(8,128)(2,1)} %pw.3) | copy-start | bytes 786436
  19.7 10.0 %copy-start.1 = (bf16[2,128,128]{2,1,0:T(8,128)(2,1)S(1)}, bf16[2,128,128]{2,1,0:T(8,128)(2,1)}, u32[]{:S(2)}) copy-start(bf16[2,128,128]{2,1,0:T(8,128)(2,1)} %gw.3) | copy-start | bytes 196612
  19.8 10.0 %copy-start.2 = (bf16[2,128,128]{2,1,0:T(8,128)(2,1)S(1)}, bf16[2,128,128]{2,1,0:T(8,128)(2,1)}, u32[]{:S(2)}) copy-start(bf16[2,128,128]{2,1,0:T(8,128)(2,1)} %ow.3) | copy-start | bytes 196612

commit v7 on v6

--- a/solution.py
+++ b/solution.py
@@ -116,8 +116,8 @@
     moves = [(pair, pair_in), (pb, pb_in), (gb, gb_in), (ob, ob_in), (ns, ns_in), (no, no_in)]
     moves += [(pw.at[0], pw_in), (gw.at[0], gw_in), (mask, mask_in)]
     moves = [pltpu.make_async_copy(a, b, arrived.at[n]) for n, (a, b) in enumerate(moves)]
-    for move in moves:
-        move.start()
+    for n, move in enumerate(moves):
+        move.start(priority=0 if n in (0, 6) else 1)
     for move in moves:
         move.wait()
     width = pair.shape[1]

time: 54.8 us -> 54.8 us (level)
  no operation moved by 1% of the time
where the time goes in v7:
time: 54.8 us; the launch traced here: 54.6 us
  blocking collectives  50.5 us (92%)
  Pallas kernels  3.96 us (7%)
    all_to_all x4, blocking collectives, exchange_in_order(): lax.all_to_all(blocks, 'row', split_axis=0, concat_axis=0, axis_index_gro...  50.5 us
    pallas_call x5, Pallas kernels, call(): pl.pallas_call(kernel, out_shape=[jax.ShapeDtypeStruct(*o) for o in outs]...  3.96 us

profile of v7, /device:TPU:0, one launch (start us, length us, event | category | flops | bytes accessed | tf_op | source)
XLA Modules:
  0.0 54.6 jit_solution(6844615155937174520)
XLA Ops:
  0.0 1.7 %shard_map.100 = (bf16[32,32,128]{2,1,0:T(8,128)(2,1)S(1)}, f32[128,512]{1,0:T(8,128)S(1)}, bf16[128,512]{1,0:T(8,128)(2,1)S(1)}, f32[128,32]{1,0:T(8,128)S(1)}, f32[8,128]{1,0:T(8,128)S(1)}) custom-call(bf16[4,128,128]{2,1,0:T(8,128)(2,1)} %pair.1, s32[4,128]{1,0:T(4,128)} %mask.1, bf16[2,128,512]{2,1,0:T(8,128)(2,1)} %pw.3, bf16[2,128,128]{2,1,0:T(8,128)(2,1)} %gw.3, ...), custom_call_target="tpu_custom_call" | custom-call | tf_op jit(solution)/shard_map/pallas_call | solution.py:175
  1.7 17.8 %all_to_all.20.sides = bf16[32,32,128]{2,1,0:T(8,128)(2,1)S(1)} all-to-all(bf16[32,32,128]{2,1,0:T(8,128)(2,1)S(1)} %get-tuple-element.13), channel_id=1, replica_groups={{0,1,30,31,22,23,28,29,26,27,20,21,18,19,14,15,24,25,10,11,16,17,12,13,..., dimensions={0} | all-to-all | bytes 524288 | tf_op jit(solution)/shard_map/all_to_all | solution.py:191
  19.5 0.0 copy-start
  19.5 0.2 shard_map.101
  19.8 0.0 copy-start.1
  19.8 0.0 copy-start.2
  19.8 9.9 %all_to_all.21.summed = bf16[32,16,128]{2,1,0:T(8,128)(2,1)S(1)} all-to-all(bf16[32,16,128]{2,1,0:T(8,128)(2,1)S(1)} %shard_map.101), channel_id=1, replica_groups={{0,1,30,31,22,23,28,29,26,27,20,21,18,19,14,15,24,25,10,11,16,17,12,13,..., dimensions={0} | all-to-all | bytes 262144 | tf_op jit(solution)/shard_map/all_to_all | solution.py:191
  29.7 0.0 copy-done
  29.7 0.0 copy-done.1
  29.7 0.0 copy-done.2
  29.7 0.8 %shard_map.102 = (bf16[32,32,128]{2,1,0:T(8,128)(2,1)S(1)}, f32[128,512]{1,0:T(8,128)S(1)}, bf16[128,512]{1,0:T(8,128)(2,1)S(1)}) custom-call(bf16[32,16,128]{2,1,0:T(8,128)(2,1)S(1)} %all_to_all.21.summed, bf16[128,512]{1,0:T(8,128)(2,1)S(1)} %get-tuple-element.14.old, f32[128,512]{1,0:T(8,128)S(1)} %get-tuple-element.15.old_gate, ...), custom_call_target="tpu_custom_call" | custom-call | tf_op jit(solution)/shard_map/pallas_call | solution.py:175
  30.5 12.9 %all_to_all.22.sides = bf16[32,32,128]{2,1,0:T(8,128)(2,1)S(1)} all-to-all(bf16[32,32,128]{2,1,0:T(8,128)(2,1)S(1)} %get-tuple-element.18), channel_id=1, replica_groups={{0,1,30,31,22,23,28,29,26,27,20,21,18,19,14,15,24,25,10,11,16,17,12,13,..., dimensions={0} | all-to-all | bytes 524288 | tf_op jit(solution)/shard_map/all_to_all | solution.py:191
  43.4 0.2 shard_map.103
  43.6 9.9 %all_to_all.23.summed = bf16[32,16,128]{2,1,0:T(8,128)(2,1)S(1)} all-to-all(bf16[32,16,128]{2,1,0:T(8,128)(2,1)S(1)} %shard_map.103), channel_id=1, replica_groups={{0,1,30,31,22,23,28,29,26,27,20,21,18,19,14,15,24,25,10,11,16,17,12,13,..., dimensions={0} | all-to-all | bytes 262144 | tf_op jit(solution)/shard_map/all_to_all | solution.py:191
  53.6 1.0 %shard_map.104 = bf16[4,128,128]{2,1,0:T(8,128)(2,1)} custom-call(bf16[32,16,128]{2,1,0:T(8,128)(2,1)S(1)} %all_to_all.23.summed, bf16[128,512]{1,0:T(8,128)(2,1)S(1)} %get-tuple-element.19.old, f32[128,512]{1,0:T(8,128)S(1)} %get-tuple-element.20.old_gate, f32[128,32]{1,0:T(8,128)S(1)} %get-tuple-element.16.columns, bf16[2,128,128]{2,1,0:T(8,128)(2,1)S(1)} %copy-done.2), custom_call_target="tpu_custom_call" | custom-call | tf_op jit(solution)/shard_map/pallas_call | solution.py:175
Async XLA Ops:
  19.5 10.2 %copy-start = (bf16[2,128,512]{2,1,0:T(8,128)(2,1)S(1)}, bf16[2,128,512]{2,1,0:T(8,128)(2,1)}, u32[]{:S(2)}) copy-start(bf16[2,128,512]{2,1,0:T(8,128)(2,1)} %pw.3) | copy-start | bytes 786436
  19.8 10.0 %copy-start.1 = (bf16[2,128,128]{2,1,0:T(8,128)(2,1)S(1)}, bf16[2,128,128]{2,1,0:T(8,128)(2,1)}, u32[]{:S(2)}) copy-start(bf16[2,128,128]{2,1,0:T(8,128)(2,1)} %gw.3) | copy-start | bytes 196612
  19.8 10.0 %copy-start.2 = (bf16[2,128,128]{2,1,0:T(8,128)(2,1)S(1)}, bf16[2,128,128]{2,1,0:T(8,128)(2,1)}, u32[]{:S(2)}) copy-start(bf16[2,128,128]{2,1,0:T(8,128)(2,1)} %ow.3) | copy-start | bytes 196612

commit v8 on v6

--- a/solution.py
+++ b/solution.py
@@ -97,17 +97,17 @@
     gain, offset, bias = broadcast_columns(columns, u * EACH + 7, 3, width)
     turned = out_weight.T
     mixed[...] = summed[...].astype(F32).reshape(mixed.shape)
-    results = []
     for pair in range(0, OWN, 2):
         blocks = [mixed[pl.ds(i, mixed.shape[0] // OWN, stride=OWN), :] for i in (pair, pair + 1)]
         blocks = [reorder(v, ORDERS[u][1], ORDERS[u][0]) for v in blocks]
         hidden = jnp.concatenate([layer_norm(v, gain, offset).astype(BF16) for v in blocks], 1)
         both = jnp.dot(turned, hidden, preferred_element_type=F32)
+        results = []
         for n in range(2):
             change = both[:, n * width : (n + 1) * width] + bias
             at = slice((pair + n) * width, (pair + n + 1) * width)
             results.append((z[pair + n].astype(F32) + gate[:, at] * change).astype(BF16))
-    return results
+        yield results
 
 
 def first_kernel(
@@ -137,17 +137,25 @@
 
 def middle_kernel(summed, old, old_gate, columns, keep, pw, gw, ow, send, gate, turned, mixed, mixed_back):
     width = keep.shape[1]
-    z = finish(0, [old[:, i * width : (i + 1) * width] for i in range(OWN)], summed, old_gate, ow[0], columns, mixed_back)
+    pairs = finish(0, [old[:, i * width : (i + 1) * width] for i in range(OWN)], summed, old_gate, ow[0], columns, mixed_back)
+    z = [v for pair in pairs for v in pair]
     for i in range(OWN):
         turned[:, i * width : (i + 1) * width] = z[i]
     project(1, [v.astype(F32) for v in z], keep, pw[1], gw[1], columns, send, gate, mixed)
 
 
-def last_kernel(summed, old, old_gate, columns, ow, out, mixed_back):
+def last_kernel(summed, old, old_gate, columns, ow, out, ready, left, mixed_back):
     width = out.shape[1]
-    z = finish(1, [old[:, i * width : (i + 1) * width] for i in range(OWN)], summed, old_gate, ow[1], columns, mixed_back)
-    for i in range(OWN):
-        out[i] = z[i].T
+    z = [old[:, i * width : (i + 1) * width] for i in range(OWN)]
+    moves = []
+    for n, pair in enumerate(finish(1, z, summed, old_gate, ow[1], columns, mixed_back)):
+        here = pl.ds(2 * n, 2)
+        for i, v in enumerate(pair):
+            ready[2 * n + i] = v.T
+        moves.append(pltpu.make_async_copy(ready.at[here], out.at[here], left.at[n]))
+        moves[n].start()
+    for move in moves:
+        move.wait()
 
 
 def reorder(values, have, want):
@@ -170,13 +178,12 @@
     out[...] = pack(summed).astype(BF16)
 
 
-def call(kernel, outs, scratch, *args, place=pltpu.VMEM):
-    in_vmem = pl.BlockSpec(memory_space=pltpu.VMEM)
+def call(kernel, outs, scratch, *args, place=pltpu.VMEM, result=pltpu.VMEM):
     return pl.pallas_call(
         kernel,
         out_shape=[jax.ShapeDtypeStruct(*o) for o in outs],
         in_specs=[pl.BlockSpec(memory_space=place)] * len(args),
-        out_specs=[in_vmem] * len(outs),
+        out_specs=[pl.BlockSpec(memory_space=result)] * len(outs),
         scratch_shapes=scratch,
         compiler_params=pltpu.CompilerParams(vmem_limit_bytes=24 * 2**20),
     )(*args)
@@ -207,7 +214,9 @@
     (send,) = call(functools.partial(triangle_kernel, False), summed, [], exchange_in_order(send, ORDERS[0][0]))
     send, gate, turned = call(middle_kernel, projected, [mixed, back], exchange_in_order(send, ORDERS[0][1]), turned, gate, columns, keep, pw, gw, ow)
     (send,) = call(functools.partial(triangle_kernel, True), summed, [], exchange_in_order(send, ORDERS[1][0]))
-    (out,) = call(last_kernel, [(pair_rep.shape, BF16)], [back], exchange_in_order(send, ORDERS[1][1]), turned, gate, columns, ow)
+    held = [pltpu.VMEM(pair_rep.shape, BF16), pltpu.SemaphoreType.DMA((rows_of // 2,)), back]
+    send = exchange_in_order(send, ORDERS[1][1])
+    (out,) = call(last_kernel, [(pair_rep.shape, BF16)], held, send, turned, gate, columns, ow, result=pltpu.HBM)
     return out
 
 

time: 54.8 us -> 54.8 us (level)
  no operation moved by 1% of the time
where the time goes in v8:
time: 54.8 us; the launch traced here: 54.6 us
  blocking collectives  50.5 us (92%)
  Pallas kernels  3.94 us (7%)
    all_to_all x4, blocking collectives, exchange_in_order(): lax.all_to_all(blocks, 'row', split_axis=0, concat_axis=0, axis_index_gro...  50.5 us
    pallas_call x5, Pallas kernels, call(): pl.pallas_call(kernel, out_shape=[jax.ShapeDtypeStruct(*o) for o in outs]...  3.94 us

profile of v8, /device:TPU:0, one launch (start us, length us, event | category | flops | bytes accessed | tf_op | source)
XLA Modules:
  0.0 54.6 jit_solution(10888916837163566844)
XLA Ops:
  0.0 1.7 %shard_map.100 = (bf16[32,32,128]{2,1,0:T(8,128)(2,1)S(1)}, f32[128,512]{1,0:T(8,128)S(1)}, bf16[128,512]{1,0:T(8,128)(2,1)S(1)}, f32[128,32]{1,0:T(8,128)S(1)}, f32[8,128]{1,0:T(8,128)S(1)}) custom-call(bf16[4,128,128]{2,1,0:T(8,128)(2,1)} %pair.1, s32[4,128]{1,0:T(4,128)} %mask.1, bf16[2,128,512]{2,1,0:T(8,128)(2,1)} %pw.3, bf16[2,128,128]{2,1,0:T(8,128)(2,1)} %gw.3, ...), custom_call_target="tpu_custom_call" | custom-call | tf_op jit(solution)/shard_map/pallas_call | solution.py:182
  1.7 17.8 %all_to_all.20.sides = bf16[32,32,128]{2,1,0:T(8,128)(2,1)S(1)} all-to-all(bf16[32,32,128]{2,1,0:T(8,128)(2,1)S(1)} %get-tuple-element.13), channel_id=1, replica_groups={{0,1,30,31,22,23,28,29,26,27,20,21,18,19,14,15,24,25,10,11,16,17,12,13,..., dimensions={0} | all-to-all | bytes 524288 | tf_op jit(solution)/shard_map/all_to_all | solution.py:198
  19.5 0.0 copy-start
  19.5 0.2 shard_map.101
  19.7 0.0 copy-start.1
  19.8 0.0 copy-start.2
  19.8 9.9 %all_to_all.21.summed = bf16[32,16,128]{2,1,0:T(8,128)(2,1)S(1)} all-to-all(bf16[32,16,128]{2,1,0:T(8,128)(2,1)S(1)} %shard_map.101), channel_id=1, replica_groups={{0,1,30,31,22,23,28,29,26,27,20,21,18,19,14,15,24,25,10,11,16,17,12,13,..., dimensions={0} | all-to-all | bytes 262144 | tf_op jit(solution)/shard_map/all_to_all | solution.py:198
  29.7 0.0 copy-done
  29.7 0.0 copy-done.1
  29.7 0.0 copy-done.2
  29.7 0.8 %shard_map.102 = (bf16[32,32,128]{2,1,0:T(8,128)(2,1)S(1)}, f32[128,512]{1,0:T(8,128)S(1)}, bf16[128,512]{1,0:T(8,128)(2,1)S(1)}) custom-call(bf16[32,16,128]{2,1,0:T(8,128)(2,1)S(1)} %all_to_all.21.summed, bf16[128,512]{1,0:T(8,128)(2,1)S(1)} %get-tuple-element.14.old, f32[128,512]{1,0:T(8,128)S(1)} %get-tuple-element.15.old_gate, ...), custom_call_target="tpu_custom_call" | custom-call | tf_op jit(solution)/shard_map/pallas_call | solution.py:182
  30.5 12.9 %all_to_all.22.sides = bf16[32,32,128]{2,1,0:T(8,128)(2,1)S(1)} all-to-all(bf16[32,32,128]{2,1,0:T(8,128)(2,1)S(1)} %get-tuple-element.18), channel_id=1, replica_groups={{0,1,30,31,22,23,28,29,26,27,20,21,18,19,14,15,24,25,10,11,16,17,12,13,..., dimensions={0} | all-to-all | bytes 524288 | tf_op jit(solution)/shard_map/all_to_all | solution.py:198
  43.4 0.2 shard_map.103
  43.6 9.9 %all_to_all.23.summed = bf16[32,16,128]{2,1,0:T(8,128)(2,1)S(1)} all-to-all(bf16[32,16,128]{2,1,0:T(8,128)(2,1)S(1)} %shard_map.103), channel_id=1, replica_groups={{0,1,30,31,22,23,28,29,26,27,20,21,18,19,14,15,24,25,10,11,16,17,12,13,..., dimensions={0} | all-to-all | bytes 262144 | tf_op jit(solution)/shard_map/all_to_all | solution.py:198
  53.5 1.0 %shard_map.104 = bf16[4,128,128]{2,1,0:T(8,128)(2,1)} custom-call(bf16[32,16,128]{2,1,0:T(8,128)(2,1)S(1)} %all_to_all.23.summed, bf16[128,512]{1,0:T(8,128)(2,1)S(1)} %get-tuple-element.19.old, f32[128,512]{1,0:T(8,128)S(1)} %get-tuple-element.20.old_gate, f32[128,32]{1,0:T(8,128)S(1)} %get-tuple-element.16.columns, bf16[2,128,128]{2,1,0:T(8,128)(2,1)S(1)} %copy-done.2), custom_call_target="tpu_custom_call" | custom-call | tf_op jit(solution)/shard_map/pallas_call | solution.py:182
Async XLA Ops:
  19.5 10.2 %copy-start = (bf16[2,128,512]{2,1,0:T(8,128)(2,1)S(1)}, bf16[2,128,512]{2,1,0:T(8,128)(2,1)}, u32[]{:S(2)}) copy-start(bf16[2,128,512]{2,1,0:T(8,128)(2,1)} %pw.3) | copy-start | bytes 786436
  19.7 10.0 %copy-start.1 = (bf16[2,128,128]{2,1,0:T(8,128)(2,1)S(1)}, bf16[2,128,128]{2,1,0:T(8,128)(2,1)}, u32[]{:S(2)}) copy-start(bf16[2,128,128]{2,1,0:T(8,128)(2,1)} %gw.3) | copy-start | bytes 196612
  19.8 10.0 %copy-start.2 = (bf16[2,128,128]{2,1,0:T(8,128)(2,1)S(1)}, bf16[2,128,128]{2,1,0:T(8,128)(2,1)}, u32[]{:S(2)}) copy-start(bf16[2,128,128]{2,1,0:T(8,128)(2,1)} %ow.3) | copy-start | bytes 196612

commit v9 on v6

--- a/solution.py
+++ b/solution.py
@@ -30,6 +30,13 @@
     centred = values - average
     variance = jnp.mean(centred * centred, 0, keepdims=True)
     return centred * lax.rsqrt(variance + 1e-05) * norm_gain + norm_bias
+
+
+def short_norm(values, norm_gain, norm_bias):
+    distance = values - values[0:1, :]
+    average = jnp.mean(distance, 0, keepdims=True)
+    variance = jnp.mean(distance * distance, 0, keepdims=True) - average * average
+    return (distance - average) * lax.rsqrt(variance + 1e-05) * norm_gain + norm_bias
 
 
 def pack(blocks):
@@ -73,7 +80,7 @@
     turned = [(w * jnp.asarray(k, BF16)).T if k != 1.0 else w.T for w, k in zip(turned, scales)]
     pairs = []
     for pair in range(0, OWN, 2):
-        normed = [layer_norm(z[i], gain, offset).astype(BF16) for i in (pair, pair + 1)]
+        normed = [short_norm(z[i], gain, offset).astype(BF16) for i in (pair, pair + 1)]
         pairs.append(jnp.concatenate(normed, 1))
     for side in range(2):
         for pair, normed in enumerate(pairs):
@@ -101,7 +108,7 @@
     for pair in range(0, OWN, 2):
         blocks = [mixed[pl.ds(i, mixed.shape[0] // OWN, stride=OWN), :] for i in (pair, pair + 1)]
         blocks = [reorder(v, ORDERS[u][1], ORDERS[u][0]) for v in blocks]
-        hidden = jnp.concatenate([layer_norm(v, gain, offset).astype(BF16) for v in blocks], 1)
+        hidden = jnp.concatenate([short_norm(v, gain, offset).astype(BF16) for v in blocks], 1)
         both = jnp.dot(turned, hidden, preferred_element_type=F32)
         for n in range(2):
             change = both[:, n * width : (n + 1) * width] + bias

time: 54.8 us -> 54.8 us (level)
  no operation moved by 1% of the time
where the time goes in v9:
time: 54.8 us; the launch traced here: 54.5 us
  blocking collectives  50.5 us (92%)
  Pallas kernels  3.94 us (7%)
    all_to_all x4, blocking collectives, exchange_in_order(): lax.all_to_all(blocks, 'row', split_axis=0, concat_axis=0, axis_index_gro...  50.5 us
    pallas_call x5, Pallas kernels, call(): pl.pallas_call(kernel, out_shape=[jax.ShapeDtypeStruct(*o) for o in outs]...  3.94 us

profile of v9, /device:TPU:0, one launch (start us, length us, event | category | flops | bytes accessed | tf_op | source)
XLA Modules:
  0.0 54.5 jit_solution(1205021251206451806)
XLA Ops:
  0.0 1.7 %shard_map.100 = (bf16[32,32,128]{2,1,0:T(8,128)(2,1)S(1)}, f32[128,512]{1,0:T(8,128)S(1)}, bf16[128,512]{1,0:T(8,128)(2,1)S(1)}, f32[128,32]{1,0:T(8,128)S(1)}, f32[8,128]{1,0:T(8,128)S(1)}) custom-call(bf16[4,128,128]{2,1,0:T(8,128)(2,1)} %pair.1, s32[4,128]{1,0:T(4,128)} %mask.1, bf16[2,128,512]{2,1,0:T(8,128)(2,1)} %pw.3, bf16[2,128,128]{2,1,0:T(8,128)(2,1)} %gw.3, ...), custom_call_target="tpu_custom_call" | custom-call | tf_op jit(solution)/shard_map/pallas_call | solution.py:182
  1.7 17.8 %all_to_all.20.sides = bf16[32,32,128]{2,1,0:T(8,128)(2,1)S(1)} all-to-all(bf16[32,32,128]{2,1,0:T(8,128)(2,1)S(1)} %get-tuple-element.13), channel_id=1, replica_groups={{0,1,30,31,22,23,28,29,26,27,20,21,18,19,14,15,24,25,10,11,16,17,12,13,..., dimensions={0} | all-to-all | bytes 524288 | tf_op jit(solution)/shard_map/all_to_all | solution.py:198
  19.5 0.0 copy-start
  19.5 0.2 shard_map.101
  19.7 0.0 copy-start.1
  19.7 0.0 copy-start.2
  19.8 9.9 %all_to_all.21.summed = bf16[32,16,128]{2,1,0:T(8,128)(2,1)S(1)} all-to-all(bf16[32,16,128]{2,1,0:T(8,128)(2,1)S(1)} %shard_map.101), channel_id=1, replica_groups={{0,1,30,31,22,23,28,29,26,27,20,21,18,19,14,15,24,25,10,11,16,17,12,13,..., dimensions={0} | all-to-all | bytes 262144 | tf_op jit(solution)/shard_map/all_to_all | solution.py:198
  29.7 0.0 copy-done
  29.7 0.0 copy-done.1
  29.7 0.0 copy-done.2
  29.7 0.8 %shard_map.102 = (bf16[32,32,128]{2,1,0:T(8,128)(2,1)S(1)}, f32[128,512]{1,0:T(8,128)S(1)}, bf16[128,512]{1,0:T(8,128)(2,1)S(1)}) custom-call(bf16[32,16,128]{2,1,0:T(8,128)(2,1)S(1)} %all_to_all.21.summed, bf16[128,512]{1,0:T(8,128)(2,1)S(1)} %get-tuple-element.14.old, f32[128,512]{1,0:T(8,128)S(1)} %get-tuple-element.15.old_gate, ...), custom_call_target="tpu_custom_call" | custom-call | tf_op jit(solution)/shard_map/pallas_call | solution.py:182
  30.5 12.9 %all_to_all.22.sides = bf16[32,32,128]{2,1,0:T(8,128)(2,1)S(1)} all-to-all(bf16[32,32,128]{2,1,0:T(8,128)(2,1)S(1)} %get-tuple-element.18), channel_id=1, replica_groups={{0,1,30,31,22,23,28,29,26,27,20,21,18,19,14,15,24,25,10,11,16,17,12,13,..., dimensions={0} | all-to-all | bytes 524288 | tf_op jit(solution)/shard_map/all_to_all | solution.py:198
  43.3 0.2 shard_map.103
  43.6 9.9 %all_to_all.23.summed = bf16[32,16,128]{2,1,0:T(8,128)(2,1)S(1)} all-to-all(bf16[32,16,128]{2,1,0:T(8,128)(2,1)S(1)} %shard_map.103), channel_id=1, replica_groups={{0,1,30,31,22,23,28,29,26,27,20,21,18,19,14,15,24,25,10,11,16,17,12,13,..., dimensions={0} | all-to-all | bytes 262144 | tf_op jit(solution)/shard_map/all_to_all | solution.py:198
  53.5 1.0 %shard_map.104 = bf16[4,128,128]{2,1,0:T(8,128)(2,1)} custom-call(bf16[32,16,128]{2,1,0:T(8,128)(2,1)S(1)} %all_to_all.23.summed, bf16[128,512]{1,0:T(8,128)(2,1)S(1)} %get-tuple-element.19.old, f32[128,512]{1,0:T(8,128)S(1)} %get-tuple-element.20.old_gate, f32[128,32]{1,0:T(8,128)S(1)} %get-tuple-element.16.columns, bf16[2,128,128]{2,1,0:T(8,128)(2,1)S(1)} %copy-done.2), custom_call_target="tpu_custom_call" | custom-call | tf_op jit(solution)/shard_map/pallas_call | solution.py:182
Async XLA Ops:
  19.5 10.2 %copy-start = (bf16[2,128,512]{2,1,0:T(8,128)(2,1)S(1)}, bf16[2,128,512]{2,1,0:T(8,128)(2,1)}, u32[]{:S(2)}) copy-start(bf16[2,128,512]{2,1,0:T(8,128)(2,1)} %pw.3) | copy-start | bytes 786436
  19.7 10.0 %copy-start.1 = (bf16[2,128,128]{2,1,0:T(8,128)(2,1)S(1)}, bf16[2,128,128]{2,1,0:T(8,128)(2,1)}, u32[]{:S(2)}) copy-start(bf16[2,128,128]{2,1,0:T(8,128)(2,1)} %gw.3) | copy-start | bytes 196612
  19.7 10.0 %copy-start.2 = (bf16[2,128,128]{2,1,0:T(8,128)(2,1)S(1)}, bf16[2,128,128]{2,1,0:T(8,128)(2,1)}, u32[]{:S(2)}) copy-start(bf16[2,128,128]{2,1,0:T(8,128)(2,1)} %ow.3) | copy-start | bytes 196612

commit v10 on v6

--- a/solution.py
+++ b/solution.py
@@ -62,14 +62,14 @@
     return [jnp.broadcast_to(held[:, n : n + 1], (held.shape[0], width)) for n in range(first, first + many)]
 
 
-def project(u, z, mask, proj_weight, gate_weight, columns, send, gate, mixed):
+def project(u, z, mask, proj_weight, columns, send, norm, mixed):
     width = z[0].shape[1]
     h = proj_weight.shape[1] // 4
     rows = mixed.shape[1]
-    gain, offset, *biases = broadcast_columns(columns, u * EACH, 7, width)
-    scales = (1.0, 0.5, 1.0, 0.5, 0.5)
+    gain, offset, *biases = broadcast_columns(columns, u * EACH, 6, width)
+    scales = (1.0, 0.5, 1.0, 0.5)
     biases = [b * k for b, k in zip(biases, scales)]
-    turned = [proj_weight[:, n * h : (n + 1) * h] for n in range(4)] + [gate_weight]
+    turned = [proj_weight[:, n * h : (n + 1) * h] for n in range(4)]
     turned = [(w * jnp.asarray(k, BF16)).T if k != 1.0 else w.T for w, k in zip(turned, scales)]
     pairs = []
     for pair in range(0, OWN, 2):
@@ -86,10 +86,19 @@
     for side in range(2):
         send[:, side * 16 : (side + 1) * 16, :] = mixed[side].reshape(rows // 16, 16, width).astype(BF16)
     for pair, normed in enumerate(pairs):
-        gating = jnp.dot(turned[4], normed, preferred_element_type=F32)
-        for n in range(2):
-            i = 2 * pair + n
-            gate[:, i * width : (i + 1) * width] = 0.5 * jnp.tanh(gating[:, n * width : (n + 1) * width] + biases[4]) + 0.5
+        norm[:, 2 * pair * width : 2 * (pair + 1) * width] = normed
+
+
+def output_gate(u, norm, gate_weight, columns):
+    width = norm.shape[1] // OWN
+    turned = (gate_weight * jnp.asarray(0.5, BF16)).T
+    (bias,) = broadcast_columns(columns, u * EACH + 6, 1, 2 * width)
+    gates = []
+    for pair in range(OWN // 2):
+        gating = jnp.dot(turned, norm[:, 2 * pair * width : 2 * (pair + 1) * width], preferred_element_type=F32)
+        gate = 0.5 * jnp.tanh(gating + 0.5 * bias) + 0.5
+        gates += [gate[:, :width], gate[:, width:]]
+    return gates
 
 
 def finish(u, z, summed, gate, out_weight, columns, mixed):
@@ -105,16 +114,15 @@
         both = jnp.dot(turned, hidden, preferred_element_type=F32)
         for n in range(2):
             change = both[:, n * width : (n + 1) * width] + bias
-            at = slice((pair + n) * width, (pair + n + 1) * width)
-            results.append((z[pair + n].astype(F32) + gate[:, at] * change).astype(BF16))
+            results.append((z[pair + n].astype(F32) + gate[pair + n] * change).astype(BF16))
     return results
 
 
 def first_kernel(
-    pair, mask, pw, gw, pb, gb, ob, ns, no, send, gate, turned, columns, keep, pair_in, mask_in, pw_in, gw_in, pb_in, gb_in, ob_in, ns_in, no_in, rows, arrived, mixed
+    pair, mask, pw, pb, gb, ob, ns, no, send, norm, turned, columns, keep, pair_in, mask_in, pw_in, pb_in, gb_in, ob_in, ns_in, no_in, rows, arrived, mixed
 ):
     moves = [(pair, pair_in), (pb, pb_in), (gb, gb_in), (ob, ob_in), (ns, ns_in), (no, no_in)]
-    moves += [(pw.at[0], pw_in), (gw.at[0], gw_in), (mask, mask_in)]
+    moves += [(pw.at[0], pw_in), (mask, mask_in)]
     moves = [pltpu.make_async_copy(a, b, arrived.at[n]) for n, (a, b) in enumerate(moves)]
     for move in moves:
         move.start()
@@ -132,20 +140,22 @@
             rows[u * EACH + n : u * EACH + n + 1, :] = row
     columns[...] = rows[...].T
     keep[0:OWN, :] = mask_in[...].astype(F32)
-    project(0, [v.astype(F32) for v in z], keep, pw_in[...], gw_in[...], columns, send, gate, mixed)
-
-
-def middle_kernel(summed, old, old_gate, columns, keep, pw, gw, ow, send, gate, turned, mixed, mixed_back):
+    project(0, [v.astype(F32) for v in z], keep, pw_in[...], columns, send, norm, mixed)
+
+
+def middle_kernel(summed, old, old_norm, columns, keep, pw, gw, ow, send, norm, turned, mixed, mixed_back):
     width = keep.shape[1]
-    z = finish(0, [old[:, i * width : (i + 1) * width] for i in range(OWN)], summed, old_gate, ow[0], columns, mixed_back)
+    gate = output_gate(0, old_norm, gw[0], columns)
+    z = finish(0, [old[:, i * width : (i + 1) * width] for i in range(OWN)], summed, gate, ow[0], columns, mixed_back)
     for i in range(OWN):
         turned[:, i * width : (i + 1) * width] = z[i]
-    project(1, [v.astype(F32) for v in z], keep, pw[1], gw[1], columns, send, gate, mixed)
-
-
-def last_kernel(summed, old, old_gate, columns, ow, out, mixed_back):
+    project(1, [v.astype(F32) for v in z], keep, pw[1], columns, send, norm, mixed)
+
+
+def last_kernel(summed, old, old_norm, columns, gw, ow, out, mixed_back):
     width = out.shape[1]
-    z = finish(1, [old[:, i * width : (i + 1) * width] for i in range(OWN)], summed, old_gate, ow[1], columns, mixed_back)
+    gate = output_gate(1, old_norm, gw[1], columns)
+    z = finish(1, [old[:, i * width : (i + 1) * width] for i in range(OWN)], summed, gate, ow[1], columns, mixed_back)
     for i in range(OWN):
         out[i] = z[i].T
 
@@ -194,20 +204,20 @@
 def packed_updates(count, pair_rep, pair_mask, pw, pb, gw, gb, ow, ob, ns, no):
     rows_of, width, channels = pair_rep.shape
     flat = (channels, rows_of * width)
-    projected = [((count, 32, width), BF16), (flat, F32), (flat, BF16)]
+    projected = [((count, 32, width), BF16), (flat, BF16), (flat, BF16)]
     summed = [((count, 16, width), BF16)]
-    params = [pair_rep, pair_mask, pw, gw, pb, gb, ob, ns, no]
+    params = [pair_rep, pair_mask, pw, pb, gb, ob, ns, no]
     params = [pltpu.with_memory_space_constraint(v, pltpu.HBM) for v in params]
-    held = [pltpu.VMEM(v.shape[1:] if n in (2, 3) else v.shape, v.dtype) for n, v in enumerate(params)]
+    held = [pltpu.VMEM(v.shape[1:] if n == 2 else v.shape, v.dtype) for n, v in enumerate(params)]
     held += [pltpu.VMEM((2 * EACH, channels), F32), pltpu.SemaphoreType.DMA((len(params),))]
     back = pltpu.VMEM((OWN * channels, width), F32)
     mixed = pltpu.VMEM((2, OWN * channels, width), F32)
     kept = [((channels, 2 * EACH), F32), ((2 * OWN, width), F32)]
-    send, gate, turned, columns, keep = call(first_kernel, projected + kept, held + [mixed], *params, place=pltpu.HBM)
+    send, norm, turned, columns, keep = call(first_kernel, projected + kept, held + [mixed], *params, place=pltpu.HBM)
     (send,) = call(functools.partial(triangle_kernel, False), summed, [], exchange_in_order(send, ORDERS[0][0]))
-    send, gate, turned = call(middle_kernel, projected, [mixed, back], exchange_in_order(send, ORDERS[0][1]), turned, gate, columns, keep, pw, gw, ow)
+    send, norm, turned = call(middle_kernel, projected, [mixed, back], exchange_in_order(send, ORDERS[0][1]), turned, norm, columns, keep, pw, gw, ow)
     (send,) = call(functools.partial(triangle_kernel, True), summed, [], exchange_in_order(send, ORDERS[1][0]))
-    (out,) = call(last_kernel, [(pair_rep.shape, BF16)], [back], exchange_in_order(send, ORDERS[1][1]), turned, gate, columns, ow)
+    (out,) = call(last_kernel, [(pair_rep.shape, BF16)], [back], exchange_in_order(send, ORDERS[1][1]), turned, norm, columns, gw, ow)
     return out
 
 

time: 54.8 us -> 54.8 us (level)
  no operation moved by 1% of the time
where the time goes in v10:
time: 54.8 us; the launch traced here: 54.6 us
  blocking collectives  50.5 us (92%)
  Pallas kernels  3.96 us (7%)
    all_to_all x4, blocking collectives, exchange_in_order(): lax.all_to_all(blocks, 'row', split_axis=0, concat_axis=0, axis_index_gro...  50.5 us
    pallas_call x5, Pallas kernels, call(): pl.pallas_call(kernel, out_shape=[jax.ShapeDtypeStruct(*o) for o in outs]...  3.96 us

profile of v10, /device:TPU:0, one launch (start us, length us, event | category | flops | bytes accessed | tf_op | source)
XLA Modules:
  0.0 54.6 jit_solution(4058350648194721313)
XLA Ops:
  0.0 1.7 %shard_map.100 = (bf16[32,32,128]{2,1,0:T(8,128)(2,1)S(1)}, bf16[128,512]{1,0:T(8,128)(2,1)S(1)}, bf16[128,512]{1,0:T(8,128)(2,1)S(1)}, f32[128,32]{1,0:T(8,128)S(1)}, f32[8,128]{1,0:T(8,128)S(1)}) custom-call(bf16[4,128,128]{2,1,0:T(8,128)(2,1)} %pair.1, s32[4,128]{1,0:T(4,128)} %mask.1, bf16[2,128,512]{2,1,0:T(8,128)(2,1)} %pw.3, f32[2,512]{1,0:T(2,128)} %pb.1, ...), custom_call_target="tpu_custom_call" | custom-call | tf_op jit(solution)/shard_map/pallas_call | solution.py:185
  1.7 17.8 %all_to_all.20.sides = bf16[32,32,128]{2,1,0:T(8,128)(2,1)S(1)} all-to-all(bf16[32,32,128]{2,1,0:T(8,128)(2,1)S(1)} %get-tuple-element.13), channel_id=1, replica_groups={{0,1,30,31,22,23,28,29,26,27,20,21,18,19,14,15,24,25,10,11,16,17,12,13,..., dimensions={0} | all-to-all | bytes 524288 | tf_op jit(solution)/shard_map/all_to_all | solution.py:201
  19.5 0.0 copy-start
  19.5 0.2 shard_map.101
  19.7 0.0 copy-start.1
  19.7 0.0 copy-start.2
  19.7 9.9 %all_to_all.21.summed = bf16[32,16,128]{2,1,0:T(8,128)(2,1)S(1)} all-to-all(bf16[32,16,128]{2,1,0:T(8,128)(2,1)S(1)} %shard_map.101), channel_id=1, replica_groups={{0,1,30,31,22,23,28,29,26,27,20,21,18,19,14,15,24,25,10,11,16,17,12,13,..., dimensions={0} | all-to-all | bytes 262144 | tf_op jit(solution)/shard_map/all_to_all | solution.py:201
  29.7 0.0 copy-done
  29.7 0.0 copy-done.1
  29.7 0.0 copy-done.2
  29.7 0.8 %shard_map.102 = (bf16[32,32,128]{2,1,0:T(8,128)(2,1)S(1)}, bf16[128,512]{1,0:T(8,128)(2,1)S(1)}, bf16[128,512]{1,0:T(8,128)(2,1)S(1)}) custom-call(bf16[32,16,128]{2,1,0:T(8,128)(2,1)S(1)} %all_to_all.21.summed, bf16[128,512]{1,0:T(8,128)(2,1)S(1)} %get-tuple-element.14.old, bf16[128,512]{1,0:T(8,128)(2,1)S(1)} %get-tuple-element.15.old_norm, ...), custom_call_target="tpu_custom_call" | custom-call | tf_op jit(solution)/shard_map/pallas_call | solution.py:185
  30.5 12.9 %all_to_all.22.sides = bf16[32,32,128]{2,1,0:T(8,128)(2,1)S(1)} all-to-all(bf16[32,32,128]{2,1,0:T(8,128)(2,1)S(1)} %get-tuple-element.18), channel_id=1, replica_groups={{0,1,30,31,22,23,28,29,26,27,20,21,18,19,14,15,24,25,10,11,16,17,12,13,..., dimensions={0} | all-to-all | bytes 524288 | tf_op jit(solution)/shard_map/all_to_all | solution.py:201
  43.3 0.2 shard_map.103
  43.6 9.9 %all_to_all.23.summed = bf16[32,16,128]{2,1,0:T(8,128)(2,1)S(1)} all-to-all(bf16[32,16,128]{2,1,0:T(8,128)(2,1)S(1)} %shard_map.103), channel_id=1, replica_groups={{0,1,30,31,22,23,28,29,26,27,20,21,18,19,14,15,24,25,10,11,16,17,12,13,..., dimensions={0} | all-to-all | bytes 262144 | tf_op jit(solution)/shard_map/all_to_all | solution.py:201
  53.5 1.1 %shard_map.104 = bf16[4,128,128]{2,1,0:T(8,128)(2,1)} custom-call(bf16[32,16,128]{2,1,0:T(8,128)(2,1)S(1)} %all_to_all.23.summed, bf16[128,512]{1,0:T(8,128)(2,1)S(1)} %get-tuple-element.19.old, bf16[128,512]{1,0:T(8,128)(2,1)S(1)} %get-tuple-element.20.old_norm, f32[128,32]{1,0:T(8,128)S(1)} %get-tuple-element.16.columns, ...), custom_call_target="tpu_custom_call" | custom-call | tf_op jit(solution)/shard_map/pallas_call | solution.py:185
Async XLA Ops:
  19.5 10.2 %copy-start = (bf16[2,128,512]{2,1,0:T(8,128)(2,1)S(1)}, bf16[2,128,512]{2,1,0:T(8,128)(2,1)}, u32[]{:S(2)}) copy-start(bf16[2,128,512]{2,1,0:T(8,128)(2,1)} %pw.3) | copy-start | bytes 786436
  19.7 10.0 %copy-start.1 = (bf16[2,128,128]{2,1,0:T(8,128)(2,1)S(1)}, bf16[2,128,128]{2,1,0:T(8,128)(2,1)}, u32[]{:S(2)}) copy-start(bf16[2,128,128]{2,1,0:T(8,128)(2,1)} %gw.3) | copy-start | bytes 196612
  19.7 10.0 %copy-start.2 = (bf16[2,128,128]{2,1,0:T(8,128)(2,1)S(1)}, bf16[2,128,128]{2,1,0:T(8,128)(2,1)}, u32[]{:S(2)}) copy-start(bf16[2,128,128]{2,1,0:T(8,128)(2,1)} %ow.3) | copy-start | bytes 196612

commit v11 on v6

--- a/solution.py
+++ b/solution.py
@@ -10,8 +10,8 @@
 PEERS = ("row", "ka")
 OWN = 4
 ORDERS = (
-    ((0, 15, 11, 14, 13, 10, 9, 7, 12, 5, 8, 6, 4, 3, 2, 1), (0, 15, 11, 14, 13, 10, 9, 7, 12, 5, 8, 6, 4, 3, 2, 1)),
-    ((0, 15, 11, 14, 13, 10, 9, 7, 12, 5, 8, 6, 4, 3, 2, 1), (0, 15, 11, 14, 13, 10, 9, 7, 12, 5, 8, 6, 4, 3, 2, 1)),
+    ((0, 4, 8, 12, 1, 5, 9, 13, 2, 6, 10, 14, 3, 7, 11, 15), (0, 15, 11, 14, 13, 10, 9, 7, 12, 5, 8, 6, 4, 3, 2, 1)),
+    ((0, 4, 8, 12, 1, 5, 9, 13, 2, 6, 10, 14, 3, 7, 11, 15), (0, 15, 11, 14, 13, 10, 9, 7, 12, 5, 8, 6, 4, 3, 2, 1)),
 )
 EACH = 16
 BF16, F32 = jnp.bfloat16, jnp.float32

time: 54.8 us -> 54.6 us (level)
  no operation moved by 1% of the time
where the time goes in v11:
time: 54.6 us; the launch traced here: 54.4 us
  blocking collectives  50.3 us (92%)
  Pallas kernels  3.96 us (7%)
    all_to_all x4, blocking collectives, exchange_in_order(): lax.all_to_all(blocks, 'row', split_axis=0, concat_axis=0, axis_index_gro...  50.3 us
    pallas_call x5, Pallas kernels, call(): pl.pallas_call(kernel, out_shape=[jax.ShapeDtypeStruct(*o) for o in outs]...  3.96 us

profile of v11, /device:TPU:0, one launch (start us, length us, event | category | flops | bytes accessed | tf_op | source)
XLA Modules:
  0.0 54.4 jit_solution(4244621813708049397)
XLA Ops:
  0.0 1.7 %shard_map.100 = (bf16[32,32,128]{2,1,0:T(8,128)(2,1)S(1)}, f32[128,512]{1,0:T(8,128)S(1)}, bf16[128,512]{1,0:T(8,128)(2,1)S(1)}, f32[128,32]{1,0:T(8,128)S(1)}, f32[8,128]{1,0:T(8,128)S(1)}) custom-call(bf16[4,128,128]{2,1,0:T(8,128)(2,1)} %pair.1, s32[4,128]{1,0:T(4,128)} %mask.1, bf16[2,128,512]{2,1,0:T(8,128)(2,1)} %pw.3, bf16[2,128,128]{2,1,0:T(8,128)(2,1)} %gw.3, ...), custom_call_target="tpu_custom_call" | custom-call | tf_op jit(solution)/shard_map/pallas_call | solution.py:175
  1.7 17.5 %all_to_all.20.sides = bf16[32,32,128]{2,1,0:T(8,128)(2,1)S(1)} all-to-all(bf16[32,32,128]{2,1,0:T(8,128)(2,1)S(1)} %get-tuple-element.13), channel_id=1, replica_groups={{0,1,8,9,16,17,24,25,2,3,10,11,18,19,26,27,4,5,12,13,20,21,28,29,6,7,14..., dimensions={0} | all-to-all | bytes 524288 | tf_op jit(solution)/shard_map/all_to_all | solution.py:191
  19.2 0.0 copy-start
  19.2 0.2 shard_map.101
  19.4 0.0 copy-start.1
  19.5 0.0 copy-start.2
  19.5 10.2 %all_to_all.21.summed = bf16[32,16,128]{2,1,0:T(8,128)(2,1)S(1)} all-to-all(bf16[32,16,128]{2,1,0:T(8,128)(2,1)S(1)} %shard_map.101), channel_id=1, replica_groups={{0,1,30,31,22,23,28,29,26,27,20,21,18,19,14,15,24,25,10,11,16,17,12,13,..., dimensions={0} | all-to-all | bytes 262144 | tf_op jit(solution)/shard_map/all_to_all | solution.py:191
  29.6 0.0 copy-done
  29.6 0.0 copy-done.1
  29.6 0.0 copy-done.2
  29.6 0.8 %shard_map.102 = (bf16[32,32,128]{2,1,0:T(8,128)(2,1)S(1)}, f32[128,512]{1,0:T(8,128)S(1)}, bf16[128,512]{1,0:T(8,128)(2,1)S(1)}) custom-call(bf16[32,16,128]{2,1,0:T(8,128)(2,1)S(1)} %all_to_all.21.summed, bf16[128,512]{1,0:T(8,128)(2,1)S(1)} %get-tuple-element.14.old, f32[128,512]{1,0:T(8,128)S(1)} %get-tuple-element.15.old_gate, ...), custom_call_target="tpu_custom_call" | custom-call | tf_op jit(solution)/shard_map/pallas_call | solution.py:175
  30.4 12.6 %all_to_all.22.sides = bf16[32,32,128]{2,1,0:T(8,128)(2,1)S(1)} all-to-all(bf16[32,32,128]{2,1,0:T(8,128)(2,1)S(1)} %get-tuple-element.18), channel_id=1, replica_groups={{0,1,8,9,16,17,24,25,2,3,10,11,18,19,26,27,4,5,12,13,20,21,28,29,6,7,14..., dimensions={0} | all-to-all | bytes 524288 | tf_op jit(solution)/shard_map/all_to_all | solution.py:191
  43.0 0.2 shard_map.103
  43.2 10.2 %all_to_all.23.summed = bf16[32,16,128]{2,1,0:T(8,128)(2,1)S(1)} all-to-all(bf16[32,16,128]{2,1,0:T(8,128)(2,1)S(1)} %shard_map.103), channel_id=1, replica_groups={{0,1,30,31,22,23,28,29,26,27,20,21,18,19,14,15,24,25,10,11,16,17,12,13,..., dimensions={0} | all-to-all | bytes 262144 | tf_op jit(solution)/shard_map/all_to_all | solution.py:191
  53.4 1.0 %shard_map.104 = bf16[4,128,128]{2,1,0:T(8,128)(2,1)} custom-call(bf16[32,16,128]{2,1,0:T(8,128)(2,1)S(1)} %all_to_all.23.summed, bf16[128,512]{1,0:T(8,128)(2,1)S(1)} %get-tuple-element.19.old, f32[128,512]{1,0:T(8,128)S(1)} %get-tuple-element.20.old_gate, f32[128,32]{1,0:T(8,128)S(1)} %get-tuple-element.16.columns, bf16[2,128,128]{2,1,0:T(8,128)(2,1)S(1)} %copy-done.2), custom_call_target="tpu_custom_call" | custom-call | tf_op jit(solution)/shard_map/pallas_call | solution.py:175
Async XLA Ops:
  19.2 10.4 %copy-start = (bf16[2,128,512]{2,1,0:T(8,128)(2,1)S(1)}, bf16[2,128,512]{2,1,0:T(8,128)(2,1)}, u32[]{:S(2)}) copy-start(bf16[2,128,512]{2,1,0:T(8,128)(2,1)} %pw.3) | copy-start | bytes 786436
  19.4 10.2 %copy-start.1 = (bf16[2,128,128]{2,1,0:T(8,128)(2,1)S(1)}, bf16[2,128,128]{2,1,0:T(8,128)(2,1)}, u32[]{:S(2)}) copy-start(bf16[2,128,128]{2,1,0:T(8,128)(2,1)} %gw.3) | copy-start | bytes 196612
  19.5 10.2 %copy-start.2 = (bf16[2,128,128]{2,1,0:T(8,128)(2,1)S(1)}, bf16[2,128,128]{2,1,0:T(8,128)(2,1)}, u32[]{:S(2)}) copy-start(bf16[2,128,128]{2,1,0:T(8,128)(2,1)} %ow.3) | copy-start | bytes 196612

commit v12 on v11

--- a/solution.py
+++ b/solution.py
@@ -10,8 +10,8 @@
 PEERS = ("row", "ka")
 OWN = 4
 ORDERS = (
-    ((0, 4, 8, 12, 1, 5, 9, 13, 2, 6, 10, 14, 3, 7, 11, 15), (0, 15, 11, 14, 13, 10, 9, 7, 12, 5, 8, 6, 4, 3, 2, 1)),
-    ((0, 4, 8, 12, 1, 5, 9, 13, 2, 6, 10, 14, 3, 7, 11, 15), (0, 15, 11, 14, 13, 10, 9, 7, 12, 5, 8, 6, 4, 3, 2, 1)),
+    ((0, 4, 8, 12, 1, 5, 9, 13, 2, 6, 10, 14, 3, 7, 11, 15), (0, 15, 11, 7, 3, 14, 10, 6, 2, 13, 9, 5, 1, 12, 8, 4)),
+    ((0, 15, 11, 7, 3, 14, 10, 6, 2, 13, 9, 5, 1, 12, 8, 4), (0, 15, 11, 7, 3, 14, 10, 6, 2, 13, 9, 5, 1, 12, 8, 4)),
 )
 EACH = 16
 BF16, F32 = jnp.bfloat16, jnp.float32

time: 54.6 us -> 54.2 us (level)
  no operation moved by 1% of the time
where the time goes in v12:
time: 54.2 us; the launch traced here: 54 us
  blocking collectives  50 us (92%)
  Pallas kernels  3.95 us (7%)
    all_to_all x4, blocking collectives, exchange_in_order(): lax.all_to_all(blocks, 'row', split_axis=0, concat_axis=0, axis_index_gro...  50 us
    pallas_call x5, Pallas kernels, call(): pl.pallas_call(kernel, out_shape=[jax.ShapeDtypeStruct(*o) for o in outs]...  3.95 us

profile of v12, /device:TPU:0, one launch (start us, length us, event | category | flops | bytes accessed | tf_op | source)
XLA Modules:
  0.0 54.0 jit_solution(1814763917204080238)
XLA Ops:
  0.0 1.7 %shard_map.100 = (bf16[32,32,128]{2,1,0:T(8,128)(2,1)S(1)}, f32[128,512]{1,0:T(8,128)S(1)}, bf16[128,512]{1,0:T(8,128)(2,1)S(1)}, f32[128,32]{1,0:T(8,128)S(1)}, f32[8,128]{1,0:T(8,128)S(1)}) custom-call(bf16[4,128,128]{2,1,0:T(8,128)(2,1)} %pair.1, s32[4,128]{1,0:T(4,128)} %mask.1, bf16[2,128,512]{2,1,0:T(8,128)(2,1)} %pw.3, bf16[2,128,128]{2,1,0:T(8,128)(2,1)} %gw.3, ...), custom_call_target="tpu_custom_call" | custom-call | tf_op jit(solution)/shard_map/pallas_call | solution.py:175
  1.7 17.5 %all_to_all.20.sides = bf16[32,32,128]{2,1,0:T(8,128)(2,1)S(1)} all-to-all(bf16[32,32,128]{2,1,0:T(8,128)(2,1)S(1)} %get-tuple-element.13), channel_id=1, replica_groups={{0,1,8,9,16,17,24,25,2,3,10,11,18,19,26,27,4,5,12,13,20,21,28,29,6,7,14..., dimensions={0} | all-to-all | bytes 524288 | tf_op jit(solution)/shard_map/all_to_all | solution.py:191
  19.2 0.0 copy-start
  19.2 0.2 shard_map.101
  19.4 0.0 copy-start.1
  19.5 0.0 copy-start.2
  19.5 10.2 %all_to_all.21.summed = bf16[32,16,128]{2,1,0:T(8,128)(2,1)S(1)} all-to-all(bf16[32,16,128]{2,1,0:T(8,128)(2,1)S(1)} %shard_map.101), channel_id=1, replica_groups={{0,1,30,31,22,23,14,15,6,7,28,29,20,21,12,13,4,5,26,27,18,19,10,11,2,3,..., dimensions={0} | all-to-all | bytes 262144 | tf_op jit(solution)/shard_map/all_to_all | solution.py:191
  29.6 0.0 copy-done
  29.6 0.0 copy-done.1
  29.6 0.0 copy-done.2
  29.6 0.8 %shard_map.102 = (bf16[32,32,128]{2,1,0:T(8,128)(2,1)S(1)}, f32[128,512]{1,0:T(8,128)S(1)}, bf16[128,512]{1,0:T(8,128)(2,1)S(1)}) custom-call(bf16[32,16,128]{2,1,0:T(8,128)(2,1)S(1)} %all_to_all.21.summed, bf16[128,512]{1,0:T(8,128)(2,1)S(1)} %get-tuple-element.14.old, f32[128,512]{1,0:T(8,128)S(1)} %get-tuple-element.15.old_gate, ...), custom_call_target="tpu_custom_call" | custom-call | tf_op jit(solution)/shard_map/pallas_call | solution.py:175
  30.4 11.8 %all_to_all.22.sides = bf16[32,32,128]{2,1,0:T(8,128)(2,1)S(1)} all-to-all(bf16[32,32,128]{2,1,0:T(8,128)(2,1)S(1)} %get-tuple-element.18), channel_id=1, replica_groups={{0,1,30,31,22,23,14,15,6,7,28,29,20,21,12,13,4,5,26,27,18,19,10,11,2,3,..., dimensions={0} | all-to-all | bytes 524288 | tf_op jit(solution)/shard_map/all_to_all | solution.py:191
  42.2 0.2 shard_map.103
  42.5 10.5 %all_to_all.23.summed = bf16[32,16,128]{2,1,0:T(8,128)(2,1)S(1)} all-to-all(bf16[32,16,128]{2,1,0:T(8,128)(2,1)S(1)} %shard_map.103), channel_id=1, replica_groups={{0,1,30,31,22,23,14,15,6,7,28,29,20,21,12,13,4,5,26,27,18,19,10,11,2,3,..., dimensions={0} | all-to-all | bytes 262144 | tf_op jit(solution)/shard_map/all_to_all | solution.py:191
  53.0 1.0 %shard_map.104 = bf16[4,128,128]{2,1,0:T(8,128)(2,1)} custom-call(bf16[32,16,128]{2,1,0:T(8,128)(2,1)S(1)} %all_to_all.23.summed, bf16[128,512]{1,0:T(8,128)(2,1)S(1)} %get-tuple-element.19.old, f32[128,512]{1,0:T(8,128)S(1)} %get-tuple-element.20.old_gate, f32[128,32]{1,0:T(8,128)S(1)} %get-tuple-element.16.columns, bf16[2,128,128]{2,1,0:T(8,128)(2,1)S(1)} %copy-done.2), custom_call_target="tpu_custom_call" | custom-call | tf_op jit(solution)/shard_map/pallas_call | solution.py:175
Async XLA Ops:
  19.2 10.4 %copy-start = (bf16[2,128,512]{2,1,0:T(8,128)(2,1)S(1)}, bf16[2,128,512]{2,1,0:T(8,128)(2,1)}, u32[]{:S(2)}) copy-start(bf16[2,128,512]{2,1,0:T(8,128)(2,1)} %pw.3) | copy-start | bytes 786436
  19.4 10.2 %copy-start.1 = (bf16[2,128,128]{2,1,0:T(8,128)(2,1)S(1)}, bf16[2,128,128]{2,1,0:T(8,128)(2,1)}, u32[]{:S(2)}) copy-start(bf16[2,128,128]{2,1,0:T(8,128)(2,1)} %gw.3) | copy-start | bytes 196612
  19.5 10.2 %copy-start.2 = (bf16[2,128,128]{2,1,0:T(8,128)(2,1)S(1)}, bf16[2,128,128]{2,1,0:T(8,128)(2,1)}, u32[]{:S(2)}) copy-start(bf16[2,128,128]{2,1,0:T(8,128)(2,1)} %ow.3) | copy-start | bytes 196612

commit v13 on v12

--- a/solution.py
+++ b/solution.py
@@ -10,7 +10,7 @@
 PEERS = ("row", "ka")
 OWN = 4
 ORDERS = (
-    ((0, 4, 8, 12, 1, 5, 9, 13, 2, 6, 10, 14, 3, 7, 11, 15), (0, 15, 11, 7, 3, 14, 10, 6, 2, 13, 9, 5, 1, 12, 8, 4)),
+    ((0, 15, 11, 7, 3, 14, 10, 6, 2, 13, 9, 5, 1, 12, 8, 4), (0, 15, 11, 7, 3, 14, 10, 6, 2, 13, 9, 5, 1, 12, 8, 4)),
     ((0, 15, 11, 7, 3, 14, 10, 6, 2, 13, 9, 5, 1, 12, 8, 4), (0, 15, 11, 7, 3, 14, 10, 6, 2, 13, 9, 5, 1, 12, 8, 4)),
 )
 EACH = 16

time: 54.2 us -> 54.1 us (level)
  no operation moved by 1% of the time
where the time goes in v13:
time: 54.1 us; the launch traced here: 53.8 us
  blocking collectives  49.8 us (92%)
  Pallas kernels  3.94 us (7%)
    all_to_all x4, blocking collectives, exchange_in_order(): lax.all_to_all(blocks, 'row', split_axis=0, concat_axis=0, axis_index_gro...  49.8 us
    pallas_call x5, Pallas kernels, call(): pl.pallas_call(kernel, out_shape=[jax.ShapeDtypeStruct(*o) for o in outs]...  3.94 us

profile of v13, /device:TPU:0, one launch (start us, length us, event | category | flops | bytes accessed | tf_op | source)
XLA Modules:
  0.0 53.8 jit_solution(14844021004822691047)
XLA Ops:
  0.0 1.7 %shard_map.100 = (bf16[32,32,128]{2,1,0:T(8,128)(2,1)S(1)}, f32[128,512]{1,0:T(8,128)S(1)}, bf16[128,512]{1,0:T(8,128)(2,1)S(1)}, f32[128,32]{1,0:T(8,128)S(1)}, f32[8,128]{1,0:T(8,128)S(1)}) custom-call(bf16[4,128,128]{2,1,0:T(8,128)(2,1)} %pair.1, s32[4,128]{1,0:T(4,128)} %mask.1, bf16[2,128,512]{2,1,0:T(8,128)(2,1)} %pw.3, bf16[2,128,128]{2,1,0:T(8,128)(2,1)} %gw.3, ...), custom_call_target="tpu_custom_call" | custom-call | tf_op jit(solution)/shard_map/pallas_call | solution.py:175
  1.7 16.9 %all_to_all.20.sides = bf16[32,32,128]{2,1,0:T(8,128)(2,1)S(1)} all-to-all(bf16[32,32,128]{2,1,0:T(8,128)(2,1)S(1)} %get-tuple-element.13), channel_id=1, replica_groups={{0,1,30,31,22,23,14,15,6,7,28,29,20,21,12,13,4,5,26,27,18,19,10,11,2,3,..., dimensions={0} | all-to-all | bytes 524288 | tf_op jit(solution)/shard_map/all_to_all | solution.py:191
  18.7 0.0 copy-start
  18.7 0.2 shard_map.101
  18.9 0.0 copy-start.1
  18.9 0.0 copy-start.2
  18.9 10.5 %all_to_all.21.summed = bf16[32,16,128]{2,1,0:T(8,128)(2,1)S(1)} all-to-all(bf16[32,16,128]{2,1,0:T(8,128)(2,1)S(1)} %shard_map.101), channel_id=1, replica_groups={{0,1,30,31,22,23,14,15,6,7,28,29,20,21,12,13,4,5,26,27,18,19,10,11,2,3,..., dimensions={0} | all-to-all | bytes 262144 | tf_op jit(solution)/shard_map/all_to_all | solution.py:191
  29.5 0.0 copy-done
  29.5 0.0 copy-done.1
  29.5 0.0 copy-done.2
  29.5 0.8 %shard_map.102 = (bf16[32,32,128]{2,1,0:T(8,128)(2,1)S(1)}, f32[128,512]{1,0:T(8,128)S(1)}, bf16[128,512]{1,0:T(8,128)(2,1)S(1)}) custom-call(bf16[32,16,128]{2,1,0:T(8,128)(2,1)S(1)} %all_to_all.21.summed, bf16[128,512]{1,0:T(8,128)(2,1)S(1)} %get-tuple-element.14.old, f32[128,512]{1,0:T(8,128)S(1)} %get-tuple-element.15.old_gate, ...), custom_call_target="tpu_custom_call" | custom-call | tf_op jit(solution)/shard_map/pallas_call | solution.py:175
  30.2 11.8 %all_to_all.22.sides = bf16[32,32,128]{2,1,0:T(8,128)(2,1)S(1)} all-to-all(bf16[32,32,128]{2,1,0:T(8,128)(2,1)S(1)} %get-tuple-element.18), channel_id=1, replica_groups={{0,1,30,31,22,23,14,15,6,7,28,29,20,21,12,13,4,5,26,27,18,19,10,11,2,3,..., dimensions={0} | all-to-all | bytes 524288 | tf_op jit(solution)/shard_map/all_to_all | solution.py:191
  42.0 0.2 shard_map.103
  42.3 10.5 %all_to_all.23.summed = bf16[32,16,128]{2,1,0:T(8,128)(2,1)S(1)} all-to-all(bf16[32,16,128]{2,1,0:T(8,128)(2,1)S(1)} %shard_map.103), channel_id=1, replica_groups={{0,1,30,31,22,23,14,15,6,7,28,29,20,21,12,13,4,5,26,27,18,19,10,11,2,3,..., dimensions={0} | all-to-all | bytes 262144 | tf_op jit(solution)/shard_map/all_to_all | solution.py:191
  52.8 1.0 %shard_map.104 = bf16[4,128,128]{2,1,0:T(8,128)(2,1)} custom-call(bf16[32,16,128]{2,1,0:T(8,128)(2,1)S(1)} %all_to_all.23.summed, bf16[128,512]{1,0:T(8,128)(2,1)S(1)} %get-tuple-element.19.old, f32[128,512]{1,0:T(8,128)S(1)} %get-tuple-element.20.old_gate, f32[128,32]{1,0:T(8,128)S(1)} %get-tuple-element.16.columns, bf16[2,128,128]{2,1,0:T(8,128)(2,1)S(1)} %copy-done.2), custom_call_target="tpu_custom_call" | custom-call | tf_op jit(solution)/shard_map/pallas_call | solution.py:175
Async XLA Ops:
  18.7 10.8 %copy-start = (bf16[2,128,512]{2,1,0:T(8,128)(2,1)S(1)}, bf16[2,128,512]{2,1,0:T(8,128)(2,1)}, u32[]{:S(2)}) copy-start(bf16[2,128,512]{2,1,0:T(8,128)(2,1)} %pw.3) | copy-start | bytes 786436
  18.9 10.6 %copy-start.1 = (bf16[2,128,128]{2,1,0:T(8,128)(2,1)S(1)}, bf16[2,128,128]{2,1,0:T(8,128)(2,1)}, u32[]{:S(2)}) copy-start(bf16[2,128,128]{2,1,0:T(8,128)(2,1)} %gw.3) | copy-start | bytes 196612
  18.9 10.6 %copy-start.2 = (bf16[2,128,128]{2,1,0:T(8,128)(2,1)S(1)}, bf16[2,128,128]{2,1,0:T(8,128)(2,1)}, u32[]{:S(2)}) copy-start(bf16[2,128,128]{2,1,0:T(8,128)(2,1)} %ow.3) | copy-start | bytes 196612

commit v14 on v13

--- a/solution.py
+++ b/solution.py
@@ -11,7 +11,7 @@
 OWN = 4
 ORDERS = (
     ((0, 15, 11, 7, 3, 14, 10, 6, 2, 13, 9, 5, 1, 12, 8, 4), (0, 15, 11, 7, 3, 14, 10, 6, 2, 13, 9, 5, 1, 12, 8, 4)),
-    ((0, 15, 11, 7, 3, 14, 10, 6, 2, 13, 9, 5, 1, 12, 8, 4), (0, 15, 11, 7, 3, 14, 10, 6, 2, 13, 9, 5, 1, 12, 8, 4)),
+    ((0, 15, 11, 7, 3, 14, 10, 6, 2, 13, 9, 5, 1, 12, 8, 4), (0, 15, 11, 14, 13, 10, 9, 7, 12, 5, 8, 6, 4, 3, 2, 1)),
 )
 EACH = 16
 BF16, F32 = jnp.bfloat16, jnp.float32

time: 54.1 us -> 54 us (level)
  no operation moved by 1% of the time
where the time goes in v14:
time: 54 us; the launch traced here: 53.8 us
  blocking collectives  49.8 us (92%)
  Pallas kernels  3.95 us (7%)
    all_to_all x4, blocking collectives, exchange_in_order(): lax.all_to_all(blocks, 'row', split_axis=0, concat_axis=0, axis_index_gro...  49.8 us
    pallas_call x5, Pallas kernels, call(): pl.pallas_call(kernel, out_shape=[jax.ShapeDtypeStruct(*o) for o in outs]...  3.95 us

profile of v14, /device:TPU:0, one launch (start us, length us, event | category | flops | bytes accessed | tf_op | source)
XLA Modules:
  0.0 53.8 jit_solution(10828277415675060562)
XLA Ops:
  0.0 1.7 %shard_map.100 = (bf16[32,32,128]{2,1,0:T(8,128)(2,1)S(1)}, f32[128,512]{1,0:T(8,128)S(1)}, bf16[128,512]{1,0:T(8,128)(2,1)S(1)}, f32[128,32]{1,0:T(8,128)S(1)}, f32[8,128]{1,0:T(8,128)S(1)}) custom-call(bf16[4,128,128]{2,1,0:T(8,128)(2,1)} %pair.1, s32[4,128]{1,0:T(4,128)} %mask.1, bf16[2,128,512]{2,1,0:T(8,128)(2,1)} %pw.3, bf16[2,128,128]{2,1,0:T(8,128)(2,1)} %gw.3, ...), custom_call_target="tpu_custom_call" | custom-call | tf_op jit(solution)/shard_map/pallas_call | solution.py:175
  1.7 16.9 %all_to_all.20.sides = bf16[32,32,128]{2,1,0:T(8,128)(2,1)S(1)} all-to-all(bf16[32,32,128]{2,1,0:T(8,128)(2,1)S(1)} %get-tuple-element.13), channel_id=1, replica_groups={{0,1,30,31,22,23,14,15,6,7,28,29,20,21,12,13,4,5,26,27,18,19,10,11,2,3,..., dimensions={0} | all-to-all | bytes 524288 | tf_op jit(solution)/shard_map/all_to_all | solution.py:191
  18.7 0.0 copy-start
  18.7 0.2 shard_map.101
  18.9 0.0 copy-start.1
  18.9 0.0 copy-start.2
  18.9 10.5 %all_to_all.21.summed = bf16[32,16,128]{2,1,0:T(8,128)(2,1)S(1)} all-to-all(bf16[32,16,128]{2,1,0:T(8,128)(2,1)S(1)} %shard_map.101), channel_id=1, replica_groups={{0,1,30,31,22,23,14,15,6,7,28,29,20,21,12,13,4,5,26,27,18,19,10,11,2,3,..., dimensions={0} | all-to-all | bytes 262144 | tf_op jit(solution)/shard_map/all_to_all | solution.py:191
  29.5 0.0 copy-done
  29.5 0.0 copy-done.1
  29.5 0.0 copy-done.2
  29.5 0.8 %shard_map.102 = (bf16[32,32,128]{2,1,0:T(8,128)(2,1)S(1)}, f32[128,512]{1,0:T(8,128)S(1)}, bf16[128,512]{1,0:T(8,128)(2,1)S(1)}) custom-call(bf16[32,16,128]{2,1,0:T(8,128)(2,1)S(1)} %all_to_all.21.summed, bf16[128,512]{1,0:T(8,128)(2,1)S(1)} %get-tuple-element.14.old, f32[128,512]{1,0:T(8,128)S(1)} %get-tuple-element.15.old_gate, ...), custom_call_target="tpu_custom_call" | custom-call | tf_op jit(solution)/shard_map/pallas_call | solution.py:175
  30.2 11.8 %all_to_all.22.sides = bf16[32,32,128]{2,1,0:T(8,128)(2,1)S(1)} all-to-all(bf16[32,32,128]{2,1,0:T(8,128)(2,1)S(1)} %get-tuple-element.18), channel_id=1, replica_groups={{0,1,30,31,22,23,14,15,6,7,28,29,20,21,12,13,4,5,26,27,18,19,10,11,2,3,..., dimensions={0} | all-to-all | bytes 524288 | tf_op jit(solution)/shard_map/all_to_all | solution.py:191
  42.0 0.2 shard_map.103
  42.3 10.5 %all_to_all.23.summed = bf16[32,16,128]{2,1,0:T(8,128)(2,1)S(1)} all-to-all(bf16[32,16,128]{2,1,0:T(8,128)(2,1)S(1)} %shard_map.103), channel_id=1, replica_groups={{0,1,30,31,22,23,28,29,26,27,20,21,18,19,14,15,24,25,10,11,16,17,12,13,..., dimensions={0} | all-to-all | bytes 262144 | tf_op jit(solution)/shard_map/all_to_all | solution.py:191
  52.8 1.0 %shard_map.104 = bf16[4,128,128]{2,1,0:T(8,128)(2,1)} custom-call(bf16[32,16,128]{2,1,0:T(8,128)(2,1)S(1)} %all_to_all.23.summed, bf16[128,512]{1,0:T(8,128)(2,1)S(1)} %get-tuple-element.19.old, f32[128,512]{1,0:T(8,128)S(1)} %get-tuple-element.20.old_gate, f32[128,32]{1,0:T(8,128)S(1)} %get-tuple-element.16.columns, bf16[2,128,128]{2,1,0:T(8,128)(2,1)S(1)} %copy-done.2), custom_call_target="tpu_custom_call" | custom-call | tf_op jit(solution)/shard_map/pallas_call | solution.py:175
Async XLA Ops:
  18.7 10.8 %copy-start = (bf16[2,128,512]{2,1,0:T(8,128)(2,1)S(1)}, bf16[2,128,512]{2,1,0:T(8,128)(2,1)}, u32[]{:S(2)}) copy-start(bf16[2,128,512]{2,1,0:T(8,128)(2,1)} %pw.3) | copy-start | bytes 786436
  18.9 10.6 %copy-start.1 = (bf16[2,128,128]{2,1,0:T(8,128)(2,1)S(1)}, bf16[2,128,128]{2,1,0:T(8,128)(2,1)}, u32[]{:S(2)}) copy-start(bf16[2,128,128]{2,1,0:T(8,128)(2,1)} %gw.3) | copy-start | bytes 196612
  18.9 10.6 %copy-start.2 = (bf16[2,128,128]{2,1,0:T(8,128)(2,1)S(1)}, bf16[2,128,128]{2,1,0:T(8,128)(2,1)}, u32[]{:S(2)}) copy-start(bf16[2,128,128]{2,1,0:T(8,128)(2,1)} %ow.3) | copy-start | bytes 196612

commit v15 on v14

--- a/solution.py
+++ b/solution.py
@@ -10,8 +10,8 @@
 PEERS = ("row", "ka")
 OWN = 4
 ORDERS = (
-    ((0, 15, 11, 7, 3, 14, 10, 6, 2, 13, 9, 5, 1, 12, 8, 4), (0, 15, 11, 7, 3, 14, 10, 6, 2, 13, 9, 5, 1, 12, 8, 4)),
-    ((0, 15, 11, 7, 3, 14, 10, 6, 2, 13, 9, 5, 1, 12, 8, 4), (0, 15, 11, 14, 13, 10, 9, 7, 12, 5, 8, 6, 4, 3, 2, 1)),
+    ((0, 13, 9, 5, 1, 15, 11, 7, 3, 14, 10, 6, 2, 12, 8, 4), (0, 13, 9, 5, 1, 15, 11, 7, 3, 14, 10, 6, 2, 12, 8, 4)),
+    ((0, 13, 9, 5, 1, 15, 11, 7, 3, 14, 10, 6, 2, 12, 8, 4), (0, 15, 11, 14, 13, 10, 9, 7, 12, 5, 8, 6, 4, 3, 2, 1)),
 )
 EACH = 16
 BF16, F32 = jnp.bfloat16, jnp.float32

time: 54 us -> 54 us (level)
  no operation moved by 1% of the time
where the time goes in v15:
time: 54 us; the launch traced here: 53.8 us
  blocking collectives  49.8 us (92%)
  Pallas kernels  3.95 us (7%)
    all_to_all x4, blocking collectives, exchange_in_order(): lax.all_to_all(blocks, 'row', split_axis=0, concat_axis=0, axis_index_gro...  49.8 us
    pallas_call x5, Pallas kernels, call(): pl.pallas_call(kernel, out_shape=[jax.ShapeDtypeStruct(*o) for o in outs]...  3.95 us

profile of v15, /device:TPU:0, one launch (start us, length us, event | category | flops | bytes accessed | tf_op | source)
XLA Modules:
  0.0 53.8 jit_solution(2867831825371580280)
XLA Ops:
  0.0 1.7 %shard_map.100 = (bf16[32,32,128]{2,1,0:T(8,128)(2,1)S(1)}, f32[128,512]{1,0:T(8,128)S(1)}, bf16[128,512]{1,0:T(8,128)(2,1)S(1)}, f32[128,32]{1,0:T(8,128)S(1)}, f32[8,128]{1,0:T(8,128)S(1)}) custom-call(bf16[4,128,128]{2,1,0:T(8,128)(2,1)} %pair.1, s32[4,128]{1,0:T(4,128)} %mask.1, bf16[2,128,512]{2,1,0:T(8,128)(2,1)} %pw.3, bf16[2,128,128]{2,1,0:T(8,128)(2,1)} %gw.3, ...), custom_call_target="tpu_custom_call" | custom-call | tf_op jit(solution)/shard_map/pallas_call | solution.py:175
  1.7 17.3 %all_to_all.20.sides = bf16[32,32,128]{2,1,0:T(8,128)(2,1)S(1)} all-to-all(bf16[32,32,128]{2,1,0:T(8,128)(2,1)S(1)} %get-tuple-element.13), channel_id=1, replica_groups={{0,1,26,27,18,19,10,11,2,3,30,31,22,23,14,15,6,7,28,29,20,21,12,13,4,5,..., dimensions={0} | all-to-all | bytes 524288 | tf_op jit(solution)/shard_map/all_to_all | solution.py:191
  19.0 0.0 copy-start
  19.0 0.2 shard_map.101
  19.2 0.0 copy-start.1
  19.2 0.0 copy-start.2
  19.2 10.5 %all_to_all.21.summed = bf16[32,16,128]{2,1,0:T(8,128)(2,1)S(1)} all-to-all(bf16[32,16,128]{2,1,0:T(8,128)(2,1)S(1)} %shard_map.101), channel_id=1, replica_groups={{0,1,26,27,18,19,10,11,2,3,30,31,22,23,14,15,6,7,28,29,20,21,12,13,4,5,..., dimensions={0} | all-to-all | bytes 262144 | tf_op jit(solution)/shard_map/all_to_all | solution.py:191
  29.7 0.0 copy-done
  29.7 0.0 copy-done.1
  29.7 0.0 copy-done.2
  29.7 0.8 %shard_map.102 = (bf16[32,32,128]{2,1,0:T(8,128)(2,1)S(1)}, f32[128,512]{1,0:T(8,128)S(1)}, bf16[128,512]{1,0:T(8,128)(2,1)S(1)}) custom-call(bf16[32,16,128]{2,1,0:T(8,128)(2,1)S(1)} %all_to_all.21.summed, bf16[128,512]{1,0:T(8,128)(2,1)S(1)} %get-tuple-element.14.old, f32[128,512]{1,0:T(8,128)S(1)} %get-tuple-element.15.old_gate, ...), custom_call_target="tpu_custom_call" | custom-call | tf_op jit(solution)/shard_map/pallas_call | solution.py:175
  30.5 11.9 %all_to_all.22.sides = bf16[32,32,128]{2,1,0:T(8,128)(2,1)S(1)} all-to-all(bf16[32,32,128]{2,1,0:T(8,128)(2,1)S(1)} %get-tuple-element.18), channel_id=1, replica_groups={{0,1,26,27,18,19,10,11,2,3,30,31,22,23,14,15,6,7,28,29,20,21,12,13,4,5,..., dimensions={0} | all-to-all | bytes 524288 | tf_op jit(solution)/shard_map/all_to_all | solution.py:191
  42.4 0.2 shard_map.103
  42.6 10.2 %all_to_all.23.summed = bf16[32,16,128]{2,1,0:T(8,128)(2,1)S(1)} all-to-all(bf16[32,16,128]{2,1,0:T(8,128)(2,1)S(1)} %shard_map.103), channel_id=1, replica_groups={{0,1,30,31,22,23,28,29,26,27,20,21,18,19,14,15,24,25,10,11,16,17,12,13,..., dimensions={0} | all-to-all | bytes 262144 | tf_op jit(solution)/shard_map/all_to_all | solution.py:191
  52.8 1.0 %shard_map.104 = bf16[4,128,128]{2,1,0:T(8,128)(2,1)} custom-call(bf16[32,16,128]{2,1,0:T(8,128)(2,1)S(1)} %all_to_all.23.summed, bf16[128,512]{1,0:T(8,128)(2,1)S(1)} %get-tuple-element.19.old, f32[128,512]{1,0:T(8,128)S(1)} %get-tuple-element.20.old_gate, f32[128,32]{1,0:T(8,128)S(1)} %get-tuple-element.16.columns, bf16[2,128,128]{2,1,0:T(8,128)(2,1)S(1)} %copy-done.2), custom_call_target="tpu_custom_call" | custom-call | tf_op jit(solution)/shard_map/pallas_call | solution.py:175
Async XLA Ops:
  19.0 10.8 %copy-start = (bf16[2,128,512]{2,1,0:T(8,128)(2,1)S(1)}, bf16[2,128,512]{2,1,0:T(8,128)(2,1)}, u32[]{:S(2)}) copy-start(bf16[2,128,512]{2,1,0:T(8,128)(2,1)} %pw.3) | copy-start | bytes 786436
  19.2 10.5 %copy-start.1 = (bf16[2,128,128]{2,1,0:T(8,128)(2,1)S(1)}, bf16[2,128,128]{2,1,0:T(8,128)(2,1)}, u32[]{:S(2)}) copy-start(bf16[2,128,128]{2,1,0:T(8,128)(2,1)} %gw.3) | copy-start | bytes 196612
  19.2 10.5 %copy-start.2 = (bf16[2,128,128]{2,1,0:T(8,128)(2,1)S(1)}, bf16[2,128,128]{2,1,0:T(8,128)(2,1)}, u32[]{:S(2)}) copy-start(bf16[2,128,128]{2,1,0:T(8,128)(2,1)} %ow.3) | copy-start | bytes 196612

commit v16 on v15

--- a/solution.py
+++ b/solution.py
@@ -10,8 +10,8 @@
 PEERS = ("row", "ka")
 OWN = 4
 ORDERS = (
-    ((0, 13, 9, 5, 1, 15, 11, 7, 3, 14, 10, 6, 2, 12, 8, 4), (0, 13, 9, 5, 1, 15, 11, 7, 3, 14, 10, 6, 2, 12, 8, 4)),
-    ((0, 13, 9, 5, 1, 15, 11, 7, 3, 14, 10, 6, 2, 12, 8, 4), (0, 15, 11, 14, 13, 10, 9, 7, 12, 5, 8, 6, 4, 3, 2, 1)),
+    ((0, 15, 14, 11, 10, 7, 6, 3, 2, 13, 12, 9, 8, 5, 4, 1), (0, 15, 14, 11, 10, 7, 6, 3, 2, 13, 12, 9, 8, 5, 4, 1)),
+    ((0, 15, 14, 11, 10, 7, 6, 3, 2, 13, 12, 9, 8, 5, 4, 1), (0, 15, 11, 14, 13, 10, 9, 7, 12, 5, 8, 6, 4, 3, 2, 1)),
 )
 EACH = 16
 BF16, F32 = jnp.bfloat16, jnp.float32

time: 54 us -> 54.8 us (1.015)
  blocking collectives: 49.8 us -> 50.6 us
    all_to_all x4, blocking collectives: 49.8 us -> 50.6 us  [exchange_in_order(): lax.all_to_all(blocks, 'row', split_axis=0, concat_axis=0, axis_index_gro...]
where the time goes in v16:
time: 54.8 us; the launch traced here: 54.6 us
  blocking collectives  50.6 us (92%)
  Pallas kernels  3.94 us (7%)
    all_to_all x4, blocking collectives, exchange_in_order(): lax.all_to_all(blocks, 'row', split_axis=0, concat_axis=0, axis_index_gro...  50.6 us
    pallas_call x5, Pallas kernels, call(): pl.pallas_call(kernel, out_shape=[jax.ShapeDtypeStruct(*o) for o in outs]...  3.94 us

profile of v16, /device:TPU:0, one launch (start us, length us, event | category | flops | bytes accessed | tf_op | source)
XLA Modules:
  0.0 54.6 jit_solution(1376180947250124920)
XLA Ops:
  0.0 1.7 %shard_map.100 = (bf16[32,32,128]{2,1,0:T(8,128)(2,1)S(1)}, f32[128,512]{1,0:T(8,128)S(1)}, bf16[128,512]{1,0:T(8,128)(2,1)S(1)}, f32[128,32]{1,0:T(8,128)S(1)}, f32[8,128]{1,0:T(8,128)S(1)}) custom-call(bf16[4,128,128]{2,1,0:T(8,128)(2,1)} %pair.1, s32[4,128]{1,0:T(4,128)} %mask.1, bf16[2,128,512]{2,1,0:T(8,128)(2,1)} %pw.3, bf16[2,128,128]{2,1,0:T(8,128)(2,1)} %gw.3, ...), custom_call_target="tpu_custom_call" | custom-call | tf_op jit(solution)/shard_map/pallas_call | solution.py:175
  1.7 18.1 %all_to_all.20.sides = bf16[32,32,128]{2,1,0:T(8,128)(2,1)S(1)} all-to-all(bf16[32,32,128]{2,1,0:T(8,128)(2,1)S(1)} %get-tuple-element.13), channel_id=1, replica_groups={{0,1,30,31,28,29,22,23,20,21,14,15,12,13,6,7,4,5,26,27,24,25,18,19,16,1..., dimensions={0} | all-to-all | bytes 524288 | tf_op jit(solution)/shard_map/all_to_all | solution.py:191
  19.9 0.0 copy-start
  19.9 0.2 shard_map.101
  20.1 0.0 copy-start.1
  20.1 0.0 copy-start.2
  20.1 9.7 %all_to_all.21.summed = bf16[32,16,128]{2,1,0:T(8,128)(2,1)S(1)} all-to-all(bf16[32,16,128]{2,1,0:T(8,128)(2,1)S(1)} %shard_map.101), channel_id=1, replica_groups={{0,1,30,31,28,29,22,23,20,21,14,15,12,13,6,7,4,5,26,27,24,25,18,19,16,1..., dimensions={0} | all-to-all | bytes 262144 | tf_op jit(solution)/shard_map/all_to_all | solution.py:191
  29.9 0.0 copy-done
  29.9 0.0 copy-done.1
  29.9 0.0 copy-done.2
  29.9 0.8 %shard_map.102 = (bf16[32,32,128]{2,1,0:T(8,128)(2,1)S(1)}, f32[128,512]{1,0:T(8,128)S(1)}, bf16[128,512]{1,0:T(8,128)(2,1)S(1)}) custom-call(bf16[32,16,128]{2,1,0:T(8,128)(2,1)S(1)} %all_to_all.21.summed, bf16[128,512]{1,0:T(8,128)(2,1)S(1)} %get-tuple-element.14.old, f32[128,512]{1,0:T(8,128)S(1)} %get-tuple-element.15.old_gate, ...), custom_call_target="tpu_custom_call" | custom-call | tf_op jit(solution)/shard_map/pallas_call | solution.py:175
  30.6 13.1 %all_to_all.22.sides = bf16[32,32,128]{2,1,0:T(8,128)(2,1)S(1)} all-to-all(bf16[32,32,128]{2,1,0:T(8,128)(2,1)S(1)} %get-tuple-element.18), channel_id=1, replica_groups={{0,1,30,31,28,29,22,23,20,21,14,15,12,13,6,7,4,5,26,27,24,25,18,19,16,1..., dimensions={0} | all-to-all | bytes 524288 | tf_op jit(solution)/shard_map/all_to_all | solution.py:191
  43.7 0.2 shard_map.103
  44.0 9.6 %all_to_all.23.summed = bf16[32,16,128]{2,1,0:T(8,128)(2,1)S(1)} all-to-all(bf16[32,16,128]{2,1,0:T(8,128)(2,1)S(1)} %shard_map.103), channel_id=1, replica_groups={{0,1,30,31,22,23,28,29,26,27,20,21,18,19,14,15,24,25,10,11,16,17,12,13,..., dimensions={0} | all-to-all | bytes 262144 | tf_op jit(solution)/shard_map/all_to_all | solution.py:191
  53.6 1.0 %shard_map.104 = bf16[4,128,128]{2,1,0:T(8,128)(2,1)} custom-call(bf16[32,16,128]{2,1,0:T(8,128)(2,1)S(1)} %all_to_all.23.summed, bf16[128,512]{1,0:T(8,128)(2,1)S(1)} %get-tuple-element.19.old, f32[128,512]{1,0:T(8,128)S(1)} %get-tuple-element.20.old_gate, f32[128,32]{1,0:T(8,128)S(1)} %get-tuple-element.16.columns, bf16[2,128,128]{2,1,0:T(8,128)(2,1)S(1)} %copy-done.2), custom_call_target="tpu_custom_call" | custom-call | tf_op jit(solution)/shard_map/pallas_call | solution.py:175
Async XLA Ops:
  19.9 10.0 %copy-start = (bf16[2,128,512]{2,1,0:T(8,128)(2,1)S(1)}, bf16[2,128,512]{2,1,0:T(8,128)(2,1)}, u32[]{:S(2)}) copy-start(bf16[2,128,512]{2,1,0:T(8,128)(2,1)} %pw.3) | copy-start | bytes 786436
  20.1 9.8 %copy-start.1 = (bf16[2,128,128]{2,1,0:T(8,128)(2,1)S(1)}, bf16[2,128,128]{2,1,0:T(8,128)(2,1)}, u32[]{:S(2)}) copy-start(bf16[2,128,128]{2,1,0:T(8,128)(2,1)} %gw.3) | copy-start | bytes 196612
  20.1 9.8 %copy-start.2 = (bf16[2,128,128]{2,1,0:T(8,128)(2,1)S(1)}, bf16[2,128,128]{2,1,0:T(8,128)(2,1)}, u32[]{:S(2)}) copy-start(bf16[2,128,128]{2,1,0:T(8,128)(2,1)} %ow.3) | copy-start | bytes 196612

commit v17 on v16

--- a/solution.py
+++ b/solution.py
@@ -10,8 +10,8 @@
 PEERS = ("row", "ka")
 OWN = 4
 ORDERS = (
-    ((0, 15, 14, 11, 10, 7, 6, 3, 2, 13, 12, 9, 8, 5, 4, 1), (0, 15, 14, 11, 10, 7, 6, 3, 2, 13, 12, 9, 8, 5, 4, 1)),
-    ((0, 15, 14, 11, 10, 7, 6, 3, 2, 13, 12, 9, 8, 5, 4, 1), (0, 15, 11, 14, 13, 10, 9, 7, 12, 5, 8, 6, 4, 3, 2, 1)),
+    ((15, 11, 7, 3, 14, 10, 6, 2, 13, 9, 5, 1, 12, 8, 4, 0), (15, 11, 7, 3, 14, 10, 6, 2, 13, 9, 5, 1, 12, 8, 4, 0)),
+    ((15, 11, 7, 3, 14, 10, 6, 2, 13, 9, 5, 1, 12, 8, 4, 0), (15, 11, 7, 3, 14, 10, 6, 2, 13, 9, 5, 1, 12, 8, 4, 0)),
 )
 EACH = 16
 BF16, F32 = jnp.bfloat16, jnp.float32
@@ -33,27 +33,28 @@
 
 
 def pack(blocks):
-    channels, width = blocks[0].shape
-    tiles = [b.reshape(channels // 8, 8, width) for b in blocks]
-    turned = [pltpu.roll(b, 4, axis=0).reshape(channels // 8, 8, width) for b in blocks]
+    rows, width = blocks[0].shape
+    tiles = [b.reshape(rows // 8, 8, width) for b in blocks]
+    turned = [pltpu.roll(b, 4, axis=0).reshape(rows // 8, 8, width) for b in blocks]
     low = lax.broadcasted_iota(jnp.int32, tiles[0].shape, 1) < 4
-    back = [pltpu.roll(b, channels - 4, axis=0).reshape(channels // 8, 8, width) for b in blocks]
-    even = [jnp.where(low, tiles[n], turned[n + 1]) for n in (0, 2)]
-    odd = [jnp.where(low, back[n], tiles[n + 1]) for n in (0, 2)]
-    return jnp.stack([jnp.stack(even, 1), jnp.stack(odd, 1)], 1).reshape(channels // 4, 16, width)
+    back = [pltpu.roll(b, rows - 4, axis=0).reshape(rows // 8, 8, width) for b in blocks]
+    first = [jnp.where(low, tiles[n], turned[n + 1]) for n in (0, 2)]
+    second = [jnp.where(low, back[n], tiles[n + 1]) for n in (0, 2)]
+    grouped = (rows // 32, 4, 2, 8, width)
+    return jnp.stack([jnp.stack(v, 1).reshape(grouped) for v in (first, second)], 1).reshape(rows // 4, 16, width)
 
 
 def unpack(packed):
     count, _, width = packed.shape
-    tiles = packed.reshape(count // 2, 2, 2, 8, width)
+    tiles = packed.reshape(count // 8, 2, 4, 2, 8, width)
     low = lax.broadcasted_iota(jnp.int32, (count // 2, 8, width), 1) < 4
     blocks = []
     for n in range(2):
-        even, odd = tiles[:, 0, n], tiles[:, 1, n]
-        down = pltpu.roll(odd.reshape(count * 4, width), 4, axis=0).reshape(even.shape)
-        up = pltpu.roll(even.reshape(count * 4, width), count * 4 - 4, axis=0).reshape(even.shape)
-        blocks.append(jnp.where(low, even, down).reshape(count * 4, width))
-        blocks.append(jnp.where(low, up, odd).reshape(count * 4, width))
+        first, second = [tiles[:, core, :, n].reshape(count // 2, 8, width) for core in range(2)]
+        down = pltpu.roll(second.reshape(count * 4, width), 4, axis=0).reshape(first.shape)
+        up = pltpu.roll(first.reshape(count * 4, width), count * 4 - 4, axis=0).reshape(first.shape)
+        blocks.append(jnp.where(low, first, down).reshape(count * 4, width))
+        blocks.append(jnp.where(low, up, second).reshape(count * 4, width))
     return blocks
 
 
@@ -187,7 +188,7 @@
 
 
 def exchange_in_order(blocks, chips):
-    listed = [[2 * chip + core for chip in chips for core in range(2)]]
+    listed = [[2 * chip + core for n in range(0, len(chips), 4) for core in range(2) for chip in chips[n : n + 4]]]
     return lax.all_to_all(blocks, "row", split_axis=0, concat_axis=0, axis_index_groups=listed, tiled=True)
 
 

time: 54.8 us -> 54.7 us (level)
  no operation moved by 1% of the time
where the time goes in v17:
time: 54.7 us; the launch traced here: 54.3 us
  blocking collectives  50.3 us (92%)
  Pallas kernels  3.94 us (7%)
    all_to_all x4, blocking collectives, exchange_in_order(): lax.all_to_all(blocks, 'row', split_axis=0, concat_axis=0, axis_index_gro...  50.3 us
    pallas_call x5, Pallas kernels, call(): pl.pallas_call(kernel, out_shape=[jax.ShapeDtypeStruct(*o) for o in outs]...  3.94 us

profile of v17, /device:TPU:0, one launch (start us, length us, event | category | flops | bytes accessed | tf_op | source)
XLA Modules:
  0.0 54.3 jit_solution(7824544418080697453)
XLA Ops:
  0.0 1.7 %shard_map.100 = (bf16[32,32,128]{2,1,0:T(8,128)(2,1)S(1)}, f32[128,512]{1,0:T(8,128)S(1)}, bf16[128,512]{1,0:T(8,128)(2,1)S(1)}, f32[128,32]{1,0:T(8,128)S(1)}, f32[8,128]{1,0:T(8,128)S(1)}) custom-call(bf16[4,128,128]{2,1,0:T(8,128)(2,1)} %pair.1, s32[4,128]{1,0:T(4,128)} %mask.1, bf16[2,128,512]{2,1,0:T(8,128)(2,1)} %pw.3, bf16[2,128,128]{2,1,0:T(8,128)(2,1)} %gw.3, ...), custom_call_target="tpu_custom_call" | custom-call | tf_op jit(solution)/shard_map/pallas_call | solution.py:176
  1.7 18.2 %all_to_all.20.sides = bf16[32,32,128]{2,1,0:T(8,128)(2,1)S(1)} all-to-all(bf16[32,32,128]{2,1,0:T(8,128)(2,1)S(1)} %get-tuple-element.13), channel_id=1, replica_groups={{30,22,14,6,31,23,15,7,28,20,12,4,29,21,13,5,26,18,10,2,27,19,11,3,24,1..., dimensions={0} | all-to-all | bytes 524288 | tf_op jit(solution)/shard_map/all_to_all | solution.py:192
  20.0 0.0 copy-start
  20.0 0.2 shard_map.101
  20.2 0.0 copy-start.1
  20.2 0.0 copy-start.2
  20.2 9.6 %all_to_all.21.summed = bf16[32,16,128]{2,1,0:T(8,128)(2,1)S(1)} all-to-all(bf16[32,16,128]{2,1,0:T(8,128)(2,1)S(1)} %shard_map.101), channel_id=1, replica_groups={{30,22,14,6,31,23,15,7,28,20,12,4,29,21,13,5,26,18,10,2,27,19,11,3,24,1..., dimensions={0} | all-to-all | bytes 262144 | tf_op jit(solution)/shard_map/all_to_all | solution.py:192
  29.8 0.0 copy-done
  29.8 0.0 copy-done.1
  29.8 0.0 copy-done.2
  29.8 0.8 %shard_map.102 = (bf16[32,32,128]{2,1,0:T(8,128)(2,1)S(1)}, f32[128,512]{1,0:T(8,128)S(1)}, bf16[128,512]{1,0:T(8,128)(2,1)S(1)}) custom-call(bf16[32,16,128]{2,1,0:T(8,128)(2,1)S(1)} %all_to_all.21.summed, bf16[128,512]{1,0:T(8,128)(2,1)S(1)} %get-tuple-element.14.old, f32[128,512]{1,0:T(8,128)S(1)} %get-tuple-element.15.old_gate, ...), custom_call_target="tpu_custom_call" | custom-call | tf_op jit(solution)/shard_map/pallas_call | solution.py:176
  30.6 13.1 %all_to_all.22.sides = bf16[32,32,128]{2,1,0:T(8,128)(2,1)S(1)} all-to-all(bf16[32,32,128]{2,1,0:T(8,128)(2,1)S(1)} %get-tuple-element.18), channel_id=1, replica_groups={{30,22,14,6,31,23,15,7,28,20,12,4,29,21,13,5,26,18,10,2,27,19,11,3,24,1..., dimensions={0} | all-to-all | bytes 524288 | tf_op jit(solution)/shard_map/all_to_all | solution.py:192
  43.6 0.2 shard_map.103
  43.9 9.4 %all_to_all.23.summed = bf16[32,16,128]{2,1,0:T(8,128)(2,1)S(1)} all-to-all(bf16[32,16,128]{2,1,0:T(8,128)(2,1)S(1)} %shard_map.103), channel_id=1, replica_groups={{30,22,14,6,31,23,15,7,28,20,12,4,29,21,13,5,26,18,10,2,27,19,11,3,24,1..., dimensions={0} | all-to-all | bytes 262144 | tf_op jit(solution)/shard_map/all_to_all | solution.py:192
  53.3 1.0 %shard_map.104 = bf16[4,128,128]{2,1,0:T(8,128)(2,1)} custom-call(bf16[32,16,128]{2,1,0:T(8,128)(2,1)S(1)} %all_to_all.23.summed, bf16[128,512]{1,0:T(8,128)(2,1)S(1)} %get-tuple-element.19.old, f32[128,512]{1,0:T(8,128)S(1)} %get-tuple-element.20.old_gate, f32[128,32]{1,0:T(8,128)S(1)} %get-tuple-element.16.columns, bf16[2,128,128]{2,1,0:T(8,128)(2,1)S(1)} %copy-done.2), custom_call_target="tpu_custom_call" | custom-call | tf_op jit(solution)/shard_map/pallas_call | solution.py:176
Async XLA Ops:
  20.0 9.8 %copy-start = (bf16[2,128,512]{2,1,0:T(8,128)(2,1)S(1)}, bf16[2,128,512]{2,1,0:T(8,128)(2,1)}, u32[]{:S(2)}) copy-start(bf16[2,128,512]{2,1,0:T(8,128)(2,1)} %pw.3) | copy-start | bytes 786436
  20.2 9.6 %copy-start.1 = (bf16[2,128,128]{2,1,0:T(8,128)(2,1)S(1)}, bf16[2,128,128]{2,1,0:T(8,128)(2,1)}, u32[]{:S(2)}) copy-start(bf16[2,128,128]{2,1,0:T(8,128)(2,1)} %gw.3) | copy-start | bytes 196612
  20.2 9.6 %copy-start.2 = (bf16[2,128,128]{2,1,0:T(8,128)(2,1)S(1)}, bf16[2,128,128]{2,1,0:T(8,128)(2,1)}, u32[]{:S(2)}) copy-start(bf16[2,128,128]{2,1,0:T(8,128)(2,1)} %ow.3) | copy-start | bytes 196612

commit v18 on v15

--- a/solution.py
+++ b/solution.py
@@ -13,6 +13,8 @@
     ((0, 13, 9, 5, 1, 15, 11, 7, 3, 14, 10, 6, 2, 12, 8, 4), (0, 13, 9, 5, 1, 15, 11, 7, 3, 14, 10, 6, 2, 12, 8, 4)),
     ((0, 13, 9, 5, 1, 15, 11, 7, 3, 14, 10, 6, 2, 12, 8, 4), (0, 15, 11, 14, 13, 10, 9, 7, 12, 5, 8, 6, 4, 3, 2, 1)),
 )
+COLUMNS = ((15, 11, 7, 3), (14, 10, 6, 2), (13, 9, 5, 1), (12, 8, 4, 0))
+LAST = tuple(2 * chip + core for column in COLUMNS for core in range(2) for chip in column)
 EACH = 16
 BF16, F32 = jnp.bfloat16, jnp.float32
 
@@ -96,7 +98,10 @@
     width = z[0].shape[1]
     gain, offset, bias = broadcast_columns(columns, u * EACH + 7, 3, width)
     turned = out_weight.T
-    mixed[...] = summed[...].astype(F32).reshape(mixed.shape)
+    sums = summed[...].astype(F32)
+    if u == 1:
+        sums = rearrange(sums, LAST, devices(ORDERS[u][1]))
+    mixed[...] = sums.reshape(mixed.shape)
     results = []
     for pair in range(0, OWN, 2):
         blocks = [mixed[pl.ds(i, mixed.shape[0] // OWN, stride=OWN), :] for i in (pair, pair + 1)]
@@ -156,6 +161,14 @@
     return jnp.concatenate([tiles[n : n + 1] for n in places]).reshape(values.shape)
 
 
+def devices(chips):
+    return tuple(2 * chip + core for chip in chips for core in range(2))
+
+
+def rearrange(blocks, have, want):
+    return jnp.concatenate([blocks[n : n + 1] for n in [have.index(device) for device in want]])
+
+
 def triangle_kernel(incoming, sides, out):
     come, go = ORDERS[1 if incoming else 0]
     in_mesh = tuple(range(len(come)))
@@ -167,7 +180,8 @@
         left = [reorder(v, come, go) for v in left]
         right = [reorder(v, come, in_mesh) for v in right]
         summed = [over_columns(a.astype(BF16), b.astype(BF16)) for a, b in zip(left, right)]
-    out[...] = pack(summed).astype(BF16)
+    packed = pack(summed).astype(BF16)
+    out[...] = rearrange(packed, devices(go), LAST) if incoming else packed
 
 
 def call(kernel, outs, scratch, *args, place=pltpu.VMEM):
@@ -186,9 +200,8 @@
     return lax.all_to_all(blocks, PEERS, split_axis=0, concat_axis=0, tiled=True)
 
 
-def exchange_in_order(blocks, chips):
-    listed = [[2 * chip + core for chip in chips for core in range(2)]]
-    return lax.all_to_all(blocks, "row", split_axis=0, concat_axis=0, axis_index_groups=listed, tiled=True)
+def exchange_in_order(blocks, listed):
+    return lax.all_to_all(blocks, "row", split_axis=0, concat_axis=0, axis_index_groups=[list(listed)], tiled=True)
 
 
 def packed_updates(count, pair_rep, pair_mask, pw, pb, gw, gb, ow, ob, ns, no):
@@ -204,10 +217,10 @@
     mixed = pltpu.VMEM((2, OWN * channels, width), F32)
     kept = [((channels, 2 * EACH), F32), ((2 * OWN, width), F32)]
     send, gate, turned, columns, keep = call(first_kernel, projected + kept, held + [mixed], *params, place=pltpu.HBM)
-    (send,) = call(functools.partial(triangle_kernel, False), summed, [], exchange_in_order(send, ORDERS[0][0]))
-    send, gate, turned = call(middle_kernel, projected, [mixed, back], exchange_in_order(send, ORDERS[0][1]), turned, gate, columns, keep, pw, gw, ow)
-    (send,) = call(functools.partial(triangle_kernel, True), summed, [], exchange_in_order(send, ORDERS[1][0]))
-    (out,) = call(last_kernel, [(pair_rep.shape, BF16)], [back], exchange_in_order(send, ORDERS[1][1]), turned, gate, columns, ow)
+    (send,) = call(functools.partial(triangle_kernel, False), summed, [], exchange_in_order(send, devices(ORDERS[0][0])))
+    send, gate, turned = call(middle_kernel, projected, [mixed, back], exchange_in_order(send, devices(ORDERS[0][1])), turned, gate, columns, keep, pw, gw, ow)
+    (send,) = call(functools.partial(triangle_kernel, True), summed, [], exchange_in_order(send, devices(ORDERS[1][0])))
+    (out,) = call(last_kernel, [(pair_rep.shape, BF16)], [back], exchange_in_order(send, LAST), turned, gate, columns, ow)
     return out
 
 

time: 54 us -> 54.1 us (level)
  no operation moved by 1% of the time
where the time goes in v18:
time: 54.1 us; the launch traced here: 53.7 us
  blocking collectives  49.7 us (92%)
  Pallas kernels  3.95 us (7%)
    all_to_all x4, blocking collectives, exchange_in_order(): lax.all_to_all(blocks, 'row', split_axis=0, concat_axis=0, axis_index_gro...  49.7 us
    pallas_call x5, Pallas kernels, call(): pl.pallas_call(kernel, out_shape=[jax.ShapeDtypeStruct(*o) for o in outs]...  3.95 us

profile of v18, /device:TPU:0, one launch (start us, length us, event | category | flops | bytes accessed | tf_op | source)
XLA Modules:
  0.0 53.7 jit_solution(7635124909962279175)
XLA Ops:
  0.0 1.7 %shard_map.100 = (bf16[32,32,128]{2,1,0:T(8,128)(2,1)S(1)}, f32[128,512]{1,0:T(8,128)S(1)}, bf16[128,512]{1,0:T(8,128)(2,1)S(1)}, f32[128,32]{1,0:T(8,128)S(1)}, f32[8,128]{1,0:T(8,128)S(1)}) custom-call(bf16[4,128,128]{2,1,0:T(8,128)(2,1)} %pair.1, s32[4,128]{1,0:T(4,128)} %mask.1, bf16[2,128,512]{2,1,0:T(8,128)(2,1)} %pw.3, bf16[2,128,128]{2,1,0:T(8,128)(2,1)} %gw.3, ...), custom_call_target="tpu_custom_call" | custom-call | tf_op jit(solution)/shard_map/pallas_call | solution.py:189
  1.7 17.3 %all_to_all.20.sides = bf16[32,32,128]{2,1,0:T(8,128)(2,1)S(1)} all-to-all(bf16[32,32,128]{2,1,0:T(8,128)(2,1)S(1)} %get-tuple-element.13), channel_id=1, replica_groups={{0,1,26,27,18,19,10,11,2,3,30,31,22,23,14,15,6,7,28,29,20,21,12,13,4,5,..., dimensions={0} | all-to-all | bytes 524288 | tf_op jit(solution)/shard_map/all_to_all | solution.py:204
  19.0 0.0 copy-start
  19.0 0.2 shard_map.101
  19.2 0.0 copy-start.1
  19.2 0.0 copy-start.2
  19.2 10.5 %all_to_all.21.summed = bf16[32,16,128]{2,1,0:T(8,128)(2,1)S(1)} all-to-all(bf16[32,16,128]{2,1,0:T(8,128)(2,1)S(1)} %shard_map.101), channel_id=1, replica_groups={{0,1,26,27,18,19,10,11,2,3,30,31,22,23,14,15,6,7,28,29,20,21,12,13,4,5,..., dimensions={0} | all-to-all | bytes 262144 | tf_op jit(solution)/shard_map/all_to_all | solution.py:204
  29.7 0.0 copy-done
  29.7 0.0 copy-done.1
  29.7 0.0 copy-done.2
  29.7 0.8 %shard_map.102 = (bf16[32,32,128]{2,1,0:T(8,128)(2,1)S(1)}, f32[128,512]{1,0:T(8,128)S(1)}, bf16[128,512]{1,0:T(8,128)(2,1)S(1)}) custom-call(bf16[32,16,128]{2,1,0:T(8,128)(2,1)S(1)} %all_to_all.21.summed, bf16[128,512]{1,0:T(8,128)(2,1)S(1)} %get-tuple-element.14.old, f32[128,512]{1,0:T(8,128)S(1)} %get-tuple-element.15.old_gate, ...), custom_call_target="tpu_custom_call" | custom-call | tf_op jit(solution)/shard_map/pallas_call | solution.py:189
  30.5 11.9 %all_to_all.22.sides = bf16[32,32,128]{2,1,0:T(8,128)(2,1)S(1)} all-to-all(bf16[32,32,128]{2,1,0:T(8,128)(2,1)S(1)} %get-tuple-element.18), channel_id=1, replica_groups={{0,1,26,27,18,19,10,11,2,3,30,31,22,23,14,15,6,7,28,29,20,21,12,13,4,5,..., dimensions={0} | all-to-all | bytes 524288 | tf_op jit(solution)/shard_map/all_to_all | solution.py:204
  42.4 0.2 shard_map.103
  42.6 10.1 %all_to_all.23.summed = bf16[32,16,128]{2,1,0:T(8,128)(2,1)S(1)} all-to-all(bf16[32,16,128]{2,1,0:T(8,128)(2,1)S(1)} %shard_map.103), channel_id=1, replica_groups={{30,22,14,6,31,23,15,7,28,20,12,4,29,21,13,5,26,18,10,2,27,19,11,3,24,1..., dimensions={0} | all-to-all | bytes 262144 | tf_op jit(solution)/shard_map/all_to_all | solution.py:204
  52.7 1.0 %shard_map.104 = bf16[4,128,128]{2,1,0:T(8,128)(2,1)} custom-call(bf16[32,16,128]{2,1,0:T(8,128)(2,1)S(1)} %all_to_all.23.summed, bf16[128,512]{1,0:T(8,128)(2,1)S(1)} %get-tuple-element.19.old, f32[128,512]{1,0:T(8,128)S(1)} %get-tuple-element.20.old_gate, f32[128,32]{1,0:T(8,128)S(1)} %get-tuple-element.16.columns, bf16[2,128,128]{2,1,0:T(8,128)(2,1)S(1)} %copy-done.2), custom_call_target="tpu_custom_call" | custom-call | tf_op jit(solution)/shard_map/pallas_call | solution.py:189
Async XLA Ops:
  19.0 10.8 %copy-start = (bf16[2,128,512]{2,1,0:T(8,128)(2,1)S(1)}, bf16[2,128,512]{2,1,0:T(8,128)(2,1)}, u32[]{:S(2)}) copy-start(bf16[2,128,512]{2,1,0:T(8,128)(2,1)} %pw.3) | copy-start | bytes 786436
  19.2 10.5 %copy-start.1 = (bf16[2,128,128]{2,1,0:T(8,128)(2,1)S(1)}, bf16[2,128,128]{2,1,0:T(8,128)(2,1)}, u32[]{:S(2)}) copy-start(bf16[2,128,128]{2,1,0:T(8,128)(2,1)} %gw.3) | copy-start | bytes 196612
  19.2 10.5 %copy-start.2 = (bf16[2,128,128]{2,1,0:T(8,128)(2,1)S(1)}, bf16[2,128,128]{2,1,0:T(8,128)(2,1)}, u32[]{:S(2)}) copy-start(bf16[2,128,128]{2,1,0:T(8,128)(2,1)} %ow.3) | copy-start | bytes 196612

commit v19 on v15

--- a/solution.py
+++ b/solution.py
@@ -10,7 +10,7 @@
 PEERS = ("row", "ka")
 OWN = 4
 ORDERS = (
-    ((0, 13, 9, 5, 1, 15, 11, 7, 3, 14, 10, 6, 2, 12, 8, 4), (0, 13, 9, 5, 1, 15, 11, 7, 3, 14, 10, 6, 2, 12, 8, 4)),
+    ((0, 15, 11, 7, 3, 14, 10, 6, 2, 13, 9, 5, 1, 12, 8, 4), (0, 15, 11, 7, 3, 14, 10, 6, 2, 13, 9, 5, 1, 12, 8, 4)),
     ((0, 13, 9, 5, 1, 15, 11, 7, 3, 14, 10, 6, 2, 12, 8, 4), (0, 15, 11, 14, 13, 10, 9, 7, 12, 5, 8, 6, 4, 3, 2, 1)),
 )
 EACH = 16

time: 54 us -> 54 us (level)
  no operation moved by 1% of the time
where the time goes in v19:
time: 54 us; the launch traced here: 53.8 us
  blocking collectives  49.8 us (92%)
  Pallas kernels  3.95 us (7%)
    all_to_all x4, blocking collectives, exchange_in_order(): lax.all_to_all(blocks, 'row', split_axis=0, concat_axis=0, axis_index_gro...  49.8 us
    pallas_call x5, Pallas kernels, call(): pl.pallas_call(kernel, out_shape=[jax.ShapeDtypeStruct(*o) for o in outs]...  3.95 us

profile of v19, /device:TPU:0, one launch (start us, length us, event | category | flops | bytes accessed | tf_op | source)
XLA Modules:
  0.0 53.8 jit_solution(17436108810821775029)
XLA Ops:
  0.0 1.7 %shard_map.100 = (bf16[32,32,128]{2,1,0:T(8,128)(2,1)S(1)}, f32[128,512]{1,0:T(8,128)S(1)}, bf16[128,512]{1,0:T(8,128)(2,1)S(1)}, f32[128,32]{1,0:T(8,128)S(1)}, f32[8,128]{1,0:T(8,128)S(1)}) custom-call(bf16[4,128,128]{2,1,0:T(8,128)(2,1)} %pair.1, s32[4,128]{1,0:T(4,128)} %mask.1, bf16[2,128,512]{2,1,0:T(8,128)(2,1)} %pw.3, bf16[2,128,128]{2,1,0:T(8,128)(2,1)} %gw.3, ...), custom_call_target="tpu_custom_call" | custom-call | tf_op jit(solution)/shard_map/pallas_call | solution.py:175
  1.7 16.9 %all_to_all.20.sides = bf16[32,32,128]{2,1,0:T(8,128)(2,1)S(1)} all-to-all(bf16[32,32,128]{2,1,0:T(8,128)(2,1)S(1)} %get-tuple-element.13), channel_id=1, replica_groups={{0,1,30,31,22,23,14,15,6,7,28,29,20,21,12,13,4,5,26,27,18,19,10,11,2,3,..., dimensions={0} | all-to-all | bytes 524288 | tf_op jit(solution)/shard_map/all_to_all | solution.py:191
  18.7 0.0 copy-start
  18.7 0.2 shard_map.101
  18.9 0.0 copy-start.1
  18.9 0.0 copy-start.2
  18.9 10.5 %all_to_all.21.summed = bf16[32,16,128]{2,1,0:T(8,128)(2,1)S(1)} all-to-all(bf16[32,16,128]{2,1,0:T(8,128)(2,1)S(1)} %shard_map.101), channel_id=1, replica_groups={{0,1,30,31,22,23,14,15,6,7,28,29,20,21,12,13,4,5,26,27,18,19,10,11,2,3,..., dimensions={0} | all-to-all | bytes 262144 | tf_op jit(solution)/shard_map/all_to_all | solution.py:191
  29.5 0.0 copy-done
  29.5 0.0 copy-done.1
  29.5 0.0 copy-done.2
  29.5 0.8 %shard_map.102 = (bf16[32,32,128]{2,1,0:T(8,128)(2,1)S(1)}, f32[128,512]{1,0:T(8,128)S(1)}, bf16[128,512]{1,0:T(8,128)(2,1)S(1)}) custom-call(bf16[32,16,128]{2,1,0:T(8,128)(2,1)S(1)} %all_to_all.21.summed, bf16[128,512]{1,0:T(8,128)(2,1)S(1)} %get-tuple-element.14.old, f32[128,512]{1,0:T(8,128)S(1)} %get-tuple-element.15.old_gate, ...), custom_call_target="tpu_custom_call" | custom-call | tf_op jit(solution)/shard_map/pallas_call | solution.py:175
  30.2 12.1 %all_to_all.22.sides = bf16[32,32,128]{2,1,0:T(8,128)(2,1)S(1)} all-to-all(bf16[32,32,128]{2,1,0:T(8,128)(2,1)S(1)} %get-tuple-element.18), channel_id=1, replica_groups={{0,1,26,27,18,19,10,11,2,3,30,31,22,23,14,15,6,7,28,29,20,21,12,13,4,5,..., dimensions={0} | all-to-all | bytes 524288 | tf_op jit(solution)/shard_map/all_to_all | solution.py:191
  42.4 0.2 shard_map.103
  42.6 10.2 %all_to_all.23.summed = bf16[32,16,128]{2,1,0:T(8,128)(2,1)S(1)} all-to-all(bf16[32,16,128]{2,1,0:T(8,128)(2,1)S(1)} %shard_map.103), channel_id=1, replica_groups={{0,1,30,31,22,23,28,29,26,27,20,21,18,19,14,15,24,25,10,11,16,17,12,13,..., dimensions={0} | all-to-all | bytes 262144 | tf_op jit(solution)/shard_map/all_to_all | solution.py:191
  52.8 1.0 %shard_map.104 = bf16[4,128,128]{2,1,0:T(8,128)(2,1)} custom-call(bf16[32,16,128]{2,1,0:T(8,128)(2,1)S(1)} %all_to_all.23.summed, bf16[128,512]{1,0:T(8,128)(2,1)S(1)} %get-tuple-element.19.old, f32[128,512]{1,0:T(8,128)S(1)} %get-tuple-element.20.old_gate, f32[128,32]{1,0:T(8,128)S(1)} %get-tuple-element.16.columns, bf16[2,128,128]{2,1,0:T(8,128)(2,1)S(1)} %copy-done.2), custom_call_target="tpu_custom_call" | custom-call | tf_op jit(solution)/shard_map/pallas_call | solution.py:175
Async XLA Ops:
  18.7 10.8 %copy-start = (bf16[2,128,512]{2,1,0:T(8,128)(2,1)S(1)}, bf16[2,128,512]{2,1,0:T(8,128)(2,1)}, u32[]{:S(2)}) copy-start(bf16[2,128,512]{2,1,0:T(8,128)(2,1)} %pw.3) | copy-start | bytes 786436
  18.9 10.6 %copy-start.1 = (bf16[2,128,128]{2,1,0:T(8,128)(2,1)S(1)}, bf16[2,128,128]{2,1,0:T(8,128)(2,1)}, u32[]{:S(2)}) copy-start(bf16[2,128,128]{2,1,0:T(8,128)(2,1)} %gw.3) | copy-start | bytes 196612
  18.9 10.6 %copy-start.2 = (bf16[2,128,128]{2,1,0:T(8,128)(2,1)S(1)}, bf16[2,128,128]{2,1,0:T(8,128)(2,1)}, u32[]{:S(2)}) copy-start(bf16[2,128,128]{2,1,0:T(8,128)(2,1)} %ow.3) | copy-start | bytes 196612

commit v20 on v19

--- a/solution.py
+++ b/solution.py
@@ -10,8 +10,8 @@
 PEERS = ("row", "ka")
 OWN = 4
 ORDERS = (
-    ((0, 15, 11, 7, 3, 14, 10, 6, 2, 13, 9, 5, 1, 12, 8, 4), (0, 15, 11, 7, 3, 14, 10, 6, 2, 13, 9, 5, 1, 12, 8, 4)),
-    ((0, 13, 9, 5, 1, 15, 11, 7, 3, 14, 10, 6, 2, 12, 8, 4), (0, 15, 11, 14, 13, 10, 9, 7, 12, 5, 8, 6, 4, 3, 2, 1)),
+    ((0, 14, 10, 6, 2, 15, 11, 7, 3, 13, 9, 5, 1, 12, 8, 4), (0, 14, 10, 6, 2, 15, 11, 7, 3, 13, 9, 5, 1, 12, 8, 4)),
+    ((0, 14, 10, 6, 2, 15, 11, 7, 3, 13, 9, 5, 1, 12, 8, 4), (0, 15, 11, 14, 13, 10, 9, 7, 12, 5, 8, 6, 4, 3, 2, 1)),
 )
 EACH = 16
 BF16, F32 = jnp.bfloat16, jnp.float32

time: 54 us -> 54.1 us (level)
  no operation moved by 1% of the time
where the time goes in v20:
time: 54.1 us; the launch traced here: 53.8 us
  blocking collectives  49.8 us (92%)
  Pallas kernels  3.95 us (7%)
    all_to_all x4, blocking collectives, exchange_in_order(): lax.all_to_all(blocks, 'row', split_axis=0, concat_axis=0, axis_index_gro...  49.8 us
    pallas_call x5, Pallas kernels, call(): pl.pallas_call(kernel, out_shape=[jax.ShapeDtypeStruct(*o) for o in outs]...  3.95 us

profile of v20, /device:TPU:0, one launch (start us, length us, event | category | flops | bytes accessed | tf_op | source)
XLA Modules:
  0.0 53.8 jit_solution(9450117495862086076)
XLA Ops:
  0.0 1.7 %shard_map.100 = (bf16[32,32,128]{2,1,0:T(8,128)(2,1)S(1)}, f32[128,512]{1,0:T(8,128)S(1)}, bf16[128,512]{1,0:T(8,128)(2,1)S(1)}, f32[128,32]{1,0:T(8,128)S(1)}, f32[8,128]{1,0:T(8,128)S(1)}) custom-call(bf16[4,128,128]{2,1,0:T(8,128)(2,1)} %pair.1, s32[4,128]{1,0:T(4,128)} %mask.1, bf16[2,128,512]{2,1,0:T(8,128)(2,1)} %pw.3, bf16[2,128,128]{2,1,0:T(8,128)(2,1)} %gw.3, ...), custom_call_target="tpu_custom_call" | custom-call | tf_op jit(solution)/shard_map/pallas_call | solution.py:175
  1.7 17.2 %all_to_all.20.sides = bf16[32,32,128]{2,1,0:T(8,128)(2,1)S(1)} all-to-all(bf16[32,32,128]{2,1,0:T(8,128)(2,1)S(1)} %get-tuple-element.13), channel_id=1, replica_groups={{0,1,28,29,20,21,12,13,4,5,30,31,22,23,14,15,6,7,26,27,18,19,10,11,2,3,..., dimensions={0} | all-to-all | bytes 524288 | tf_op jit(solution)/shard_map/all_to_all | solution.py:191
  19.0 0.0 copy-start
  19.0 0.2 shard_map.101
  19.2 0.0 copy-start.1
  19.2 0.0 copy-start.2
  19.2 10.5 %all_to_all.21.summed = bf16[32,16,128]{2,1,0:T(8,128)(2,1)S(1)} all-to-all(bf16[32,16,128]{2,1,0:T(8,128)(2,1)S(1)} %shard_map.101), channel_id=1, replica_groups={{0,1,28,29,20,21,12,13,4,5,30,31,22,23,14,15,6,7,26,27,18,19,10,11,2,3,..., dimensions={0} | all-to-all | bytes 262144 | tf_op jit(solution)/shard_map/all_to_all | solution.py:191
  29.7 0.0 copy-done
  29.7 0.0 copy-done.1
  29.7 0.0 copy-done.2
  29.7 0.8 %shard_map.102 = (bf16[32,32,128]{2,1,0:T(8,128)(2,1)S(1)}, f32[128,512]{1,0:T(8,128)S(1)}, bf16[128,512]{1,0:T(8,128)(2,1)S(1)}) custom-call(bf16[32,16,128]{2,1,0:T(8,128)(2,1)S(1)} %all_to_all.21.summed, bf16[128,512]{1,0:T(8,128)(2,1)S(1)} %get-tuple-element.14.old, f32[128,512]{1,0:T(8,128)S(1)} %get-tuple-element.15.old_gate, ...), custom_call_target="tpu_custom_call" | custom-call | tf_op jit(solution)/shard_map/pallas_call | solution.py:175
  30.5 11.8 %all_to_all.22.sides = bf16[32,32,128]{2,1,0:T(8,128)(2,1)S(1)} all-to-all(bf16[32,32,128]{2,1,0:T(8,128)(2,1)S(1)} %get-tuple-element.18), channel_id=1, replica_groups={{0,1,28,29,20,21,12,13,4,5,30,31,22,23,14,15,6,7,26,27,18,19,10,11,2,3,..., dimensions={0} | all-to-all | bytes 524288 | tf_op jit(solution)/shard_map/all_to_all | solution.py:191
  42.4 0.2 shard_map.103
  42.6 10.2 %all_to_all.23.summed = bf16[32,16,128]{2,1,0:T(8,128)(2,1)S(1)} all-to-all(bf16[32,16,128]{2,1,0:T(8,128)(2,1)S(1)} %shard_map.103), channel_id=1, replica_groups={{0,1,30,31,22,23,28,29,26,27,20,21,18,19,14,15,24,25,10,11,16,17,12,13,..., dimensions={0} | all-to-all | bytes 262144 | tf_op jit(solution)/shard_map/all_to_all | solution.py:191
  52.8 1.0 %shard_map.104 = bf16[4,128,128]{2,1,0:T(8,128)(2,1)} custom-call(bf16[32,16,128]{2,1,0:T(8,128)(2,1)S(1)} %all_to_all.23.summed, bf16[128,512]{1,0:T(8,128)(2,1)S(1)} %get-tuple-element.19.old, f32[128,512]{1,0:T(8,128)S(1)} %get-tuple-element.20.old_gate, f32[128,32]{1,0:T(8,128)S(1)} %get-tuple-element.16.columns, bf16[2,128,128]{2,1,0:T(8,128)(2,1)S(1)} %copy-done.2), custom_call_target="tpu_custom_call" | custom-call | tf_op jit(solution)/shard_map/pallas_call | solution.py:175
Async XLA Ops:
  19.0 10.8 %copy-start = (bf16[2,128,512]{2,1,0:T(8,128)(2,1)S(1)}, bf16[2,128,512]{2,1,0:T(8,128)(2,1)}, u32[]{:S(2)}) copy-start(bf16[2,128,512]{2,1,0:T(8,128)(2,1)} %pw.3) | copy-start | bytes 786436
  19.2 10.6 %copy-start.1 = (bf16[2,128,128]{2,1,0:T(8,128)(2,1)S(1)}, bf16[2,128,128]{2,1,0:T(8,128)(2,1)}, u32[]{:S(2)}) copy-start(bf16[2,128,128]{2,1,0:T(8,128)(2,1)} %gw.3) | copy-start | bytes 196612
  19.2 10.5 %copy-start.2 = (bf16[2,128,128]{2,1,0:T(8,128)(2,1)S(1)}, bf16[2,128,128]{2,1,0:T(8,128)(2,1)}, u32[]{:S(2)}) copy-start(bf16[2,128,128]{2,1,0:T(8,128)(2,1)} %ow.3) | copy-start | bytes 196612

commit v21 on v15

--- a/solution.py
+++ b/solution.py
@@ -11,7 +11,7 @@
 OWN = 4
 ORDERS = (
     ((0, 13, 9, 5, 1, 15, 11, 7, 3, 14, 10, 6, 2, 12, 8, 4), (0, 13, 9, 5, 1, 15, 11, 7, 3, 14, 10, 6, 2, 12, 8, 4)),
-    ((0, 13, 9, 5, 1, 15, 11, 7, 3, 14, 10, 6, 2, 12, 8, 4), (0, 15, 11, 14, 13, 10, 9, 7, 12, 5, 8, 6, 4, 3, 2, 1)),
+    ((0, 13, 9, 5, 1, 15, 11, 7, 3, 14, 10, 6, 2, 12, 8, 4), (0, 13, 9, 5, 1, 15, 11, 7, 3, 14, 10, 6, 2, 12, 8, 4)),
 )
 EACH = 16
 BF16, F32 = jnp.bfloat16, jnp.float32

time: 54 us -> 54.3 us (level)
  no operation moved by 1% of the time
where the time goes in v21:
time: 54.3 us; the launch traced here: 54.1 us
  blocking collectives  50.1 us (92%)
  Pallas kernels  3.94 us (7%)
    all_to_all x4, blocking collectives, exchange_in_order(): lax.all_to_all(blocks, 'row', split_axis=0, concat_axis=0, axis_index_gro...  50.1 us
    pallas_call x5, Pallas kernels, call(): pl.pallas_call(kernel, out_shape=[jax.ShapeDtypeStruct(*o) for o in outs]...  3.94 us

profile of v21, /device:TPU:0, one launch (start us, length us, event | category | flops | bytes accessed | tf_op | source)
XLA Modules:
  0.0 54.1 jit_solution(15842166730434677855)
XLA Ops:
  0.0 1.7 %shard_map.100 = (bf16[32,32,128]{2,1,0:T(8,128)(2,1)S(1)}, f32[128,512]{1,0:T(8,128)S(1)}, bf16[128,512]{1,0:T(8,128)(2,1)S(1)}, f32[128,32]{1,0:T(8,128)S(1)}, f32[8,128]{1,0:T(8,128)S(1)}) custom-call(bf16[4,128,128]{2,1,0:T(8,128)(2,1)} %pair.1, s32[4,128]{1,0:T(4,128)} %mask.1, bf16[2,128,512]{2,1,0:T(8,128)(2,1)} %pw.3, bf16[2,128,128]{2,1,0:T(8,128)(2,1)} %gw.3, ...), custom_call_target="tpu_custom_call" | custom-call | tf_op jit(solution)/shard_map/pallas_call | solution.py:175
  1.7 17.3 %all_to_all.20.sides = bf16[32,32,128]{2,1,0:T(8,128)(2,1)S(1)} all-to-all(bf16[32,32,128]{2,1,0:T(8,128)(2,1)S(1)} %get-tuple-element.13), channel_id=1, replica_groups={{0,1,26,27,18,19,10,11,2,3,30,31,22,23,14,15,6,7,28,29,20,21,12,13,4,5,..., dimensions={0} | all-to-all | bytes 524288 | tf_op jit(solution)/shard_map/all_to_all | solution.py:191
  19.0 0.0 copy-start
  19.0 0.2 shard_map.101
  19.2 0.0 copy-start.1
  19.2 0.0 copy-start.2
  19.2 10.5 %all_to_all.21.summed = bf16[32,16,128]{2,1,0:T(8,128)(2,1)S(1)} all-to-all(bf16[32,16,128]{2,1,0:T(8,128)(2,1)S(1)} %shard_map.101), channel_id=1, replica_groups={{0,1,26,27,18,19,10,11,2,3,30,31,22,23,14,15,6,7,28,29,20,21,12,13,4,5,..., dimensions={0} | all-to-all | bytes 262144 | tf_op jit(solution)/shard_map/all_to_all | solution.py:191
  29.7 0.0 copy-done
  29.7 0.0 copy-done.1
  29.7 0.0 copy-done.2
  29.7 0.8 %shard_map.102 = (bf16[32,32,128]{2,1,0:T(8,128)(2,1)S(1)}, f32[128,512]{1,0:T(8,128)S(1)}, bf16[128,512]{1,0:T(8,128)(2,1)S(1)}) custom-call(bf16[32,16,128]{2,1,0:T(8,128)(2,1)S(1)} %all_to_all.21.summed, bf16[128,512]{1,0:T(8,128)(2,1)S(1)} %get-tuple-element.14.old, f32[128,512]{1,0:T(8,128)S(1)} %get-tuple-element.15.old_gate, ...), custom_call_target="tpu_custom_call" | custom-call | tf_op jit(solution)/shard_map/pallas_call | solution.py:175
  30.5 11.9 %all_to_all.22.sides = bf16[32,32,128]{2,1,0:T(8,128)(2,1)S(1)} all-to-all(bf16[32,32,128]{2,1,0:T(8,128)(2,1)S(1)} %get-tuple-element.18), channel_id=1, replica_groups={{0,1,26,27,18,19,10,11,2,3,30,31,22,23,14,15,6,7,28,29,20,21,12,13,4,5,..., dimensions={0} | all-to-all | bytes 524288 | tf_op jit(solution)/shard_map/all_to_all | solution.py:191
  42.4 0.2 shard_map.103
  42.6 10.5 %all_to_all.23.summed = bf16[32,16,128]{2,1,0:T(8,128)(2,1)S(1)} all-to-all(bf16[32,16,128]{2,1,0:T(8,128)(2,1)S(1)} %shard_map.103), channel_id=1, replica_groups={{0,1,26,27,18,19,10,11,2,3,30,31,22,23,14,15,6,7,28,29,20,21,12,13,4,5,..., dimensions={0} | all-to-all | bytes 262144 | tf_op jit(solution)/shard_map/all_to_all | solution.py:191
  53.1 1.0 %shard_map.104 = bf16[4,128,128]{2,1,0:T(8,128)(2,1)} custom-call(bf16[32,16,128]{2,1,0:T(8,128)(2,1)S(1)} %all_to_all.23.summed, bf16[128,512]{1,0:T(8,128)(2,1)S(1)} %get-tuple-element.19.old, f32[128,512]{1,0:T(8,128)S(1)} %get-tuple-element.20.old_gate, f32[128,32]{1,0:T(8,128)S(1)} %get-tuple-element.16.columns, bf16[2,128,128]{2,1,0:T(8,128)(2,1)S(1)} %copy-done.2), custom_call_target="tpu_custom_call" | custom-call | tf_op jit(solution)/shard_map/pallas_call | solution.py:175
Async XLA Ops:
  19.0 10.8 %copy-start = (bf16[2,128,512]{2,1,0:T(8,128)(2,1)S(1)}, bf16[2,128,512]{2,1,0:T(8,128)(2,1)}, u32[]{:S(2)}) copy-start(bf16[2,128,512]{2,1,0:T(8,128)(2,1)} %pw.3) | copy-start | bytes 786436
  19.2 10.5 %copy-start.1 = (bf16[2,128,128]{2,1,0:T(8,128)(2,1)S(1)}, bf16[2,128,128]{2,1,0:T(8,128)(2,1)}, u32[]{:S(2)}) copy-start(bf16[2,128,128]{2,1,0:T(8,128)(2,1)} %gw.3) | copy-start | bytes 196612
  19.2 10.5 %copy-start.2 = (bf16[2,128,128]{2,1,0:T(8,128)(2,1)S(1)}, bf16[2,128,128]{2,1,0:T(8,128)(2,1)}, u32[]{:S(2)}) copy-start(bf16[2,128,128]{2,1,0:T(8,128)(2,1)} %ow.3) | copy-start | bytes 196612

commit v22 on v19

--- a/solution.py
+++ b/solution.py
@@ -10,7 +10,7 @@
 PEERS = ("row", "ka")
 OWN = 4
 ORDERS = (
-    ((0, 15, 11, 7, 3, 14, 10, 6, 2, 13, 9, 5, 1, 12, 8, 4), (0, 15, 11, 7, 3, 14, 10, 6, 2, 13, 9, 5, 1, 12, 8, 4)),
+    ((0, 15, 11, 7, 3, 14, 10, 6, 2, 13, 9, 5, 1, 12, 8, 4), (0, 13, 9, 5, 1, 15, 11, 7, 3, 14, 10, 6, 2, 12, 8, 4)),
     ((0, 13, 9, 5, 1, 15, 11, 7, 3, 14, 10, 6, 2, 12, 8, 4), (0, 15, 11, 14, 13, 10, 9, 7, 12, 5, 8, 6, 4, 3, 2, 1)),
 )
 EACH = 16

time: 54 us -> 54.1 us (level)
  no operation moved by 1% of the time
where the time goes in v22:
time: 54.1 us; the launch traced here: 53.8 us
  blocking collectives  49.8 us (92%)
  Pallas kernels  3.95 us (7%)
    all_to_all x4, blocking collectives, exchange_in_order(): lax.all_to_all(blocks, 'row', split_axis=0, concat_axis=0, axis_index_gro...  49.8 us
    pallas_call x5, Pallas kernels, call(): pl.pallas_call(kernel, out_shape=[jax.ShapeDtypeStruct(*o) for o in outs]...  3.95 us

profile of v22, /device:TPU:0, one launch (start us, length us, event | category | flops | bytes accessed | tf_op | source)
XLA Modules:
  0.0 53.8 jit_solution(14026050458537023710)
XLA Ops:
  0.0 1.7 %shard_map.100 = (bf16[32,32,128]{2,1,0:T(8,128)(2,1)S(1)}, f32[128,512]{1,0:T(8,128)S(1)}, bf16[128,512]{1,0:T(8,128)(2,1)S(1)}, f32[128,32]{1,0:T(8,128)S(1)}, f32[8,128]{1,0:T(8,128)S(1)}) custom-call(bf16[4,128,128]{2,1,0:T(8,128)(2,1)} %pair.1, s32[4,128]{1,0:T(4,128)} %mask.1, bf16[2,128,512]{2,1,0:T(8,128)(2,1)} %pw.3, bf16[2,128,128]{2,1,0:T(8,128)(2,1)} %gw.3, ...), custom_call_target="tpu_custom_call" | custom-call | tf_op jit(solution)/shard_map/pallas_call | solution.py:175
  1.7 16.9 %all_to_all.20.sides = bf16[32,32,128]{2,1,0:T(8,128)(2,1)S(1)} all-to-all(bf16[32,32,128]{2,1,0:T(8,128)(2,1)S(1)} %get-tuple-element.13), channel_id=1, replica_groups={{0,1,30,31,22,23,14,15,6,7,28,29,20,21,12,13,4,5,26,27,18,19,10,11,2,3,..., dimensions={0} | all-to-all | bytes 524288 | tf_op jit(solution)/shard_map/all_to_all | solution.py:191
  18.7 0.0 copy-start
  18.7 0.2 shard_map.101
  18.9 0.0 copy-start.1
  18.9 0.0 copy-start.2
  18.9 10.8 %all_to_all.21.summed = bf16[32,16,128]{2,1,0:T(8,128)(2,1)S(1)} all-to-all(bf16[32,16,128]{2,1,0:T(8,128)(2,1)S(1)} %shard_map.101), channel_id=1, replica_groups={{0,1,26,27,18,19,10,11,2,3,30,31,22,23,14,15,6,7,28,29,20,21,12,13,4,5,..., dimensions={0} | all-to-all | bytes 262144 | tf_op jit(solution)/shard_map/all_to_all | solution.py:191
  29.7 0.0 copy-done
  29.7 0.0 copy-done.1
  29.7 0.0 copy-done.2
  29.7 0.8 %shard_map.102 = (bf16[32,32,128]{2,1,0:T(8,128)(2,1)S(1)}, f32[128,512]{1,0:T(8,128)S(1)}, bf16[128,512]{1,0:T(8,128)(2,1)S(1)}) custom-call(bf16[32,16,128]{2,1,0:T(8,128)(2,1)S(1)} %all_to_all.21.summed, bf16[128,512]{1,0:T(8,128)(2,1)S(1)} %get-tuple-element.14.old, f32[128,512]{1,0:T(8,128)S(1)} %get-tuple-element.15.old_gate, ...), custom_call_target="tpu_custom_call" | custom-call | tf_op jit(solution)/shard_map/pallas_call | solution.py:175
  30.5 11.9 %all_to_all.22.sides = bf16[32,32,128]{2,1,0:T(8,128)(2,1)S(1)} all-to-all(bf16[32,32,128]{2,1,0:T(8,128)(2,1)S(1)} %get-tuple-element.18), channel_id=1, replica_groups={{0,1,26,27,18,19,10,11,2,3,30,31,22,23,14,15,6,7,28,29,20,21,12,13,4,5,..., dimensions={0} | all-to-all | bytes 524288 | tf_op jit(solution)/shard_map/all_to_all | solution.py:191
  42.4 0.2 shard_map.103
  42.6 10.2 %all_to_all.23.summed = bf16[32,16,128]{2,1,0:T(8,128)(2,1)S(1)} all-to-all(bf16[32,16,128]{2,1,0:T(8,128)(2,1)S(1)} %shard_map.103), channel_id=1, replica_groups={{0,1,30,31,22,23,28,29,26,27,20,21,18,19,14,15,24,25,10,11,16,17,12,13,..., dimensions={0} | all-to-all | bytes 262144 | tf_op jit(solution)/shard_map/all_to_all | solution.py:191
  52.8 1.0 %shard_map.104 = bf16[4,128,128]{2,1,0:T(8,128)(2,1)} custom-call(bf16[32,16,128]{2,1,0:T(8,128)(2,1)S(1)} %all_to_all.23.summed, bf16[128,512]{1,0:T(8,128)(2,1)S(1)} %get-tuple-element.19.old, f32[128,512]{1,0:T(8,128)S(1)} %get-tuple-element.20.old_gate, f32[128,32]{1,0:T(8,128)S(1)} %get-tuple-element.16.columns, bf16[2,128,128]{2,1,0:T(8,128)(2,1)S(1)} %copy-done.2), custom_call_target="tpu_custom_call" | custom-call | tf_op jit(solution)/shard_map/pallas_call | solution.py:175
Async XLA Ops:
  18.7 11.1 %copy-start = (bf16[2,128,512]{2,1,0:T(8,128)(2,1)S(1)}, bf16[2,128,512]{2,1,0:T(8,128)(2,1)}, u32[]{:S(2)}) copy-start(bf16[2,128,512]{2,1,0:T(8,128)(2,1)} %pw.3) | copy-start | bytes 786436
  18.9 10.8 %copy-start.1 = (bf16[2,128,128]{2,1,0:T(8,128)(2,1)S(1)}, bf16[2,128,128]{2,1,0:T(8,128)(2,1)}, u32[]{:S(2)}) copy-start(bf16[2,128,128]{2,1,0:T(8,128)(2,1)} %gw.3) | copy-start | bytes 196612
  18.9 10.8 %copy-start.2 = (bf16[2,128,128]{2,1,0:T(8,128)(2,1)S(1)}, bf16[2,128,128]{2,1,0:T(8,128)(2,1)}, u32[]{:S(2)}) copy-start(bf16[2,128,128]{2,1,0:T(8,128)(2,1)} %ow.3) | copy-start | bytes 196612
